TPU v7x, 128 devices: a whole 4x4x4 slice. The times are simulated.
128 devices in a mesh: ctx: 8 (over z_lo, x), fsdp: 16 (over z_hi, y, core).
Axes of the slice: x: 4, y: 4, z: 4 (z_hi: 2, z_lo: 2; z = z_hi * 2 + z_lo), core: 2. Of those that a mesh axis runs over, the one named last changes fastest.
Arguments:
- tokens: bfloat16 [32, 1024, 768], P('fsdp', 'ctx'), may hold values from -6 to 6
- lengths: int32 [32], P('fsdp'), may hold values from 1 to 1024, as said below
- deal: int32 [8], replicated, may hold values from 0 to 7, each once
- gain_attn: bfloat16 [768], P('fsdp'), may hold values from 0.25 to 1.75
- w_qkv: bfloat16 [768, 2304], P('fsdp'), may hold values from -0.3125 to 0.3125
- w_out: bfloat16 [768, 768], P('fsdp'), may hold values from -0.625 to 0.625
- gain_mlp: bfloat16 [768], P('fsdp'), may hold values from 0.25 to 1.75
- w_in: bfloat16 [768, 2304], P('fsdp'), may hold values from -0.21875 to 0.21875
- w_down: bfloat16 [1152, 768], P('fsdp'), may hold values from -0.375 to 0.375
- cotangent: bfloat16 [32, 1024, 768], P('fsdp', 'ctx'), may hold values from -6 to 6
Outputs:
- layer_out: bfloat16 [32, 1024, 768], P('fsdp', 'ctx')
- grad_tokens: float32 [32, 1024, 768], P('fsdp', 'ctx')
- grad_gain_attn: float32 [768], P('fsdp')
- grad_w_qkv: float32 [768, 2304], P('fsdp')
- grad_w_out: float32 [768, 768], P('fsdp')
- grad_gain_mlp: float32 [768], P('fsdp')
- grad_w_in: float32 [768, 2304], P('fsdp')
- grad_w_down: float32 [1152, 768], P('fsdp')
Inputs may be any that keep to these rules, and one draw needn't show every extreme that they name: `lengths`: in each aligned group of 2 sequences one, drawn from the seed, has length 1024.
All inputs are finite; a program needn't handle non-finite values.
Results may differ from a plain program's by a relative error of at most 0.028.
Values may be sent and summed in bfloat16 or wider, within the bound.
No kernel may reach another device: no remote copies, remote signals or barrier semaphores. Data moves between devices by JAX's collectives and lax.ppermute only.
A program may use at most 128 MiB of HBM per device.

v0:
```python
import math

import jax
import jax.numpy as jnp
from jax import lax
from jax.sharding import PartitionSpec as P

HEADS = 12
HD = 64
BLK = 128


EPS = 1e-05
THETA = 160000.0
NEGATIVE = -1e30
INV_ROOT_TWO = 0.7071067811865476
INV_ROOT_TWO_PI = 0.3989422804014327


def gather_by_exchange(part, axis, n):
    return lax.all_to_all(jnp.broadcast_to(part[None], (n, *part.shape)), axis, 0, 0)


def core_pairs(n):
    return [(k, k ^ 1) for k in range(n)]


def core_groups(n):
    return [list(range(first, n, 2)) for first in range(2)]


def gather_two_level(part, axis):
    n = lax.axis_size(axis)
    mine = lax.all_to_all(
        jnp.broadcast_to(part[None], (n // 2, *part.shape)),
        axis,
        0,
        0,
        axis_index_groups=core_groups(n),
    )
    other = lax.ppermute(mine, axis, core_pairs(n))
    even = lax.axis_index(axis) % 2 == 0
    return jnp.where(even, mine, other), jnp.where(even, other, mine)


def reduce_two_level(parts, axis):
    n = lax.axis_size(axis)
    core = lax.axis_index(axis) % 2
    paired = parts.reshape(n // 2, 2, *parts.shape[1:])
    away = lax.dynamic_index_in_dim(paired, 1 - core, 1, keepdims=False)
    kept = lax.dynamic_index_in_dim(paired, core, 1, keepdims=False)
    came = lax.ppermute(away, axis, core_pairs(n))
    both = low(kept.astype(jnp.float32) + came.astype(jnp.float32))
    shares = lax.all_to_all(both, axis, 0, 0, tiled=True, axis_index_groups=core_groups(n))
    return low(jnp.sum(shares.astype(jnp.float32), 0))


def low(values):
    return values.astype(jnp.bfloat16)


def tables(positions):
    halves = jnp.arange(HD // 2, dtype=jnp.float32)
    frequency = THETA ** (-2.0 * halves / HD)
    angles = positions.astype(jnp.float32)[:, None] * frequency[None, :]
    cosine = jnp.cos(angles)
    sine = jnp.sin(angles)
    return (jnp.concatenate([cosine, cosine], -1), jnp.concatenate([sine, sine], -1))


def turned(values):
    halfway = values.shape[-1] // 2
    return jnp.concatenate([-values[..., halfway:], values[..., :halfway]], -1)


def rotary(values, cosine, sine):
    return values * cosine + turned(values) * sine


def unrotary(grads_in, cosine, sine):
    return grads_in * cosine - turned(grads_in) * sine


def norm_forward(rows_in, gain):
    centre = rows_in - jnp.mean(rows_in, -1, keepdims=True)
    variance = jnp.mean(centre * centre, -1, keepdims=True)
    inverse = lax.rsqrt(variance + EPS)
    normed = centre * inverse
    return (normed * gain.astype(jnp.float32), normed, inverse)


def norm_backward(grad_rows, gain, normed, inverse):
    scaled = grad_rows * gain.astype(jnp.float32)
    grad_gain = jnp.sum(grad_rows * normed, 0)
    grad_rows_in = inverse * (
        scaled
        - jnp.mean(scaled, -1, keepdims=True)
        - normed * jnp.mean(scaled * normed, -1, keepdims=True)
    )
    return (grad_rows_in, grad_gain)


def attention_forward(query, keys, values, keep, factor):
    scores = jnp.einsum("qhd,khd->hqk", query, keys, preferred_element_type=jnp.float32) * factor
    scores = jnp.where(keep[None, None, :], scores, NEGATIVE)
    maximum = jnp.max(scores, -1, keepdims=True)
    exponent = jnp.exp(scores - maximum)
    row_total = jnp.sum(exponent, -1, keepdims=True)
    probs = exponent / row_total
    attended = jnp.einsum("hqk,khd->qhd", low(probs), values, preferred_element_type=jnp.float32)
    return attended, (maximum + jnp.log(row_total))[..., 0]


def attention_backward(query, keys, values, grad_heads, log_total, keep, factor):
    scores = jnp.einsum("qhd,khd->hqk", query, keys, preferred_element_type=jnp.float32) * factor
    scores = jnp.where(keep[None, None, :], scores, NEGATIVE)
    probs = jnp.exp(scores - log_total[..., None])
    grad_probs = jnp.einsum("qhd,khd->hqk", grad_heads, values, preferred_element_type=jnp.float32)
    delta = jnp.sum(probs * grad_probs, -1, keepdims=True)
    grad_scores = low(probs * (grad_probs - delta))
    grad_query = factor * jnp.einsum(
        "hqk,khd->qhd", grad_scores, keys, preferred_element_type=jnp.float32
    )
    grad_key = factor * jnp.einsum(
        "hqk,qhd->khd", grad_scores, query, preferred_element_type=jnp.float32
    )
    grad_value = jnp.einsum(
        "hqk,qhd->khd", low(probs), grad_heads, preferred_element_type=jnp.float32
    )
    return grad_query, grad_key, grad_value


def body(tokens, lengths, deal, gain_attn, w_qkv, w_out, gain_mlp, w_in, w_down, cotangent):
    seqs, local_len, width = tokens.shape
    ctx = lax.axis_size("ctx")
    fsdp = lax.axis_size("fsdp")
    spread = ctx // seqs
    group = HEADS // spread
    span = group * HD
    full_len = local_len * ctx
    rows = seqs * local_len
    factor = HD ** (-0.5)
    context = lax.axis_index("ctx")
    own_seq = context // spread
    own_group = context % spread
    depth = w_qkv.shape[0]
    hidden = w_in.shape[1] // 2
    down_rows = w_down.shape[0]
    f32 = jnp.float32

    offsets = jnp.arange(BLK, dtype=jnp.int32)
    own_pos = lax.dynamic_slice_in_dim(deal, context, 1)[0] * BLK + offsets
    all_pos = (deal[:, None] * BLK + offsets[None, :]).reshape(full_len)
    length = lax.dynamic_slice_in_dim(lengths, own_seq, 1)[0]
    own_keep = own_pos[None, :] < lengths[:, None]
    all_keep = all_pos < length

    qkv_own = lax.dynamic_index_in_dim(
        w_qkv.reshape(depth, 3, spread, span), own_group, 2, keepdims=False
    ).reshape(depth, 3 * span)
    gains_wide = jnp.stack([gain_attn, gain_mlp], 1)
    fill = jnp.zeros((depth, 640 - 3 * span - 2), jnp.bfloat16)
    first_all = jnp.stack(
        gather_two_level(jnp.concatenate([qkv_own, gains_wide, fill], 1), "fsdp"), 1
    ).reshape(fsdp * depth, 640)
    sequence = lax.all_to_all(jnp.repeat(tokens, spread, axis=0), "ctx", 0, 0, tiled=True)

    wqkv_part = first_all[:, : 3 * span]
    gain_one = first_all[:, 3 * span]
    gain_two = first_all[:, 3 * span + 1]

    count = w_in.shape[1] // width
    pieces = [w_in[:, k * width : (k + 1) * width] for k in range(count)]
    stacked = jnp.concatenate([*pieces, w_out, w_down], 0)
    stacked, first_all = lax.optimization_barrier((stacked, first_all))
    stacked_all = gather_two_level(stacked, "fsdp")

    cosine, sine = tables(all_pos)
    cosine = cosine[:, None, :]
    sine = sine[:, None, :]

    a_rows, seq_normed, _ = norm_forward(sequence.astype(f32).reshape(full_len, width), gain_one)
    a_low = low(a_rows)
    joined = jnp.dot(a_low, wqkv_part, preferred_element_type=f32).reshape(
        full_len, 3, group, HD
    )
    query = low(rotary(joined[:, 0], cosine, sine))
    keys = low(rotary(joined[:, 1], cosine, sine))
    values = low(joined[:, 2])
    attended, log_total = attention_forward(query, keys, values, all_keep, factor)
    attended = low(jnp.where(all_keep[:, None, None], attended, 0.0))
    att_back = lax.all_to_all(attended.reshape(ctx, local_len, span), "ctx", 0, 0, tiled=True)
    att_low = (
        att_back.reshape(seqs, spread, local_len, span).transpose(0, 2, 1, 3).reshape(rows, width)
    )

    def whole(start, height):
        halves = [part[:, start : start + height] for part in stacked_all]
        return jnp.stack(halves, 1).reshape(fsdp * height, width)

    win_all = jnp.concatenate([whole(k * depth, depth) for k in range(count)], 1)
    wout_all = whole(count * depth, depth)
    wdown_all = whole((count + 1) * depth, down_rows)

    resid = tokens.astype(f32).reshape(rows, width)
    mixed = resid + jnp.dot(att_low, wout_all, preferred_element_type=f32)
    normed_mid, normed_two, inverse_two = norm_forward(mixed, gain_two)
    b_low = low(normed_mid)
    gate_up = jnp.dot(b_low, win_all, preferred_element_type=f32)
    gate_in = gate_up[:, :hidden]
    up_half = gate_up[:, hidden:]
    normal_cdf = 0.5 * (1.0 + lax.erf(gate_in * INV_ROOT_TWO))
    gelu_out = gate_in * normal_cdf
    hid_low = low(gelu_out * up_half)
    output = mixed + jnp.dot(hid_low, wdown_all, preferred_element_type=f32)

    grad_low = cotangent.reshape(rows, width)
    grad_out = grad_low.astype(f32)
    grad_wdown = jnp.einsum("rf,rd->fd", hid_low, grad_low, preferred_element_type=f32)
    grad_hid = jnp.einsum("rd,fd->rf", grad_low, wdown_all, preferred_element_type=f32)
    normal_pdf = jnp.exp(-0.5 * gate_in * gate_in) * INV_ROOT_TWO_PI
    grad_gate = grad_hid * up_half * (normal_cdf + gate_in * normal_pdf)
    grad_up = grad_hid * gelu_out
    grad_gate_up = low(jnp.concatenate([grad_gate, grad_up], 1))
    grad_win = low(jnp.einsum("rd,rf->df", b_low, grad_gate_up, preferred_element_type=f32))
    grad_b = jnp.einsum("rf,df->rd", grad_gate_up, win_all, preferred_element_type=f32)
    grad_norm_two, grad_gain_two = norm_backward(grad_b, gain_two, normed_two, inverse_two)
    grad_mixed = grad_out + grad_norm_two
    grad_att = low(grad_mixed)
    grad_wout = jnp.einsum("rd,re->de", att_low, grad_att, preferred_element_type=f32)
    grad_attended = jnp.einsum("re,de->rd", grad_att, wout_all, preferred_element_type=f32)
    grad_heads = jnp.where(own_keep.reshape(rows, 1), grad_attended, 0.0)
    grad_heads = (
        low(grad_heads)
        .reshape(seqs, local_len, spread, span)
        .transpose(0, 2, 1, 3)
        .reshape(ctx, local_len, span)
    )
    grads_stacked = jnp.concatenate(
        [
            *[
                grad_win[:, k * width : (k + 1) * width].reshape(fsdp, depth, width)
                for k in range(count)
            ],
            low(grad_wout).reshape(fsdp, depth, width),
            low(grad_wdown).reshape(fsdp, down_rows, width),
        ],
        1,
    )
    grads_stacked, grad_heads = lax.optimization_barrier((grads_stacked, grad_heads))

    all_grad = lax.all_to_all(grad_heads, "ctx", 0, 0, tiled=True).reshape(full_len, group, HD)
    grads_part = reduce_two_level(grads_stacked, "fsdp")
    grad_query, grad_key, grad_value = attention_backward(
        query, keys, values, all_grad, log_total, all_keep, factor
    )
    grad_qkv = low(
        jnp.concatenate(
            [
                unrotary(grad_query, cosine, sine).reshape(full_len, span),
                unrotary(grad_key, cosine, sine).reshape(full_len, span),
                grad_value.reshape(full_len, span),
            ],
            1,
        )
    )
    grad_wqkv = low(jnp.einsum("rd,rf->df", a_low, grad_qkv, preferred_element_type=f32))
    grad_a_part = jnp.einsum("rf,df->rd", grad_qkv, wqkv_part, preferred_element_type=f32)
    grad_gain_one = jnp.sum(grad_a_part * seq_normed, 0)
    last = jnp.concatenate(
        [
            grad_wqkv,
            jnp.stack([low(grad_gain_one), low(grad_gain_two)], 1),
            jnp.zeros((fsdp * depth, 640 - 3 * span - 2), jnp.bfloat16),
        ],
        1,
    )
    last = reduce_two_level(last.reshape(fsdp, depth, 640), "fsdp")
    last_rows = last.size // width
    grad_a_parts = lax.all_to_all(
        low(grad_a_part).reshape(ctx, local_len, width), "ctx", 0, 0, tiled=True
    )
    grad_a = jnp.sum(
        grad_a_parts.reshape(seqs, spread, local_len, width).astype(f32), 1
    ).reshape(rows, width)
    _, normed_one, inverse_one = norm_forward(resid, gain_one)
    grad_norm_one, _ = norm_backward(grad_a, gain_one, normed_one, inverse_one)
    grad_input = grad_mixed + grad_norm_one

    own_rows = grads_part.shape[0] // ctx
    shares = lax.all_to_all(grads_part.reshape(ctx, own_rows, width), "ctx", 0, 0, tiled=True)
    share = low(jnp.sum(shares.astype(f32), 0))
    ends = gather_by_exchange(
        jnp.concatenate([last.reshape(last_rows, width), share], 0), "ctx", ctx
    )
    last_all = ends[:, :last_rows].reshape(ctx, depth, 640).astype(f32)
    summed = ends[:, last_rows:].reshape(ctx * own_rows, width).astype(f32)
    grad_wqkv_out = (
        jnp.sum(last_all[:, :, : 3 * span].reshape(seqs, spread, depth, 3, span), 0)
        .transpose(1, 2, 0, 3)
        .reshape(depth, 3 * width)
    )
    gains_out = jnp.sum(last_all[:, :, 3 * span : 3 * span + 2], 0)
    return (
        low(output.reshape(tokens.shape)),
        grad_input.reshape(tokens.shape),
        gains_out[:, 0],
        grad_wqkv_out,
        summed[count * depth : (count + 1) * depth],
        gains_out[:, 1],
        jnp.concatenate([summed[k * depth : (k + 1) * depth] for k in range(count)], 1),
        summed[(count + 1) * depth :],
    )


def solution(mesh):
    placed = (
        P("fsdp", "ctx", None),
        P("fsdp"),
        P(),
        P("fsdp"),
        P("fsdp", None),
        P("fsdp", None),
        P("fsdp"),
        P("fsdp", None),
        P("fsdp", None),
        P("fsdp", "ctx", None),
    )
    return jax.shard_map(
        body,
        mesh=mesh,
        in_specs=placed,
        out_specs=(
            P("fsdp", "ctx", None),
            P("fsdp", "ctx", None),
            P("fsdp"),
            P("fsdp", None),
            P("fsdp", None),
            P("fsdp"),
            P("fsdp", None),
            P("fsdp", None),
        ),
        check_vma=False,
    )
```

profile of v0, /device:TPU:1, one launch (start us, length us, event | category | flops | bytes accessed | tf_op | source)
XLA Modules:
  0.0 344.9 jit_solution(196029776003477889)
XLA Ops:
  5.1 8.3 %all-to-all-start.1 = ((bf16[8,48,640]{2,1,0:T(8,128)(2,1)}), bf16[8,48,640]{2,1,0:T(8,128)(2,1)S(1)}, u32[]{:S(2)}, u32[]{:S(2)}) async-start(bf16[8,48,640]{2,1,0:T(8,128)(2,1)} %broadcast_in_dim.51), calls=%async_computation.1 | async-start | bytes 983040 | tf_op jit(solution)/shard_map/all_to_all | solution.py:34
  13.6 11.2 %all-to-all-done.1 = bf16[8,48,640]{2,1,0:T(8,128)(2,1)S(1)} async-done(((bf16[8,48,640]{2,1,0:T(8,128)(2,1)}), bf16[8,48,640]{2,1,0:T(8,128)(2,1)S(1)}, u32[]{:S(2)}, u32[]{:S(2)}) %all-to-all-start.1) | async-done | bytes 491552 | tf_op jit(solution)/shard_map/all_to_all | solution.py:34
  26.1 4.5 %all-to-all-start = ((bf16[8,128,768]{2,1,0:T(8,128)(2,1)}), bf16[8,128,768]{2,1,0:T(8,128)(2,1)S(1)}, u32[]{:S(2)}, u32[]{:S(2)}) async-start(bf16[8,128,768]{2,1,0:T(8,128)(2,1)} %bitcast.3), calls=%async_computation | async-start | bytes 3145728 | tf_op jit(solution)/shard_map/all_to_all | solution.py:166
  36.6 15.4 %all-to-all-done = bf16[8,128,768]{2,1,0:T(8,128)(2,1)S(1)} async-done(((bf16[8,128,768]{2,1,0:T(8,128)(2,1)}), bf16[8,128,768]{2,1,0:T(8,128)(2,1)S(1)}, u32[]{:S(2)}, u32[]{:S(2)}) %all-to-all-start) | async-done | bytes 1572896 | tf_op jit(solution)/shard_map/all_to_all | solution.py:166
  52.0 2.9 broadcast_in_dim.59
  54.9 4.5 %all-to-all-start.3 = ((bf16[8,264,768]{2,1,0:T(8,128)(2,1)}), bf16[8,264,768]{2,1,0:T(8,128)(2,1)}, u32[]{:S(2)}, u32[]{:S(2)}) async-start(bf16[8,264,768]{2,1,0:T(8,128)(2,1)} %broadcast_in_dim.59), calls=%async_computation.3 | async-start | bytes 6488064 | tf_op jit(solution)/shard_map/all_to_all | solution.py:34
  61.4 2.2 copy.93
  69.6 30.6 %all-to-all-done.3 = bf16[8,264,768]{2,1,0:T(8,128)(2,1)} async-done(((bf16[8,264,768]{2,1,0:T(8,128)(2,1)}), bf16[8,264,768]{2,1,0:T(8,128)(2,1)}, u32[]{:S(2)}, u32[]{:S(2)}) %all-to-all-start.3) | async-done | bytes 3244064 | tf_op jit(solution)/shard_map/all_to_all | solution.py:34
  101.6 2.3 fusion.63
  103.9 1.8 fusion
  105.7 2.8 copy-done
  108.7 3.5 %fusion.16 = bf16[3,64,1024]{2,1,0:T(8,128)(2,1)S(1)} fusion(f32[3,1024,1024]{1,2,0:T(8,128)S(1)} %get-tuple-element.75, f32[3,1024]{1,0:T(4,128)S(1)} %fusion, f32[3,1024]{1,0:T(4,128)S(1)} %get-tuple-element.74, pred[1024]{0:T(1024)(128)(4,1)S(1)} %fusion.51, f32[1024,3,3,64]{0,3,2,1:T(8,128)} %copy-done.2), kind=kOutput, calls=%fused_computation.43 | convolution fusion | flops 412483584 | bytes 13394944 | tf_op jit(solution)/shard_map/hqk,khd->qhd/dot_general | solution.py:110
  113.1 3.6 %all-to-all-start.2 = ((bf16[8,128,192]{1,2,0:T(8,128)(2,1)}), bf16[8,128,192]{1,2,0:T(8,128)(2,1)S(1)}, u32[]{:S(2)}, u32[]{:S(2)}) async-start(bf16[8,128,192]{1,2,0:T(8,128)(2,1)} %copy.95), calls=%async_computation.2 | async-start | bytes 786432 | tf_op jit(solution)/shard_map/all_to_all | solution.py:192
  118.0 7.6 %all-to-all-done.2 = bf16[8,128,192]{1,2,0:T(8,128)(2,1)S(1)} async-done(((bf16[8,128,192]{1,2,0:T(8,128)(2,1)}), bf16[8,128,192]{1,2,0:T(8,128)(2,1)S(1)}, u32[]{:S(2)}, u32[]{:S(2)}) %all-to-all-start.2) | async-done | bytes 393248 | tf_op jit(solution)/shard_map/all_to_all | solution.py:192
  126.0 3.3 broadcast_select_fusion.1
  133.0 1.8 fusion.22
  134.8 1.8 multiply_reduce_fusion.3
  136.6 3.0 convolution_convert_fusion
  142.7 1.9 copy.103
  144.6 1.8 reshape.423
  146.4 1.8 copy.104
  148.2 2.3 fusion.61
  157.1 4.1 %all-to-all-start.4 = ((bf16[8,128,192]{1,2,0:T(8,128)(2,1)}), bf16[8,128,192]{1,2,0:T(8,128)(2,1)}, u32[]{:S(2)}, u32[]{:S(2)}) async-start(bf16[8,128,192]{1,2,0:T(8,128)(2,1)} %bitcast.209), calls=%async_computation.4 | async-start | bytes 786432 | tf_op jit(solution)/shard_map/all_to_all | solution.py:252
  161.9 1.7 convert_element_type.242
  163.6 3.9 %dynamic-slice_bitcast_fusion = bf16[8,264,768]{2,1,0:T(8,128)(2,1)} fusion(bf16[8,2,264,768]{3,2,1,0:T(8,128)(2,1)} %bitcast.69, s32[]{:T(128)S(6)} %select_n.95), kind=kLoop, calls=%fused_computation.16 | loop fusion | bytes 6488068 | tf_op jit(solution)/shard_map/jit(dynamic_index_in_dim)/squeeze | solution.py:50
  168.4 1.6 all-to-all-done.4
  170.0 2.0 copy.105
  172.0 1.9 reshape.425
  173.9 7.5 %multiply_reduce_fusion = (f32[3,1024]{1,0:T(4,128)S(1)}, f32[3,1024,1024]{1,2,0:T(8,128)S(1)}) fusion(f32[3,1024,1024]{1,2,0:T(8,128)} %copy-done, f32[3,1024]{1,0:T(4,128)S(1)} %log_add_fusion, bf16[1024,3,64]{0,2,1:T(8,128)(2,1)} %reshape.425, f32[1024,3,3,64]{0,3,2,1:T(8,128)} %copy-done.2), kind=kOutput, calls=%fused_computation.1 | convolution fusion | flops 412087296 | bytes 25976832 | tf_op jit(solution)/shard_map/qhd,khd->hqk/dot_general | solution.py:118
  181.5 6.8 %multiply_convert_fusion = bf16[3,1024,1024]{1,2,0:T(8,128)(2,1)S(1)} fusion(f32[3,1024,1024]{1,2,0:T(8,128)S(1)} %get-tuple-element.80, f32[3,1024,1024]{1,2,0:T(8,128)} %copy-done, f32[3,1024]{1,0:T(4,128)S(1)} %get-tuple-element.79, f32[3,1024]{1,0:T(4,128)S(1)} %log_add_fusion), kind=kLoop, calls=%fused_computation | loop fusion | flops 12582912 | bytes 31481856 | tf_op jit(solution)/shard_map/convert_element_type | solution.py:59
  188.3 2.0 broadcast_multiply_fusion
  193.5 2.0 fusion.12
  195.6 3.0 multiply_reduce_fusion.1
  198.6 2.0 convolution_convert_fusion.3
  206.3 2.0 fusion.23
  208.2 13.1 %all-to-all-start.6 = ((bf16[8,48,640]{2,1,0:T(8,128)(2,1)}), bf16[8,48,640]{2,1,0:T(8,128)(2,1)S(1)}, u32[]{:S(2)}, u32[]{:S(2)}) async-start(bf16[8,48,640]{2,1,0:T(8,128)(2,1)} %fusion.23), calls=%async_computation.6 | async-start | bytes 983040 | tf_op jit(solution)/shard_map/all_to_all | solution.py:54
  221.4 5.4 %fusion.2 = bf16[8,264,768]{2,1,0:T(8,128)(2,1)} fusion(bf16[8,264,768]{2,1,0:T(8,128)(2,1)} %collective-permute-done.3, bf16[8,2,264,768]{3,2,1,0:T(8,128)(2,1)} %bitcast.69, s32[]{:T(128)S(6)} %select_n.94), kind=kLoop, calls=%fused_computation.9 | loop fusion | flops 6488064 | bytes 9732100 | tf_op jit(solution)/shard_map/convert_element_type | solution.py:59
  226.8 6.0 %all-to-all-done.6 = bf16[8,48,640]{2,1,0:T(8,128)(2,1)S(1)} async-done(((bf16[8,48,640]{2,1,0:T(8,128)(2,1)}), bf16[8,48,640]{2,1,0:T(8,128)(2,1)S(1)}, u32[]{:S(2)}, u32[]{:S(2)}) %all-to-all-start.6) | async-done | bytes 491552 | tf_op jit(solution)/shard_map/all_to_all | solution.py:54
  232.8 44.6 %all_to_all.50 = bf16[8,264,768]{2,1,0:T(8,128)(2,1)} all-to-all(bf16[8,264,768]{2,1,0:T(8,128)(2,1)} %fusion.2), channel_id=1, replica_groups={{0,2,4,6,8,10,12,14},{1,3,5,7,9,11,13,15},{16,18,20,22,24,26,28,30},{17..., dimensions={0} | all-to-all | bytes 6488064 | tf_op jit(solution)/shard_map/all_to_all | solution.py:54
  277.4 3.6 %all-to-all-start.5 = ((bf16[8,128,768]{2,1,0:T(8,128)(2,1)}), bf16[8,128,768]{2,1,0:T(8,128)(2,1)S(1)}, u32[]{:S(2)}, u32[]{:S(2)}) async-start(bf16[8,128,768]{2,1,0:T(8,128)(2,1)} %bitcast.207), calls=%async_computation.5 | async-start | bytes 3145728 | tf_op jit(solution)/shard_map/all_to_all | solution.py:280
  281.4 3.2 reduce_sum.205
  284.6 1.9 reshape.435
  286.5 15.8 %all-to-all-done.5 = bf16[8,128,768]{2,1,0:T(8,128)(2,1)S(1)} async-done(((bf16[8,128,768]{2,1,0:T(8,128)(2,1)}), bf16[8,128,768]{2,1,0:T(8,128)(2,1)S(1)}, u32[]{:S(2)}, u32[]{:S(2)}) %all-to-all-start.5) | async-done | bytes 1572896 | tf_op jit(solution)/shard_map/all_to_all | solution.py:280
  302.4 4.1 %all-to-all-start.8 = ((bf16[8,33,768]{2,1,0:T(8,128)(2,1)}), bf16[8,33,768]{2,1,0:T(8,128)(2,1)}, u32[]{:S(2)}, u32[]{:S(2)}) async-start(bf16[8,33,768]{2,1,0:T(8,128)(2,1)} %reshape.435), calls=%async_computation.8 | async-start | bytes 983040 | tf_op jit(solution)/shard_map/all_to_all | solution.py:291
  306.5 3.1 fusion.10
  311.6 4.7 %all-to-all-done.8 = bf16[8,33,768]{2,1,0:T(8,128)(2,1)} async-done(((bf16[8,33,768]{2,1,0:T(8,128)(2,1)}), bf16[8,33,768]{2,1,0:T(8,128)(2,1)}, u32[]{:S(2)}, u32[]{:S(2)}) %all-to-all-start.8) | async-done | bytes 405536 | tf_op jit(solution)/shard_map/all_to_all | solution.py:291
  319.3 3.6 %all-to-all-start.9 = ((bf16[8,73,768]{2,1,0:T(8,128)(2,1)}), bf16[8,73,768]{2,1,0:T(8,128)(2,1)S(1)}, u32[]{:S(2)}, u32[]{:S(2)}) async-start(bf16[8,73,768]{2,1,0:T(8,128)(2,1)} %broadcast_in_dim.63), calls=%async_computation.9 | async-start | bytes 1966080 | tf_op jit(solution)/shard_map/all_to_all | solution.py:21
  324.4 13.6 %all-to-all-done.9 = bf16[8,73,768]{2,1,0:T(8,128)(2,1)S(1)} async-done(((bf16[8,73,768]{2,1,0:T(8,128)(2,1)}), bf16[8,73,768]{2,1,0:T(8,128)(2,1)S(1)}, u32[]{:S(2)}, u32[]{:S(2)}) %all-to-all-start.9) | async-done | bytes 897056 | tf_op jit(solution)/shard_map/all_to_all | solution.py:21
  (194 shorter events, 59.8 us)
Async XLA Ops:
  0.6 12.8 %copy-start.23 = (bf16[48,2304]{1,0:T(8,128)(2,1)S(1)}, bf16[48,2304]{1,0:T(8,128)(2,1)}, u32[]{:S(2)}) copy-start(bf16[48,2304]{1,0:T(8,128)(2,1)} %param.17) | copy-start | bytes 663556
  0.6 12.9 %copy-start.35 = (s32[8]{0:T(128)S(1)}, s32[8]{0:T(128)}, u32[]{:S(2)}) copy-start(s32[8]{0:T(128)} %param.12) | copy-start | bytes 100
  0.7 24.2 %copy-start.1 = (bf16[2,128,768]{2,1,0:T(8,128)(2,1)S(1)}, bf16[2,128,768]{2,1,0:T(8,128)(2,1)}, u32[]{:S(2)}) copy-start(bf16[2,128,768]{2,1,0:T(8,128)(2,1)} %param.10) | copy-start | bytes 1179652
  4.2 21.9 %copy-start.31 = (bf16[640]{0:T(1024)(128)(2,1)}, bf16[640]{0:T(1024)(128)(2,1)S(1)}, u32[]{:S(2)}) copy-start(bf16[640]{0:T(1024)(128)(2,1)S(1)} %pad.44.clone) | copy-start | bytes 3844
  5.1 19.7 %all-to-all-start.1 = ((bf16[8,48,640]{2,1,0:T(8,128)(2,1)}), bf16[8,48,640]{2,1,0:T(8,128)(2,1)S(1)}, u32[]{:S(2)}, u32[]{:S(2)}) async-start(bf16[8,48,640]{2,1,0:T(8,128)(2,1)} %broadcast_in_dim.51), calls=%async_computation.1 | async-start | bytes 983040 | tf_op jit(solution)/shard_map/all_to_all | solution.py:34
  13.5 19.5 %copy-start.26 = (bf16[48,768]{1,0:T(8,128)(2,1)S(1)}, bf16[48,768]{1,0:T(8,128)(2,1)}, u32[]{:S(2)}) copy-start(bf16[48,768]{1,0:T(8,128)(2,1)} %param.15) | copy-start | bytes 221188
  13.5 19.5 %copy-start.36 = (s32[2]{0:T(128)S(1)}, s32[2]{0:T(128)}, u32[]{:S(2)}) copy-start(s32[2]{0:T(128)} %param.11) | copy-start | bytes 28
  13.6 20.1 %copy-start.25 = (bf16[72,768]{1,0:T(8,128)(2,1)S(1)}, bf16[72,768]{1,0:T(8,128)(2,1)}, u32[]{:S(2)}) copy-start(bf16[72,768]{1,0:T(8,128)(2,1)} %param.18) | copy-start | bytes 331780
  26.1 25.9 %all-to-all-start = ((bf16[8,128,768]{2,1,0:T(8,128)(2,1)}), bf16[8,128,768]{2,1,0:T(8,128)(2,1)S(1)}, u32[]{:S(2)}, u32[]{:S(2)}) async-start(bf16[8,128,768]{2,1,0:T(8,128)(2,1)} %bitcast.3), calls=%async_computation | async-start | bytes 3145728 | tf_op jit(solution)/shard_map/all_to_all | solution.py:166
  31.9 3.4 collective-permute-start
  33.6 2.7 copy-start.22
  36.6 27.1 %copy-start.4 = (bf16[8,2,48,640]{3,2,1,0:T(8,128)(2,1)}, bf16[8,2,48,640]{3,2,1,0:T(8,128)(2,1)S(1)}, u32[]{:S(2)}) copy-start(bf16[8,2,48,640]{3,2,1,0:T(8,128)(2,1)S(1)} %copy.92) | copy-start | bytes 2949124
  54.9 45.4 %all-to-all-start.3 = ((bf16[8,264,768]{2,1,0:T(8,128)(2,1)}), bf16[8,264,768]{2,1,0:T(8,128)(2,1)}, u32[]{:S(2)}, u32[]{:S(2)}) async-start(bf16[8,264,768]{2,1,0:T(8,128)(2,1)} %broadcast_in_dim.59), calls=%async_computation.3 | async-start | bytes 6488064 | tf_op jit(solution)/shard_map/all_to_all | solution.py:34
  60.4 7.6 %copy-start.13 = (f32[1024,64]{0,1:T(8,128)}, f32[1024,64]{0,1:T(8,128)S(1)}, u32[]{:S(2)}) copy-start(f32[1024,64]{0,1:T(8,128)S(1)} %pad_maximum_fusion.17) | copy-start | bytes 786436
  64.0 2.6 copy-start.27
  64.8 1.7 copy-start.20
  69.6 34.3 %copy-start.8 = (bf16[1024,3,64]{0,2,1:T(8,128)(2,1)}, bf16[1024,3,64]{0,2,1:T(8,128)(2,1)S(1)}, u32[]{:S(2)}) copy-start(bf16[1024,3,64]{0,2,1:T(8,128)(2,1)S(1)} %get-tuple-element.40) | copy-start | bytes 1179652
  69.6 34.3 %copy-start.10 = (bf16[1024,3,64]{0,2,1:T(8,128)(2,1)}, bf16[1024,3,64]{0,2,1:T(8,128)(2,1)S(1)}, u32[]{:S(2)}) copy-start(bf16[1024,3,64]{0,2,1:T(8,128)(2,1)S(1)} %get-tuple-element.41) | copy-start | bytes 1179652
  100.2 25.8 %collective-permute-start.1 = (bf16[8,264,768]{2,1,0:T(8,128)(2,1)}, bf16[8,264,768]{2,1,0:T(8,128)(2,1)}, u32[]{:S(2)}, u32[]{:S(2)}) collective-permute-start(bf16[8,264,768]{2,1,0:T(8,128)(2,1)} %all-to-all-done.3), channel_id=1, source_target_pairs={{0,1},{1,0},{2,3},{3,2},{4,5},{5,4},{6,7},{7,6},{8,9},{9,8},{10,11... | collective-permute-start | bytes 9732104 | tf_op jit(solution)/shard_map/ppermute | solution.py:41
  103.9 4.6 %copy-start = (f32[3,1024,1024]{1,2,0:T(8,128)}, f32[3,1024,1024]{1,2,0:T(8,128)S(1)}, u32[]{:S(2)}) copy-start(f32[3,1024,1024]{1,2,0:T(8,128)S(1)} %get-tuple-element.75) | copy-start | bytes 37748740
  103.9 4.7 %copy-start.24 = (f32[3,1024]{1,0:T(4,128)}, f32[3,1024]{1,0:T(4,128)S(1)}, u32[]{:S(2)}) copy-start(f32[3,1024]{1,0:T(4,128)S(1)} %get-tuple-element.74) | copy-start | bytes 36868
  108.7 3.5 %copy-start.30 = (f32[3,1024]{1,0:T(4,128)}, f32[3,1024]{1,0:T(4,128)S(1)}, u32[]{:S(2)}) copy-start(f32[3,1024]{1,0:T(4,128)S(1)} %fusion) | copy-start | bytes 36868
  113.1 12.5 %all-to-all-start.2 = ((bf16[8,128,192]{1,2,0:T(8,128)(2,1)}), bf16[8,128,192]{1,2,0:T(8,128)(2,1)S(1)}, u32[]{:S(2)}, u32[]{:S(2)}) async-start(bf16[8,128,192]{1,2,0:T(8,128)(2,1)} %copy.95), calls=%async_computation.2 | async-start | bytes 786432 | tf_op jit(solution)/shard_map/all_to_all | solution.py:192
  130.4 2.6 copy-start.3
  148.2 2.3 copy-start.15
  148.2 2.3 copy-start.18
  152.4 2.3 copy-start.6
  157.1 12.9 %all-to-all-start.4 = ((bf16[8,128,192]{1,2,0:T(8,128)(2,1)}), bf16[8,128,192]{1,2,0:T(8,128)(2,1)}, u32[]{:S(2)}, u32[]{:S(2)}) async-start(bf16[8,128,192]{1,2,0:T(8,128)(2,1)} %bitcast.209), calls=%async_computation.4 | async-start | bytes 786432 | tf_op jit(solution)/shard_map/all_to_all | solution.py:252
  167.5 53.9 %collective-permute-start.3 = (bf16[8,264,768]{2,1,0:T(8,128)(2,1)}, bf16[8,264,768]{2,1,0:T(8,128)(2,1)}, u32[]{:S(2)}, u32[]{:S(2)}) collective-permute-start(bf16[8,264,768]{2,1,0:T(8,128)(2,1)} %dynamic-slice_bitcast_fusion), channel_id=1, source_target_pairs={{0,1},{1,0},{2,3},{3,2},{4,5},{5,4},{6,7},{7,6},{8,9},{9,8},{10,11... | collective-permute-start | bytes 9732104 | tf_op jit(solution)/shard_map/ppermute | solution.py:52
  181.5 6.8 %copy-start.11 = (bf16[1024,3,64]{0,2,1:T(8,128)(2,1)S(1)}, bf16[1024,3,64]{0,2,1:T(8,128)(2,1)}, u32[]{:S(2)}) copy-start(bf16[1024,3,64]{0,2,1:T(8,128)(2,1)} %copy-done.10) | copy-start | bytes 1179652
  181.5 8.9 %copy-start.9 = (bf16[1024,3,64]{0,2,1:T(8,128)(2,1)S(1)}, bf16[1024,3,64]{0,2,1:T(8,128)(2,1)}, u32[]{:S(2)}) copy-start(bf16[1024,3,64]{0,2,1:T(8,128)(2,1)} %copy-done.8) | copy-start | bytes 1179652
  188.3 5.2 %slice-start = ((s8[12582912]{0:T(1024)(128)(4,1)}), s8[4194304]{0:T(1024)(128)(4,1)S(1)}, s32[]{:S(2)}) async-start(s8[12582912]{0:T(1024)(128)(4,1)} %bitcast.187), calls=%async_computation.10 | async-start | bytes 8388608
  188.3 5.2 %slice-start.1 = ((s8[12582912]{0:T(1024)(128)(4,1)}), s8[4194304]{0:T(1024)(128)(4,1)S(1)}, s32[]{:S(2)}) async-start(s8[12582912]{0:T(1024)(128)(4,1)} %bitcast.187), calls=%async_computation.11 | async-start | bytes 8388608
  190.4 3.1 slice-start.2
  191.8 1.7 copy-start.7
  193.5 2.1 copy-start.5
  193.5 2.1 copy-start.28
  193.5 2.1 copy-start.33
  193.5 2.1 copy-start.34
  198.6 3.9 %copy-start.21 = (bf16[8,2,48,1]{3,2,1,0:T(8,128)(2,1)S(1)}, bf16[8,2,48,1]{3,2,1,0:T(8,128)(2,1)}, u32[]{:S(2)}) copy-start(bf16[8,2,48,1]{3,2,1,0:T(8,128)(2,1)} %convert_element_type.242) | copy-start | bytes 4612
  198.6 3.9 %copy-start.32 = (bf16[640]{0:T(1024)(128)(2,1)S(1)}, bf16[640]{0:T(1024)(128)(2,1)}, u32[]{:S(2)}) copy-start(bf16[640]{0:T(1024)(128)(2,1)} %copy-done.31) | copy-start | bytes 3844
  203.9 2.4 collective-permute-start.2
  208.2 24.5 %all-to-all-start.6 = ((bf16[8,48,640]{2,1,0:T(8,128)(2,1)}), bf16[8,48,640]{2,1,0:T(8,128)(2,1)S(1)}, u32[]{:S(2)}, u32[]{:S(2)}) async-start(bf16[8,48,640]{2,1,0:T(8,128)(2,1)} %fusion.23), calls=%async_computation.6 | async-start | bytes 983040 | tf_op jit(solution)/shard_map/all_to_all | solution.py:54
  232.8 44.6 %copy-start.16 = (bf16[8,48,640]{2,1,0:T(8,128)(2,1)}, bf16[8,48,640]{2,1,0:T(8,128)(2,1)S(1)}, u32[]{:S(2)}) copy-start(bf16[8,48,640]{2,1,0:T(8,128)(2,1)S(1)} %all-to-all-done.6) | copy-start | bytes 1474564
  277.4 24.9 %all-to-all-start.5 = ((bf16[8,128,768]{2,1,0:T(8,128)(2,1)}), bf16[8,128,768]{2,1,0:T(8,128)(2,1)S(1)}, u32[]{:S(2)}, u32[]{:S(2)}) async-start(bf16[8,128,768]{2,1,0:T(8,128)(2,1)} %bitcast.207), calls=%async_computation.5 | async-start | bytes 3145728 | tf_op jit(solution)/shard_map/all_to_all | solution.py:280
  302.4 14.0 %all-to-all-start.8 = ((bf16[8,33,768]{2,1,0:T(8,128)(2,1)}), bf16[8,33,768]{2,1,0:T(8,128)(2,1)}, u32[]{:S(2)}, u32[]{:S(2)}) async-start(bf16[8,33,768]{2,1,0:T(8,128)(2,1)} %reshape.435), calls=%async_computation.8 | async-start | bytes 983040 | tf_op jit(solution)/shard_map/all_to_all | solution.py:291
  311.6 11.3 %copy-start.29 = (f32[768]{0:T(1024)S(1)}, f32[768]{0:T(1024)}, u32[]{:S(2)}) copy-start(f32[768]{0:T(1024)} %copy-done.27) | copy-start | bytes 9220
  319.3 18.6 %all-to-all-start.9 = ((bf16[8,73,768]{2,1,0:T(8,128)(2,1)}), bf16[8,73,768]{2,1,0:T(8,128)(2,1)S(1)}, u32[]{:S(2)}, u32[]{:S(2)}) async-start(bf16[8,73,768]{2,1,0:T(8,128)(2,1)} %broadcast_in_dim.63), calls=%async_computation.9 | async-start | bytes 1966080 | tf_op jit(solution)/shard_map/all_to_all | solution.py:21
  (5 other events, 6.2 us)
where the time goes:
time: 352 us; the launch traced here: 345 us
  waiting for transfers between devices  108 us (31%)
  local copies, waits for them, and re-layouts  55.1 us (16%)
  starting transfers between devices  53.6 us (15%)
  blocking collectives  44.6 us (13%)
  other arithmetic  41 us (12%)
  matrix products  39.7 us (11%)
    all_to_all x1, blocking collectives, reduce_two_level(): lax.all_to_all(both, axis, 0, 0, tiled=True, axis_index_groups=core_group...  44.6 us
    all_to_all x2, waiting for transfers between devices, gather_two_level(): lax.all_to_all(jnp.broadcast_to(part[None], (n // 2, *part.shape)), axis,...  41.9 us
    all_to_all x1, waiting for transfers between devices, body(): lax.all_to_all(low(grad_a_part).reshape(ctx, local_len, width), 'ctx', 0,...  15.8 us
    all_to_all x1, waiting for transfers between devices, body(): lax.all_to_all(jnp.repeat(tokens, spread, axis=0), 'ctx', 0, 0, tiled=True)  15.4 us
    convert_element_type x5, other arithmetic, low(): return values.astype(jnp.bfloat16)  15.1 us
    all_to_all x1, waiting for transfers between devices, gather_by_exchange(): lax.all_to_all(jnp.broadcast_to(part[None], (n, *part.shape)), axis, 0, 0)  13.6 us
    all_to_all x1, starting transfers between devices, reduce_two_level(): lax.all_to_all(both, axis, 0, 0, tiled=True, axis_index_groups=core_group...  13.1 us
    all_to_all x2, starting transfers between devices, gather_two_level(): lax.all_to_all(jnp.broadcast_to(part[None], (n // 2, *part.shape)), axis,...  12.8 us
  transfers between devices with their start and end apart: 13, of which 10 were waited for; matrix products, arithmetic and copies ran while one was open for 23% of the time, Pallas kernels for 0%

commit v1 on v0

--- a/solution.py
+++ b/solution.py
@@ -29,30 +29,28 @@
     return [list(range(first, n, 2)) for first in range(2)]
 
 
-def gather_two_level(part, axis):
+def gather_doubling(part, axis):
     n = lax.axis_size(axis)
-    mine = lax.all_to_all(
-        jnp.broadcast_to(part[None], (n // 2, *part.shape)),
-        axis,
-        0,
-        0,
-        axis_index_groups=core_groups(n),
-    )
-    other = lax.ppermute(mine, axis, core_pairs(n))
-    even = lax.axis_index(axis) % 2 == 0
-    return jnp.where(even, mine, other), jnp.where(even, other, mine)
-
-
-def reduce_two_level(parts, axis):
+    index = lax.axis_index(axis)
+    held = part[None]
+    bit = n // 2
+    while bit:
+        came = lax.ppermute(held, axis, [(k, k ^ bit) for k in range(n)])
+        first = (index & bit) == 0
+        held = jnp.where(first, jnp.stack([held, came], 1), jnp.stack([came, held], 1))
+        held = held.reshape(-1, *part.shape)
+        bit //= 2
+    return held
+
+
+def core_sum(parts, axis):
     n = lax.axis_size(axis)
     core = lax.axis_index(axis) % 2
     paired = parts.reshape(n // 2, 2, *parts.shape[1:])
     away = lax.dynamic_index_in_dim(paired, 1 - core, 1, keepdims=False)
     kept = lax.dynamic_index_in_dim(paired, core, 1, keepdims=False)
     came = lax.ppermute(away, axis, core_pairs(n))
-    both = low(kept.astype(jnp.float32) + came.astype(jnp.float32))
-    shares = lax.all_to_all(both, axis, 0, 0, tiled=True, axis_index_groups=core_groups(n))
-    return low(jnp.sum(shares.astype(jnp.float32), 0))
+    return low(kept.astype(jnp.float32) + came.astype(jnp.float32))
 
 
 def low(values):
@@ -160,8 +158,8 @@
     ).reshape(depth, 3 * span)
     gains_wide = jnp.stack([gain_attn, gain_mlp], 1)
     fill = jnp.zeros((depth, 640 - 3 * span - 2), jnp.bfloat16)
-    first_all = jnp.stack(
-        gather_two_level(jnp.concatenate([qkv_own, gains_wide, fill], 1), "fsdp"), 1
+    first_all = gather_doubling(
+        jnp.concatenate([qkv_own, gains_wide, fill], 1), "fsdp"
     ).reshape(fsdp * depth, 640)
     sequence = lax.all_to_all(jnp.repeat(tokens, spread, axis=0), "ctx", 0, 0, tiled=True)
 
@@ -172,8 +170,7 @@
     count = w_in.shape[1] // width
     pieces = [w_in[:, k * width : (k + 1) * width] for k in range(count)]
     stacked = jnp.concatenate([*pieces, w_out, w_down], 0)
-    stacked, first_all = lax.optimization_barrier((stacked, first_all))
-    stacked_all = gather_two_level(stacked, "fsdp")
+    stacked_all = lax.all_gather(stacked, "fsdp", axis=0)
 
     cosine, sine = tables(all_pos)
     cosine = cosine[:, None, :]
@@ -195,8 +192,7 @@
     )
 
     def whole(start, height):
-        halves = [part[:, start : start + height] for part in stacked_all]
-        return jnp.stack(halves, 1).reshape(fsdp * height, width)
+        return stacked_all[:, start : start + height].reshape(fsdp * height, width)
 
     win_all = jnp.concatenate([whole(k * depth, depth) for k in range(count)], 1)
     wout_all = whole(count * depth, depth)
@@ -236,21 +232,27 @@
         .transpose(0, 2, 1, 3)
         .reshape(ctx, local_len, span)
     )
-    grads_stacked = jnp.concatenate(
+    main_rows = ((count + 1) * depth + down_rows) // (8 * ctx) * 8 * ctx
+    chunk = main_rows // ctx
+    grad_wdown = low(grad_wdown).reshape(fsdp, down_rows, width)
+    split = main_rows - (count + 1) * depth
+    grads_main = jnp.concatenate(
         [
             *[
                 grad_win[:, k * width : (k + 1) * width].reshape(fsdp, depth, width)
                 for k in range(count)
             ],
             low(grad_wout).reshape(fsdp, depth, width),
-            low(grad_wdown).reshape(fsdp, down_rows, width),
+            grad_wdown[:, :split],
         ],
         1,
     )
-    grads_stacked, grad_heads = lax.optimization_barrier((grads_stacked, grad_heads))
+    main_pair = core_sum(grads_main, "fsdp")
+    main_pair = main_pair.reshape(fsdp // 2, ctx, chunk, width).transpose(1, 0, 2, 3)
+    main_part = lax.psum_scatter(main_pair, "ctx", scatter_dimension=0, tiled=True)
+    main_part = main_part.reshape(fsdp // 2, chunk, width)
 
     all_grad = lax.all_to_all(grad_heads, "ctx", 0, 0, tiled=True).reshape(full_len, group, HD)
-    grads_part = reduce_two_level(grads_stacked, "fsdp")
     grad_query, grad_key, grad_value = attention_backward(
         query, keys, values, all_grad, log_total, all_keep, factor
     )
@@ -275,8 +277,11 @@
         ],
         1,
     )
-    last = reduce_two_level(last.reshape(fsdp, depth, 640), "fsdp")
-    last_rows = last.size // width
+    last = jnp.concatenate(
+        [last.reshape(fsdp, -1, width), grad_wdown[:, split:]], 1
+    )
+    last = core_sum(last, "fsdp")
+    last_rows = last.shape[1]
     grad_a_parts = lax.all_to_all(
         low(grad_a_part).reshape(ctx, local_len, width), "ctx", 0, 0, tiled=True
     )
@@ -287,14 +292,20 @@
     grad_norm_one, _ = norm_backward(grad_a, gain_one, normed_one, inverse_one)
     grad_input = grad_mixed + grad_norm_one
 
-    own_rows = grads_part.shape[0] // ctx
-    shares = lax.all_to_all(grads_part.reshape(ctx, own_rows, width), "ctx", 0, 0, tiled=True)
+    shares = lax.all_to_all(
+        jnp.concatenate([last, main_part], 1),
+        "fsdp",
+        0,
+        0,
+        tiled=True,
+        axis_index_groups=core_groups(fsdp),
+    )
     share = low(jnp.sum(shares.astype(f32), 0))
-    ends = gather_by_exchange(
-        jnp.concatenate([last.reshape(last_rows, width), share], 0), "ctx", ctx
-    )
-    last_all = ends[:, :last_rows].reshape(ctx, depth, 640).astype(f32)
-    summed = ends[:, last_rows:].reshape(ctx * own_rows, width).astype(f32)
+    ends = gather_by_exchange(share, "ctx", ctx)
+    extra = down_rows - split
+    last_all = ends[:, : last_rows - extra].reshape(ctx, depth, 640).astype(f32)
+    down_end = jnp.sum(ends[:, last_rows - extra : last_rows].astype(f32), 0)
+    summed = ends[:, last_rows:].reshape(main_rows, width).astype(f32)
     grad_wqkv_out = (
         jnp.sum(last_all[:, :, : 3 * span].reshape(seqs, spread, depth, 3, span), 0)
         .transpose(1, 2, 0, 3)
@@ -309,7 +320,7 @@
         summed[count * depth : (count + 1) * depth],
         gains_out[:, 1],
         jnp.concatenate([summed[k * depth : (k + 1) * depth] for k in range(count)], 1),
-        summed[(count + 1) * depth :],
+        jnp.concatenate([summed[(count + 1) * depth :], down_end], 0),
     )
 
 

time: 352 us -> 275 us (0.78)
  blocking collectives: 44.6 us -> 0 us
  waiting for transfers between devices: 108 us -> 87.2 us
  starting transfers between devices: 53.6 us -> 39.5 us
  between operations: 2.8 us -> 16.1 us
  other arithmetic: 41 us -> 34.9 us
    all_to_all x1 -> x0, blocking collectives: 44.6 us -> none  [reduce_two_level(): lax.all_to_all(both, axis, 0, 0, tiled=True, axis_index_groups=core_group...]
    all_to_all x4 -> x1, waiting for transfers between devices: 52.6 us -> 10.1 us  [body(): lax.all_to_all(jnp.concatenate([last, main_part], 1), 'fsdp', 0, 0, tiled...]
    all_to_all x4 -> x1, starting transfers between devices: 30.1 us -> 5.8 us  [body(): lax.all_to_all(jnp.concatenate([last, main_part], 1), 'fsdp', 0, 0, tiled...]
    all_gather x0 -> x1, waiting for transfers between devices: none -> 19.6 us  [body(): stacked_all = lax.all_gather(stacked, 'fsdp', axis=0)]
    all_to_all x1, waiting for transfers between devices: 15.4 us -> 0.01 us  [body(): lax.all_to_all(jnp.repeat(tokens, spread, axis=0), 'ctx', 0, 0, tiled=True)]
    reduce_scatter x0 -> x1, waiting for transfers between devices: none -> 13.8 us  [body(): lax.psum_scatter(main_pair, 'ctx', scatter_dimension=0, tiled=True)]
    all_to_all x1, waiting for transfers between devices: 15.8 us -> 2.87 us  [body(): lax.all_to_all(low(grad_a_part).reshape(ctx, local_len, width), 'ctx', 0,...]
    ppermute x4 -> x6, waiting for transfers between devices: 1.5 us -> 13.5 us  [the longest x4 12 us: gather_doubling(): came = lax.ppermute(held, axis, [(k, k ^ bit) for k in range(n)])]
  transfers between devices with their start and end apart: 13 -> 14, of which waited for: 10 -> 10; matrix products, arithmetic and copies ran while one was open for 23% -> 30% of each run, Pallas kernels for 0% -> 0%
where the time goes in v1:
time: 275 us; the launch traced here: 270 us
  waiting for transfers between devices  87.2 us (32%)
  local copies, waits for them, and re-layouts  56 us (20%)
  starting transfers between devices  39.5 us (14%)
  matrix products  36.7 us (13%)
  other arithmetic  34.9 us (13%)
  between operations  16.1 us (6%)
    all_gather x1, waiting for transfers between devices, body(): stacked_all = lax.all_gather(stacked, 'fsdp', axis=0)  19.6 us
    reduce_scatter x1, waiting for transfers between devices, body(): lax.psum_scatter(main_pair, 'ctx', scatter_dimension=0, tiled=True)  13.8 us
    unnamed x103, local copies, waits for them, and re-layouts  13.4 us
    all_to_all x1, waiting for transfers between devices, gather_by_exchange(): lax.all_to_all(jnp.broadcast_to(part[None], (n, *part.shape)), axis, 0, 0)  13.1 us
    convert_element_type x5, other arithmetic, low(): return values.astype(jnp.bfloat16)  12.4 us
    ppermute x4, waiting for transfers between devices, gather_doubling(): came = lax.ppermute(held, axis, [(k, k ^ bit) for k in range(n)])  12 us
    ppermute x4, starting transfers between devices, gather_doubling(): came = lax.ppermute(held, axis, [(k, k ^ bit) for k in range(n)])  10.3 us
    all_to_all x1, waiting for transfers between devices, body(): lax.all_to_all(jnp.concatenate([last, main_part], 1), 'fsdp', 0, 0, tiled...  10.1 us
  transfers between devices with their start and end apart: 14, of which 10 were waited for; matrix products, arithmetic and copies ran while one was open for 30% of the time, Pallas kernels for 0%

profile of v1, /device:TPU:1, one launch (start us, length us, event | category | flops | bytes accessed | tf_op | source)
XLA Modules:
  0.0 270.5 jit_solution(14993967127064614335)
XLA Ops:
  16.1 4.5 %collective-permute-start = (bf16[1,48,640]{2,1,0:T(8,128)(2,1)S(1)}, bf16[1,48,640]{2,1,0:T(8,128)(2,1)S(1)}, u32[]{:S(2)}, u32[]{:S(2)}) collective-permute-start(bf16[1,48,640]{2,1,0:T(8,128)(2,1)S(1)} %get-tuple-element.51), channel_id=1, source_target_pairs={{0,8},{1,9},{2,10},{3,11},{4,12},{5,13},{6,14},{7,15},{8,0},{9,1},... | collective-permute-start | bytes 184328 | tf_op jit(solution)/shard_map/ppermute | solution.py:38
  21.9 4.5 %all-to-all-start = ((bf16[8,128,768]{2,1,0:T(8,128)(2,1)}), bf16[8,128,768]{2,1,0:T(8,128)(2,1)S(1)}, u32[]{:S(2)}, u32[]{:S(2)}) async-start(bf16[8,128,768]{2,1,0:T(8,128)(2,1)} %bitcast.3), calls=%async_computation | async-start | bytes 3145728 | tf_op jit(solution)/shard_map/all_to_all | solution.py:164
  26.4 3.0 %collective-permute-start.1 = (bf16[2,48,640]{2,1,0:T(8,128)(2,1)S(1)}, bf16[2,48,640]{2,1,0:T(8,128)(2,1)S(1)}, u32[]{:S(2)}, u32[]{:S(2)}) collective-permute-start(bf16[2,48,640]{2,1,0:T(8,128)(2,1)S(1)} %maximum_select_fusion.4), channel_id=1, source_target_pairs={{0,4},{1,5},{2,6},{3,7},{4,0},{5,1},{6,2},{7,3},{8,12},{9,13},{10,... | collective-permute-start | bytes 368648 | tf_op jit(solution)/shard_map/ppermute | solution.py:38
  29.4 5.8 %collective-permute-done.1 = bf16[2,48,640]{2,1,0:T(8,128)(2,1)S(1)} collective-permute-done((bf16[2,48,640]{2,1,0:T(8,128)(2,1)S(1)}, bf16[2,48,640]{2,1,0:T(8,128)(2,1)S(1)}, u32[]{:S(2)}, u32[]{:S(2)}) %collective-permute-start.1) | collective-permute-done | bytes 122912 | tf_op jit(solution)/shard_map/ppermute | solution.py:38
  35.8 6.2 %collective-permute-done.2 = bf16[4,48,640]{2,1,0:T(8,128)(2,1)S(1)} collective-permute-done((bf16[4,48,640]{2,1,0:T(8,128)(2,1)S(1)}, bf16[4,48,640]{2,1,0:T(8,128)(2,1)S(1)}, u32[]{:S(2)}, u32[]{:S(2)}) %collective-permute-start.2) | collective-permute-done | bytes 245792 | tf_op jit(solution)/shard_map/ppermute | solution.py:38
  42.1 2.3 collective-permute-start.3
  49.8 2.2 copy.120
  56.8 2.4 fusion.70
  59.2 1.7 fusion
  60.9 2.9 %copy-done = f32[3,1024,1024]{1,2,0:T(8,128)} copy-done((f32[3,1024,1024]{1,2,0:T(8,128)}, f32[3,1024,1024]{1,2,0:T(8,128)S(1)}, u32[]{:S(2)}) %copy-start) | copy-done | bytes 12582936
  63.9 2.3 fusion.16
  67.1 5.1 %all-to-all-start.1 = ((bf16[8,128,192]{1,2,0:T(8,128)(2,1)}), bf16[8,128,192]{1,2,0:T(8,128)(2,1)S(1)}, u32[]{:S(2)}, u32[]{:S(2)}) async-start(bf16[8,128,192]{1,2,0:T(8,128)(2,1)} %copy.122), calls=%async_computation.1 | async-start | bytes 786432 | tf_op jit(solution)/shard_map/all_to_all | solution.py:189
  72.2 9.0 %all-to-all-done.1 = bf16[8,128,192]{1,2,0:T(8,128)(2,1)S(1)} async-done(((bf16[8,128,192]{1,2,0:T(8,128)(2,1)}), bf16[8,128,192]{1,2,0:T(8,128)(2,1)S(1)}, u32[]{:S(2)}, u32[]{:S(2)}) %all-to-all-start.1) | async-done | bytes 393248 | tf_op jit(solution)/shard_map/all_to_all | solution.py:189
  81.6 19.6 %all-gather.3.cloned.1.call-done = bf16[4224,768]{1,0:T(8,128)(2,1)} async-done(((bf16[264,768]{1,0:T(8,128)(2,1)}), bf16[4224,768]{1,0:T(8,128)(2,1)}) %all-gather.3.cloned.1.call-update) | async-done | bytes 6488080 | tf_op jit(solution)/shard_map/all_gather | solution.py:173
  101.2 1.6 slice.185
  102.8 3.3 %fusion.67 = (bf16[16,48,768]{2,1,0:T(8,128)(2,1)S(1)}, bf16[16,48,768]{2,1,0:T(8,128)(2,1)S(1)}, bf16[16,48,768]{2,1,0:T(8,128)(2,1)S(1)}, bf16[16,48,768]{2,1,0:T(8,128)(2,1)S(1)}) fusion(bf16[16,264,768]{2,1,0:T(8,128)(2,1)} %bitcast.198), kind=kLoop, calls=%fused_computation.179 | loop fusion | bytes 9437184 | tf_op jit(solution)/shard_map/slice | solution.py:195
  109.2 1.8 multiply_reduce_fusion.3
  116.4 2.0 dynamic-slice_bitcast_fusion
  118.4 1.5 copy-done.3
  121.5 2.5 fusion.11
  124.0 1.9 copy.125
  125.9 1.8 reshape.537
  127.8 1.8 copy.126
  129.6 4.3 %all-to-all-start.2 = ((bf16[8,128,192]{1,2,0:T(8,128)(2,1)}), bf16[8,128,192]{1,2,0:T(8,128)(2,1)}, u32[]{:S(2)}, u32[]{:S(2)}) async-start(bf16[8,128,192]{1,2,0:T(8,128)(2,1)} %bitcast.219), calls=%async_computation.2 | async-start | bytes 786432 | tf_op jit(solution)/shard_map/all_to_all | solution.py:255
  134.8 1.6 slice.190
  137.7 5.1 %all-to-all-done.2 = bf16[8,128,192]{1,2,0:T(8,128)(2,1)} async-done(((bf16[8,128,192]{1,2,0:T(8,128)(2,1)}), bf16[8,128,192]{1,2,0:T(8,128)(2,1)}, u32[]{:S(2)}, u32[]{:S(2)}) %all-to-all-start.2) | async-done | bytes 393248 | tf_op jit(solution)/shard_map/all_to_all | solution.py:255
  142.8 2.0 copy.127
  144.8 1.9 reshape.539
  146.7 3.6 %fusion.4 = bf16[8,256,768]{2,1,0:T(8,128)(2,1)S(1)} fusion(bf16[8,256,768]{2,1,0:T(8,128)(2,1)} %collective-permute-done.5, bf16[8,2,256,768]{3,2,1,0:T(8,128)(2,1)} %copy-done.3, s32[]{:T(128)S(6)} %select_n.153), kind=kLoop, calls=%fused_computation.10 | loop fusion | flops 6291456 | bytes 9437188 | tf_op jit(solution)/shard_map/convert_element_type | solution.py:57
  150.3 1.8 copy.154
  152.2 7.5 %multiply_reduce_fusion = (f32[3,1024]{1,0:T(4,128)S(1)}, f32[3,1024,1024]{1,2,0:T(8,128)S(1)}) fusion(f32[3,1024,1024]{1,2,0:T(8,128)} %copy-done, f32[3,1024]{1,0:T(4,128)S(1)} %log_add_fusion, bf16[1024,3,64]{0,2,1:T(8,128)(2,1)} %reshape.539, f32[1024,3,3,64]{0,3,2,1:T(8,128)} %copy-done.4), kind=kOutput, calls=%fused_computation.1 | convolution fusion | flops 412087296 | bytes 25976832 | tf_op jit(solution)/shard_map/qhd,khd->hqk/dot_general | solution.py:116
  159.7 6.8 %multiply_convert_fusion = bf16[3,1024,1024]{1,2,0:T(8,128)(2,1)S(1)} fusion(f32[3,1024,1024]{1,2,0:T(8,128)S(1)} %get-tuple-element.68, f32[3,1024,1024]{1,2,0:T(8,128)} %copy-done, f32[3,1024]{1,0:T(4,128)S(1)} %get-tuple-element.67, f32[3,1024]{1,0:T(4,128)S(1)} %log_add_fusion), kind=kLoop, calls=%fused_computation | loop fusion | flops 12582912 | bytes 31481856 | tf_op jit(solution)/shard_map/convert_element_type | solution.py:57
  166.6 2.0 broadcast_multiply_fusion
  171.9 2.0 fusion.12
  174.0 3.3 %multiply_reduce_fusion.1 = (bf16[768]{0:T(1024)(128)(2,1)S(1)}, bf16[1024,768]{1,0:T(8,128)(2,1)}, bf16[1024,768]{1,0:T(8,128)(2,1)}) fusion(bf16[8,128,768]{2,1,0:T(8,128)(2,1)S(1)} %all-to-all-done, f32[1024]{0:T(1024)S(1)} %copy-done.41, f32[1024]{0:T(1024)S(1)} %copy-done.40, f32[768]{0:T(1024)S(1)} %copy-done.34, bf16[768,640]{1,0:T(8,128)(2,1)S(1)} %bitcast.202, ...), kind=kOutput, calls=%fused_computation.21 | convolution fusion | flops 915799296 | bytes 6894080 | tf_op jit(solution)/shard_map/rf,df->rd/dot_general | solution.py:270
  177.3 4.7 %all-to-all-start.3 = ((bf16[8,128,768]{2,1,0:T(8,128)(2,1)}), bf16[8,128,768]{2,1,0:T(8,128)(2,1)}, u32[]{:S(2)}, u32[]{:S(2)}) async-start(bf16[8,128,768]{2,1,0:T(8,128)(2,1)} %bitcast.216), calls=%async_computation.3 | async-start | bytes 3145728 | tf_op jit(solution)/shard_map/all_to_all | solution.py:285
  182.0 2.5 convolution_convert_fusion.3
  186.1 2.1 concatenate.101
  189.4 1.5 collective-permute-done.4
  191.9 13.8 %reduce-scatter.2.cloned.1.call-done = bf16[1,8,32,768]{3,2,1,0:T(8,128)(2,1)} async-done(((bf16[8,8,32,768]{3,2,1,0:T(8,128)(2,1)}), bf16[1,8,32,768]{3,2,1,0:T(8,128)(2,1)}) %reduce-scatter.2.cloned.1.call-update) | async-done | bytes 393232 | tf_op jit(solution)/shard_map/reduce_scatter | solution.py:252
  205.8 2.0 pad_maximum_fusion.5
  207.8 2.9 %all-to-all-done.3 = bf16[8,128,768]{2,1,0:T(8,128)(2,1)} async-done(((bf16[8,128,768]{2,1,0:T(8,128)(2,1)}), bf16[8,128,768]{2,1,0:T(8,128)(2,1)}, u32[]{:S(2)}, u32[]{:S(2)}) %all-to-all-start.3) | async-done | bytes 1572896 | tf_op jit(solution)/shard_map/all_to_all | solution.py:285
  210.6 5.8 %all-to-all-start.4 = ((bf16[8,80,768]{2,1,0:T(8,128)(2,1)}), bf16[8,80,768]{2,1,0:T(8,128)(2,1)}, u32[]{:S(2)}, u32[]{:S(2)}) async-start(bf16[8,80,768]{2,1,0:T(8,128)(2,1)} %pad_maximum_fusion.5), calls=%async_computation.5 | async-start | bytes 1966080 | tf_op jit(solution)/shard_map/all_to_all | solution.py:295
  216.7 2.9 %fusion.10 = bf16[256,768]{1,0:T(8,128)(2,1)} fusion(f32[256,768]{1,0:T(8,128)S(1)} %get-tuple-element.65, bf16[256,1152]{1,0:T(8,128)(2,1)S(1)} %copy-done.20, bf16[1152,768]{1,0:T(8,128)(2,1)} %bitcast.194), kind=kOutput, calls=%fused_computation.39 | convolution fusion | flops 453378048 | bytes 3538944 | tf_op jit(solution)/shard_map/dot_general | solution.py:211
  219.6 1.7 convert_reduce_fusion
  221.3 10.1 %all-to-all-done.4 = bf16[8,80,768]{2,1,0:T(8,128)(2,1)} async-done(((bf16[8,80,768]{2,1,0:T(8,128)(2,1)}), bf16[8,80,768]{2,1,0:T(8,128)(2,1)}, u32[]{:S(2)}, u32[]{:S(2)}) %all-to-all-start.4) | async-done | bytes 983072 | tf_op jit(solution)/shard_map/all_to_all | solution.py:295
  233.8 3.6 %all-to-all-start.5 = ((bf16[8,80,768]{2,1,0:T(8,128)(2,1)}), bf16[8,80,768]{2,1,0:T(8,128)(2,1)S(1)}, u32[]{:S(2)}, u32[]{:S(2)}) async-start(bf16[8,80,768]{2,1,0:T(8,128)(2,1)} %broadcast_in_dim.96), calls=%async_computation.6 | async-start | bytes 1966080 | tf_op jit(solution)/shard_map/all_to_all | solution.py:21
  238.9 13.1 %all-to-all-done.5 = bf16[8,80,768]{2,1,0:T(8,128)(2,1)S(1)} async-done(((bf16[8,80,768]{2,1,0:T(8,128)(2,1)}), bf16[8,80,768]{2,1,0:T(8,128)(2,1)S(1)}, u32[]{:S(2)}, u32[]{:S(2)}) %all-to-all-start.5) | async-done | bytes 983072 | tf_op jit(solution)/shard_map/all_to_all | solution.py:21
  (204 shorter events, 55.9 us)
Async XLA Ops:
  7.2 13.4 %copy-start.1 = (bf16[2,128,768]{2,1,0:T(8,128)(2,1)S(1)}, bf16[2,128,768]{2,1,0:T(8,128)(2,1)}, u32[]{:S(2)}) copy-start(bf16[2,128,768]{2,1,0:T(8,128)(2,1)} %param.10) | copy-start | bytes 1179652
  7.2 94.1 %all-gather.3.cloned.1.call-start = ((), (), s32[]{:S(2)}) async-start(), calls=%async_computation.8 | async-start | bytes 6893568 | tf_op jit(solution)/shard_map/all_gather | solution.py:173
  16.0 5.9 %copy-start.37 = (bf16[640]{0:T(1024)(128)(2,1)}, bf16[640]{0:T(1024)(128)(2,1)S(1)}, u32[]{:S(2)}) copy-start(bf16[640]{0:T(1024)(128)(2,1)S(1)} %pad.56.clone) | copy-start | bytes 3844
  16.1 13.3 %copy-start.42 = (s32[8]{0:T(128)S(1)}, s32[8]{0:T(128)}, u32[]{:S(2)}) copy-start(s32[8]{0:T(128)} %param.12) | copy-start | bytes 100
  16.1 10.3 %collective-permute-start = (bf16[1,48,640]{2,1,0:T(8,128)(2,1)S(1)}, bf16[1,48,640]{2,1,0:T(8,128)(2,1)S(1)}, u32[]{:S(2)}, u32[]{:S(2)}) collective-permute-start(bf16[1,48,640]{2,1,0:T(8,128)(2,1)S(1)} %get-tuple-element.51), channel_id=1, source_target_pairs={{0,8},{1,9},{2,10},{3,11},{4,12},{5,13},{6,14},{7,15},{8,0},{9,1},... | collective-permute-start | bytes 184328 | tf_op jit(solution)/shard_map/ppermute | solution.py:38
  21.9 30.4 %all-to-all-start = ((bf16[8,128,768]{2,1,0:T(8,128)(2,1)}), bf16[8,128,768]{2,1,0:T(8,128)(2,1)S(1)}, u32[]{:S(2)}, u32[]{:S(2)}) async-start(bf16[8,128,768]{2,1,0:T(8,128)(2,1)} %bitcast.3), calls=%async_computation | async-start | bytes 3145728 | tf_op jit(solution)/shard_map/all_to_all | solution.py:164
  26.3 18.7 %copy-start.43 = (s32[2]{0:T(128)S(1)}, s32[2]{0:T(128)}, u32[]{:S(2)}) copy-start(s32[2]{0:T(128)} %param.11) | copy-start | bytes 28
  26.4 8.8 %collective-permute-start.1 = (bf16[2,48,640]{2,1,0:T(8,128)(2,1)S(1)}, bf16[2,48,640]{2,1,0:T(8,128)(2,1)S(1)}, u32[]{:S(2)}, u32[]{:S(2)}) collective-permute-start(bf16[2,48,640]{2,1,0:T(8,128)(2,1)S(1)} %maximum_select_fusion.4), channel_id=1, source_target_pairs={{0,4},{1,5},{2,6},{3,7},{4,0},{5,1},{6,2},{7,3},{8,12},{9,13},{10,... | collective-permute-start | bytes 368648 | tf_op jit(solution)/shard_map/ppermute | solution.py:38
  35.3 6.7 %collective-permute-start.2 = (bf16[4,48,640]{2,1,0:T(8,128)(2,1)S(1)}, bf16[4,48,640]{2,1,0:T(8,128)(2,1)S(1)}, u32[]{:S(2)}, u32[]{:S(2)}) collective-permute-start(bf16[4,48,640]{2,1,0:T(8,128)(2,1)S(1)} %bitcast.230), channel_id=1, source_target_pairs={{0,2},{1,3},{2,0},{3,1},{4,6},{5,7},{6,4},{7,5},{8,10},{9,11},{10,... | collective-permute-start | bytes 737288 | tf_op jit(solution)/shard_map/ppermute | solution.py:38
  42.1 5.0 %collective-permute-start.3 = (bf16[8,48,640]{2,1,0:T(8,128)(2,1)S(1)}, bf16[8,48,640]{2,1,0:T(8,128)(2,1)}, u32[]{:S(2)}, u32[]{:S(2)}) collective-permute-start(bf16[8,48,640]{2,1,0:T(8,128)(2,1)S(1)} %bitcast.212), channel_id=1, source_target_pairs={{0,1},{1,0},{2,3},{3,2},{4,5},{5,4},{6,7},{7,6},{8,9},{9,8},{10,11... | collective-permute-start | bytes 1474568 | tf_op jit(solution)/shard_map/ppermute | solution.py:38
  45.7 10.7 %copy-start.17 = (f32[1024,64]{0,1:T(8,128)}, f32[1024,64]{0,1:T(8,128)S(1)}, u32[]{:S(2)}) copy-start(f32[1024,64]{0,1:T(8,128)S(1)} %pad_maximum_fusion.12) | copy-start | bytes 786436
  48.6 4.0 %copy-start.7 = (bf16[8,2,48,640]{3,2,1,0:T(8,128)(2,1)}, bf16[8,2,48,640]{3,2,1,0:T(8,128)(2,1)S(1)}, u32[]{:S(2)}) copy-start(bf16[8,2,48,640]{3,2,1,0:T(8,128)(2,1)S(1)} %copy.119) | copy-start | bytes 2949124
  52.3 2.6 copy-start.33
  56.1 4.9 %copy-start.4 = (f32[1024,3,3,64]{0,3,2,1:T(8,128)}, f32[1024,3,3,64]{0,3,2,1:T(8,128)S(1)}, u32[]{:S(2)}) copy-start(f32[1024,3,3,64]{0,3,2,1:T(8,128)S(1)} %fusion.72) | copy-start | bytes 7077892
  56.8 2.4 copy-start.10
  56.8 2.4 copy-start.12
  59.1 4.6 %copy-start = (f32[3,1024,1024]{1,2,0:T(8,128)}, f32[3,1024,1024]{1,2,0:T(8,128)S(1)}, u32[]{:S(2)}) copy-start(f32[3,1024,1024]{1,2,0:T(8,128)S(1)} %get-tuple-element.63) | copy-start | bytes 37748740
  59.2 4.7 %copy-start.32 = (f32[3,1024]{1,0:T(4,128)}, f32[3,1024]{1,0:T(4,128)S(1)}, u32[]{:S(2)}) copy-start(f32[3,1024]{1,0:T(4,128)S(1)} %get-tuple-element.62) | copy-start | bytes 36868
  63.9 2.3 copy-start.36
  67.1 14.1 %all-to-all-start.1 = ((bf16[8,128,192]{1,2,0:T(8,128)(2,1)}), bf16[8,128,192]{1,2,0:T(8,128)(2,1)S(1)}, u32[]{:S(2)}, u32[]{:S(2)}) async-start(bf16[8,128,192]{1,2,0:T(8,128)(2,1)} %copy.122), calls=%async_computation.1 | async-start | bytes 786432 | tf_op jit(solution)/shard_map/all_to_all | solution.py:189
  81.6 24.5 %copy-start.15 = (bf16[2,128,4,192]{1,0,3,2:T(2,128)(2,1)}, bf16[2,128,4,192]{1,0,3,2:T(2,128)(2,1)S(1)}, u32[]{:S(2)}) copy-start(bf16[2,128,4,192]{1,0,3,2:T(2,128)(2,1)S(1)} %copy.123) | copy-start | bytes 1179652
  102.8 5.3 %copy-start.5 = (bf16[16,72,768]{2,1,0:T(8,128)(2,1)}, bf16[16,72,768]{2,1,0:T(8,128)(2,1)S(1)}, u32[]{:S(2)}) copy-start(bf16[16,72,768]{2,1,0:T(8,128)(2,1)S(1)} %slice.185) | copy-start | bytes 5308420
  109.2 4.8 %copy-start.19 = (bf16[256,1152]{1,0:T(8,128)(2,1)}, bf16[256,1152]{1,0:T(8,128)(2,1)S(1)}, u32[]{:S(2)}) copy-start(bf16[256,1152]{1,0:T(8,128)(2,1)S(1)} %get-tuple-element.30) | copy-start | bytes 1769476
  116.4 3.5 %copy-start.3 = (bf16[8,2,256,768]{3,2,1,0:T(8,128)(2,1)}, bf16[8,2,256,768]{3,2,1,0:T(8,128)(2,1)S(1)}, u32[]{:S(2)}) copy-start(bf16[8,2,256,768]{3,2,1,0:T(8,128)(2,1)S(1)} %constant_dynamic-update-slice_fusion.2) | copy-start | bytes 18874372
  119.9 26.8 %collective-permute-start.5 = (bf16[8,256,768]{2,1,0:T(8,128)(2,1)}, bf16[8,256,768]{2,1,0:T(8,128)(2,1)}, u32[]{:S(2)}, u32[]{:S(2)}) collective-permute-start(bf16[8,256,768]{2,1,0:T(8,128)(2,1)} %dynamic-slice_bitcast_fusion), channel_id=1, source_target_pairs={{0,1},{1,0},{2,3},{3,2},{4,5},{5,4},{6,7},{7,6},{8,9},{9,8},{10,11... | collective-permute-start | bytes 9437192 | tf_op jit(solution)/shard_map/ppermute | solution.py:52
  129.6 13.2 %all-to-all-start.2 = ((bf16[8,128,192]{1,2,0:T(8,128)(2,1)}), bf16[8,128,192]{1,2,0:T(8,128)(2,1)}, u32[]{:S(2)}, u32[]{:S(2)}) async-start(bf16[8,128,192]{1,2,0:T(8,128)(2,1)} %bitcast.219), calls=%async_computation.2 | async-start | bytes 786432 | tf_op jit(solution)/shard_map/all_to_all | solution.py:255
  133.8 71.9 %reduce-scatter.2.cloned.1.call-start = ((), (), s32[]{:S(2)}) async-start(), calls=%async_computation.7 | async-start | bytes 3538944 | tf_op jit(solution)/shard_map/reduce_scatter | solution.py:252
  159.7 6.8 %copy-start.13 = (bf16[1024,3,64]{0,2,1:T(8,128)(2,1)S(1)}, bf16[1024,3,64]{0,2,1:T(8,128)(2,1)}, u32[]{:S(2)}) copy-start(bf16[1024,3,64]{0,2,1:T(8,128)(2,1)} %copy-done.12) | copy-start | bytes 1179652
  166.5 2.2 copy-start.11
  166.6 4.2 %slice-start = ((s8[12582912]{0:T(1024)(128)(4,1)}), s8[4194304]{0:T(1024)(128)(4,1)S(1)}, s32[]{:S(2)}) async-start(s8[12582912]{0:T(1024)(128)(4,1)} %bitcast.186), calls=%async_computation.9 | async-start | bytes 8388608
  166.6 4.2 %slice-start.1 = ((s8[12582912]{0:T(1024)(128)(4,1)}), s8[4194304]{0:T(1024)(128)(4,1)S(1)}, s32[]{:S(2)}) async-start(s8[12582912]{0:T(1024)(128)(4,1)} %bitcast.186), calls=%async_computation.10 | async-start | bytes 8388608
  168.7 3.1 %slice-start.2 = ((s8[12582912]{0:T(1024)(128)(4,1)}), s8[4194304]{0:T(1024)(128)(4,1)S(1)}, s32[]{:S(2)}) async-start(s8[12582912]{0:T(1024)(128)(4,1)} %bitcast.186), calls=%async_computation.11 | async-start | bytes 8388608
  171.8 2.1 copy-start.34
  171.9 2.1 copy-start.40
  171.9 2.1 copy-start.41
  173.9 3.3 %copy-start.26 = (bf16[3,64,1024]{2,1,0:T(8,128)(2,1)}, bf16[3,64,1024]{2,1,0:T(8,128)(2,1)S(1)}, u32[]{:S(2)}) copy-start(bf16[3,64,1024]{2,1,0:T(8,128)(2,1)S(1)} %fusion.12) | copy-start | bytes 1179652
  177.3 4.7 %copy-start.29 = (bf16[1024,3,64]{0,2,1:T(8,128)(2,1)S(1)}, bf16[1024,3,64]{0,2,1:T(8,128)(2,1)}, u32[]{:S(2)}) copy-start(bf16[1024,3,64]{0,2,1:T(8,128)(2,1)} %copy-done.28) | copy-start | bytes 1179652
  177.3 4.7 %copy-start.31 = (bf16[1024,3,64]{0,2,1:T(8,128)(2,1)S(1)}, bf16[1024,3,64]{0,2,1:T(8,128)(2,1)}, u32[]{:S(2)}) copy-start(bf16[1024,3,64]{0,2,1:T(8,128)(2,1)} %copy-done.30) | copy-start | bytes 1179652
  177.3 4.7 %copy-start.27 = (bf16[3,64,1024]{2,1,0:T(8,128)(2,1)S(1)}, bf16[3,64,1024]{2,1,0:T(8,128)(2,1)}, u32[]{:S(2)}) copy-start(bf16[3,64,1024]{2,1,0:T(8,128)(2,1)} %copy-done.26) | copy-start | bytes 1179652
  177.3 33.4 %all-to-all-start.3 = ((bf16[8,128,768]{2,1,0:T(8,128)(2,1)}), bf16[8,128,768]{2,1,0:T(8,128)(2,1)}, u32[]{:S(2)}, u32[]{:S(2)}) async-start(bf16[8,128,768]{2,1,0:T(8,128)(2,1)} %bitcast.216), calls=%async_computation.3 | async-start | bytes 3145728 | tf_op jit(solution)/shard_map/all_to_all | solution.py:285
  182.0 2.5 copy-start.38
  182.0 2.5 copy-start.39
  184.8 3.5 %copy-start.21 = (bf16[16,8,768]{2,1,0:T(8,128)(2,1)S(1)}, bf16[16,8,768]{2,1,0:T(8,128)(2,1)}, u32[]{:S(2)}) copy-start(bf16[16,8,768]{2,1,0:T(8,128)(2,1)} %slice.190) | copy-start | bytes 589828
  188.4 2.5 collective-permute-start.4
  191.9 24.8 %copy-start.20 = (bf16[256,1152]{1,0:T(8,128)(2,1)S(1)}, bf16[256,1152]{1,0:T(8,128)(2,1)}, u32[]{:S(2)}) copy-start(bf16[256,1152]{1,0:T(8,128)(2,1)} %copy-done.19) | copy-start | bytes 1769476
  210.6 20.8 %all-to-all-start.4 = ((bf16[8,80,768]{2,1,0:T(8,128)(2,1)}), bf16[8,80,768]{2,1,0:T(8,128)(2,1)}, u32[]{:S(2)}, u32[]{:S(2)}) async-start(bf16[8,80,768]{2,1,0:T(8,128)(2,1)} %pad_maximum_fusion.5), calls=%async_computation.5 | async-start | bytes 1966080 | tf_op jit(solution)/shard_map/all_to_all | solution.py:295
  221.3 16.0 %copy-start.35 = (f32[768]{0:T(1024)S(1)}, f32[768]{0:T(1024)}, u32[]{:S(2)}) copy-start(f32[768]{0:T(1024)} %copy-done.33) | copy-start | bytes 9220
  233.8 18.2 %all-to-all-start.5 = ((bf16[8,80,768]{2,1,0:T(8,128)(2,1)}), bf16[8,80,768]{2,1,0:T(8,128)(2,1)S(1)}, u32[]{:S(2)}, u32[]{:S(2)}) async-start(bf16[8,80,768]{2,1,0:T(8,128)(2,1)} %broadcast_in_dim.96), calls=%async_computation.6 | async-start | bytes 1966080 | tf_op jit(solution)/shard_map/all_to_all | solution.py:21
  (13 other events, 20.0 us)
Sparse Core Ops, SparseCore 0:
  12.6 88.5 all-gather.2
  152.3 53.4 reduce-scatter.1

commit v2 on v1

v2 whole, which is shorter than its diff:
```python
import math

import jax
import jax.numpy as jnp
from jax import lax
from jax.experimental import pallas as pl
from jax.experimental.pallas import tpu as pltpu
from jax.sharding import PartitionSpec as P

HEADS = 12
HD = 64
BLK = 128


EPS = 1e-05
THETA = 160000.0
NEGATIVE = -1e30
INV_ROOT_TWO = 0.7071067811865476
INV_ROOT_TWO_PI = 0.3989422804014327


def gather_by_exchange(part, axis, n):
    return lax.all_to_all(jnp.broadcast_to(part[None], (n, *part.shape)), axis, 0, 0)


def core_pairs(n):
    return [(k, k ^ 1) for k in range(n)]


def core_groups(n):
    return [list(range(first, n, 2)) for first in range(2)]


def gather_doubling(part, axis):
    n = lax.axis_size(axis)
    index = lax.axis_index(axis)
    held = part[None]
    bit = n // 2
    while bit:
        came = lax.ppermute(held, axis, [(k, k ^ bit) for k in range(n)])
        first = (index & bit) == 0
        held = jnp.where(first, jnp.stack([held, came], 1), jnp.stack([came, held], 1))
        held = held.reshape(-1, *part.shape)
        bit //= 2
    return held


def gather_two_level(part, axis):
    n = lax.axis_size(axis)
    mine = lax.all_to_all(
        jnp.broadcast_to(part[None], (n // 2, *part.shape)),
        axis,
        0,
        0,
        axis_index_groups=core_groups(n),
    )
    other = lax.ppermute(mine, axis, core_pairs(n))
    even = lax.axis_index(axis) % 2 == 0
    return jnp.where(even, mine, other), jnp.where(even, other, mine)


def core_sum(parts, axis):
    n = lax.axis_size(axis)
    core = lax.axis_index(axis) % 2
    paired = parts.reshape(n // 2, 2, *parts.shape[1:])
    away = lax.dynamic_index_in_dim(paired, 1 - core, 1, keepdims=False)
    kept = lax.dynamic_index_in_dim(paired, core, 1, keepdims=False)
    came = lax.ppermute(away, axis, core_pairs(n))
    return low(kept.astype(jnp.float32) + came.astype(jnp.float32))


def spread_sum(parts, axis):
    groups = core_groups(lax.axis_size(axis))
    shares = lax.all_to_all(parts, axis, 0, 0, tiled=True, axis_index_groups=groups)
    return low(jnp.sum(shares.astype(jnp.float32), 0))


def low(values):
    return values.astype(jnp.bfloat16)


def tables(positions):
    halves = jnp.arange(HD // 2, dtype=jnp.float32)
    frequency = THETA ** (-2.0 * halves / HD)
    angles = frequency[:, None] * positions.astype(jnp.float32)[None, :]
    return jnp.cos(angles), jnp.sin(angles)


def norm_forward(rows_in, gain):
    centre = rows_in - jnp.mean(rows_in, -1, keepdims=True)
    variance = jnp.mean(centre * centre, -1, keepdims=True)
    inverse = lax.rsqrt(variance + EPS)
    normed = centre * inverse
    return (normed * gain.astype(jnp.float32), normed, inverse)


def norm_backward(grad_rows, gain, normed, inverse):
    scaled = grad_rows * gain.astype(jnp.float32)
    grad_gain = jnp.sum(grad_rows * normed, 0)
    grad_rows_in = inverse * (
        scaled
        - jnp.mean(scaled, -1, keepdims=True)
        - normed * jnp.mean(scaled * normed, -1, keepdims=True)
    )
    return (grad_rows_in, grad_gain)


NN = (((1,), (0,)), ((), ()))
NT = (((1,), (1,)), ((), ()))
ROWS = 256
COLS = 256


def product(left, right, dims=NN):
    return lax.dot_general(left, right, dims, preferred_element_type=jnp.float32)


def forward_kernel(
    seq_ref, w_ref, cos_ref, sin_ref, bias_ref, keep_ref, out_ref, a_ref, qkv_ref, lse_ref, o_ref
):
    full_len, width = seq_ref.shape
    span = o_ref.shape[0]
    group = span // HD
    half = HD // 2
    blk = out_ref.shape[2]
    gain = w_ref[:, 512:640].astype(jnp.float32).T[3 * span - 512 : 3 * span - 511]
    w_turned = w_ref[:, : 3 * span].astype(jnp.float32).T.astype(jnp.bfloat16)
    for start in range(0, full_len, ROWS):
        rows = slice(start, start + ROWS)
        x = seq_ref[rows].astype(jnp.float32)
        centre = x - jnp.mean(x, -1, keepdims=True)
        variance = jnp.mean(centre * centre, -1, keepdims=True)
        a_low = (centre * lax.rsqrt(variance + EPS) * gain).astype(jnp.bfloat16)
        a_ref[rows] = a_low
        joined = product(w_turned, a_low, NT)
        cosine = cos_ref[:, rows]
        sine = sin_ref[:, rows]
        for part in range(2 * group):
            one = joined[part * HD : part * HD + half]
            two = joined[part * HD + half : (part + 1) * HD]
            scale = HD ** (-0.5) if part < group else 1.0
            for at, value in (
                (0, one * cosine - two * sine),
                (half, two * cosine + one * sine),
            ):
                qkv_ref[part * HD + at : part * HD + at + half, rows] = (
                    value.astype(jnp.bfloat16) * scale
                ).astype(jnp.bfloat16)
        qkv_ref[2 * span :, rows] = joined[2 * span :].astype(jnp.bfloat16)
    for head in range(group):
        here = slice(head * HD, (head + 1) * HD)
        keys = qkv_ref[span + head * HD : span + (head + 1) * HD].T
        values = qkv_ref[2 * span + head * HD : 2 * span + (head + 1) * HD]
        for start in range(0, full_len, COLS):
            cols = slice(start, start + COLS)
            scores = product(keys, qkv_ref[here, cols]) + bias_ref[...]
            maximum = jnp.max(scores, 0, keepdims=True)
            exponent = jnp.exp(scores - maximum)
            total = jnp.sum(exponent, 0, keepdims=True)
            attended = product(values, exponent.astype(jnp.bfloat16))
            attended = attended * (keep_ref[:, cols] / total)
            o_ref[here, cols] = attended
            lse_ref[head : head + 1, cols] = maximum + jnp.log(total)
            for first in range(0, COLS, blk):
                out_ref[(start + first) // blk, here, :] = attended[
                    :, first : first + blk
                ].astype(jnp.bfloat16)


def backward_kernel(
    do_ref, qkv_ref, lse_ref, o_ref, cos_ref, sin_ref, bias_ref, keep_ref, g_ref, dk_ref, dv_ref
):
    span, full_len = o_ref.shape
    group = span // HD
    half = HD // 2
    blk = do_ref.shape[2]
    for head in range(group):
        here = slice(head * HD, (head + 1) * HD)
        keys_turned = qkv_ref[span + head * HD : span + (head + 1) * HD]
        keys = keys_turned.T
        values = qkv_ref[2 * span + head * HD : 2 * span + (head + 1) * HD].T
        for start in range(0, full_len, COLS):
            cols = slice(start, start + COLS)
            query = qkv_ref[here, cols]
            grad_out = jnp.concatenate(
                [do_ref[(start + first) // blk, here, :] for first in range(0, COLS, blk)], 1
            )
            grad_out = grad_out.astype(jnp.float32) * keep_ref[:, cols]
            delta = jnp.sum(grad_out * o_ref[here, cols], 0, keepdims=True)
            grad_out = grad_out.astype(jnp.bfloat16)
            scores = product(keys, query) + bias_ref[...]
            probs = jnp.exp(scores - lse_ref[head : head + 1, cols])
            grad_scores = (probs * (product(values, grad_out) - delta)).astype(jnp.bfloat16)
            grad_value = product(grad_out, probs.astype(jnp.bfloat16), NT)
            grad_key = product(query, grad_scores, NT)
            if start == 0:
                dv_ref[...] = grad_value
                dk_ref[...] = grad_key
            else:
                dv_ref[...] += grad_value
                dk_ref[...] += grad_key
            grad_query = product(keys_turned, grad_scores) * HD ** (-0.5)
            cosine = cos_ref[:, cols]
            sine = sin_ref[:, cols]
            one, two = grad_query[:half], grad_query[half:]
            g_ref[head * HD : head * HD + half, cols] = (one * cosine + two * sine).astype(
                jnp.bfloat16
            )
            g_ref[head * HD + half : (head + 1) * HD, cols] = (
                two * cosine - one * sine
            ).astype(jnp.bfloat16)
        one, two = dk_ref[:half], dk_ref[half:]
        cosine = cos_ref[...]
        sine = sin_ref[...]
        low_at = span + head * HD
        g_ref[low_at : low_at + half] = (one * cosine + two * sine).astype(jnp.bfloat16)
        g_ref[low_at + half : low_at + HD] = (two * cosine - one * sine).astype(jnp.bfloat16)
        g_ref[2 * span + head * HD : 2 * span + (head + 1) * HD] = dv_ref[...].astype(
            jnp.bfloat16
        )


def on_device(kernel, outs, args, scratch=(), name=None):
    space = pl.BlockSpec(memory_space=pltpu.VMEM)
    return pl.pallas_call(
        kernel,
        out_shape=[jax.ShapeDtypeStruct(shape, dtype) for shape, dtype in outs],
        in_specs=[space] * len(args),
        out_specs=[space] * len(outs),
        scratch_shapes=list(scratch),
        compiler_params=pltpu.CompilerParams(vmem_limit_bytes=48 * 1024 * 1024),
        name=name,
    )(*args)


def body(tokens, lengths, deal, gain_attn, w_qkv, w_out, gain_mlp, w_in, w_down, cotangent):
    seqs, local_len, width = tokens.shape
    ctx = lax.axis_size("ctx")
    fsdp = lax.axis_size("fsdp")
    spread = ctx // seqs
    group = HEADS // spread
    span = group * HD
    full_len = local_len * ctx
    rows = seqs * local_len
    context = lax.axis_index("ctx")
    own_seq = context // spread
    own_group = context % spread
    depth = w_qkv.shape[0]
    hidden = w_in.shape[1] // 2
    down_rows = w_down.shape[0]
    f32 = jnp.float32

    offsets = jnp.arange(BLK, dtype=jnp.int32)
    all_pos = (deal[:, None] * BLK + offsets[None, :]).reshape(full_len)
    length = lax.dynamic_slice_in_dim(lengths, own_seq, 1)[0]
    all_keep = all_pos < length

    qkv_own = lax.dynamic_index_in_dim(
        w_qkv.reshape(depth, 3, spread, span), own_group, 2, keepdims=False
    ).reshape(depth, 3 * span)
    gains_wide = jnp.stack([gain_attn, gain_mlp], 1)
    fill = jnp.zeros((depth, 640 - 3 * span - 2), jnp.bfloat16)
    first_all = gather_doubling(
        jnp.concatenate([qkv_own, gains_wide, fill], 1), "fsdp"
    ).reshape(fsdp * depth, 640)
    sequence = lax.all_to_all(jnp.repeat(tokens, spread, axis=0), "ctx", 0, 0, tiled=True)

    wqkv_part = first_all[:, : 3 * span]
    gain_one = first_all[:, 3 * span]
    gain_two = first_all[:, 3 * span + 1]

    win_all = lax.all_gather(w_in, "fsdp", axis=0, tiled=True)
    stacked, sequence = lax.optimization_barrier(
        (jnp.concatenate([w_out, w_down], 0), sequence)
    )
    stacked_all = gather_two_level(stacked, "fsdp")

    cosine, sine = tables(all_pos)
    bias = jnp.where(all_keep, 0.0, NEGATIVE).astype(f32)[:, None]
    keep_row = all_keep.astype(f32)[None, :]
    sequence = sequence.reshape(full_len, width)
    attended, a_low, qkv, log_total, unrounded = on_device(
        forward_kernel,
        [
            ((ctx, span, local_len), jnp.bfloat16),
            ((full_len, width), jnp.bfloat16),
            ((3 * span, full_len), jnp.bfloat16),
            ((8, full_len), f32),
            ((span, full_len), f32),
        ],
        (sequence, first_all, cosine, sine, bias, keep_row),
        name="attention_forward",
    )
    att_back = lax.all_to_all(attended, "ctx", 0, 0, tiled=True)
    att_turned = att_back.reshape(seqs, width, local_len)

    def whole(start, height):
        halves = [part[:, start : start + height] for part in stacked_all]
        return jnp.stack(halves, 1).reshape(fsdp * height, width)

    wout_all = whole(0, depth)
    wdown_all = whole(depth, down_rows)

    resid = tokens.astype(f32).reshape(rows, width)
    mixed = resid + jnp.einsum(
        "sdr,de->sre", att_turned, wout_all, preferred_element_type=f32
    ).reshape(rows, width)
    normed_mid, normed_two, inverse_two = norm_forward(mixed, gain_two)
    b_low = low(normed_mid)
    gate_up = jnp.dot(b_low, win_all, preferred_element_type=f32)
    gate_in = gate_up[:, :hidden]
    up_half = gate_up[:, hidden:]
    normal_cdf = 0.5 * (1.0 + lax.erf(gate_in * INV_ROOT_TWO))
    gelu_out = gate_in * normal_cdf
    hid_low = low(gelu_out * up_half)
    output = mixed + jnp.dot(hid_low, wdown_all, preferred_element_type=f32)

    grad_low = cotangent.reshape(rows, width)
    grad_out = grad_low.astype(f32)
    grad_hid = jnp.einsum("rd,fd->rf", grad_low, wdown_all, preferred_element_type=f32)
    normal_pdf = jnp.exp(-0.5 * gate_in * gate_in) * INV_ROOT_TWO_PI
    grad_gate = grad_hid * up_half * (normal_cdf + gate_in * normal_pdf)
    grad_up = grad_hid * gelu_out
    grad_gate_up = low(jnp.concatenate([grad_gate, grad_up], 1))
    grad_b = jnp.einsum("rf,df->rd", grad_gate_up, win_all, preferred_element_type=f32)
    grad_norm_two, grad_gain_two = norm_backward(grad_b, gain_two, normed_two, inverse_two)
    grad_mixed = grad_out + grad_norm_two
    grad_att = low(grad_mixed)
    grad_att = grad_att.reshape(seqs, local_len, width)
    grad_heads = low(
        jnp.einsum("de,sre->sdr", wout_all, grad_att, preferred_element_type=f32)
    ).reshape(ctx, span, local_len)
    hid_low, b_low, grad_gate_up, grad_heads = lax.optimization_barrier(
        (hid_low, b_low, grad_gate_up, grad_heads)
    )
    grad_wout = jnp.einsum("sdr,sre->de", att_turned, grad_att, preferred_element_type=f32)
    grad_wdown = jnp.einsum("rf,rd->fd", hid_low, grad_low, preferred_element_type=f32)
    grad_win = low(jnp.einsum("rd,rf->df", b_low, grad_gate_up, preferred_element_type=f32))
    count = w_in.shape[1] // width
    main_rows = ((count + 1) * depth + down_rows) // (8 * ctx) * 8 * ctx
    chunk = main_rows // ctx
    grad_wdown = low(grad_wdown).reshape(fsdp, down_rows, width)
    split = main_rows - (count + 1) * depth
    grads_main = jnp.concatenate(
        [
            *[
                grad_win[:, k * width : (k + 1) * width].reshape(fsdp, depth, width)
                for k in range(count)
            ],
            low(grad_wout).reshape(fsdp, depth, width),
            grad_wdown[:, :split],
        ],
        1,
    )
    main_pair = core_sum(grads_main, "fsdp")
    main_pair = main_pair.reshape(fsdp // 2, ctx, chunk, width).transpose(1, 0, 2, 3)
    main_part = lax.psum_scatter(main_pair, "ctx", scatter_dimension=0, tiled=True)
    main_part = main_part.reshape(fsdp // 2, chunk, width)

    all_grad = lax.all_to_all(grad_heads, "ctx", 0, 0, tiled=True)
    grad_qkv = on_device(
        backward_kernel,
        [((3 * span, full_len), jnp.bfloat16)],
        (all_grad, qkv, log_total, unrounded, cosine, sine, bias, keep_row),
        [pltpu.VMEM((HD, full_len), f32)] * 2,
        name="attention_backward",
    )[0]
    grad_a_part = jnp.einsum("fr,df->rd", grad_qkv, wqkv_part, preferred_element_type=f32)
    grad_wqkv = low(jnp.einsum("rd,fr->df", a_low, grad_qkv, preferred_element_type=f32))
    _, seq_normed, _ = norm_forward(sequence.astype(f32), gain_one)
    grad_gain_one = jnp.sum(grad_a_part * seq_normed, 0)
    last = jnp.concatenate(
        [
            grad_wqkv,
            jnp.stack([low(grad_gain_one), low(grad_gain_two)], 1),
            jnp.zeros((fsdp * depth, 640 - 3 * span - 2), jnp.bfloat16),
        ],
        1,
    )
    last = jnp.concatenate(
        [last.reshape(fsdp, -1, width), grad_wdown[:, split:]], 1
    )
    last = core_sum(last, "fsdp")
    last_rows = last.shape[1]
    grad_a_parts = lax.all_to_all(
        low(grad_a_part).reshape(ctx, local_len, width), "ctx", 0, 0, tiled=True
    )
    grad_a = jnp.sum(
        grad_a_parts.reshape(seqs, spread, local_len, width).astype(f32), 1
    ).reshape(rows, width)
    _, normed_one, inverse_one = norm_forward(resid, gain_one)
    grad_norm_one, _ = norm_backward(grad_a, gain_one, normed_one, inverse_one)
    grad_input = grad_mixed + grad_norm_one

    last = spread_sum(last, "fsdp")
    main_part = spread_sum(main_part, "fsdp")
    share = jnp.concatenate([last, main_part], 0)
    ends = gather_by_exchange(share, "ctx", ctx)
    extra = down_rows - split
    last_all = ends[:, : last_rows - extra].reshape(ctx, depth, 640).astype(f32)
    down_end = jnp.sum(ends[:, last_rows - extra : last_rows].astype(f32), 0)
    summed = ends[:, last_rows:].reshape(main_rows, width).astype(f32)
    grad_wqkv_out = (
        jnp.sum(last_all[:, :, : 3 * span].reshape(seqs, spread, depth, 3, span), 0)
        .transpose(1, 2, 0, 3)
        .reshape(depth, 3 * width)
    )
    gains_out = jnp.sum(last_all[:, :, 3 * span : 3 * span + 2], 0)
    return (
        low(output.reshape(tokens.shape)),
        grad_input.reshape(tokens.shape),
        gains_out[:, 0],
        grad_wqkv_out,
        summed[count * depth : (count + 1) * depth],
        gains_out[:, 1],
        jnp.concatenate([summed[k * depth : (k + 1) * depth] for k in range(count)], 1),
        jnp.concatenate([summed[(count + 1) * depth :], down_end], 0),
    )


def solution(mesh):
    placed = (
        P("fsdp", "ctx", None),
        P("fsdp"),
        P(),
        P("fsdp"),
        P("fsdp", None),
        P("fsdp", None),
        P("fsdp"),
        P("fsdp", None),
        P("fsdp", None),
        P("fsdp", "ctx", None),
    )
    return jax.shard_map(
        body,
        mesh=mesh,
        in_specs=placed,
        out_specs=(
            P("fsdp", "ctx", None),
            P("fsdp", "ctx", None),
            P("fsdp"),
            P("fsdp", None),
            P("fsdp", None),
            P("fsdp"),
            P("fsdp", None),
            P("fsdp", None),
        ),
        check_vma=False,
    )
```

time: 275 us -> 339 us (1.23)
  blocking collectives: 0 us -> 38.4 us
  waiting for transfers between devices: 87.2 us -> 123 us
  local copies, waits for them, and re-layouts: 56 us -> 35.6 us
  Pallas kernels: 0 us -> 20.1 us
  matrix products: 36.7 us -> 17 us
  starting transfers between devices: 39.5 us -> 58.9 us
  other arithmetic: 34.9 us -> 26.4 us
    unnamed x2 -> x3, waiting for transfers between devices: 0.03 us -> 50.1 us
    all_to_all x0 -> x1, blocking collectives: none -> 38.4 us  [spread_sum(): lax.all_to_all(parts, axis, 0, 0, tiled=True, axis_index_groups=groups)]
    all_to_all x1, waiting for transfers between devices: 0.01 us -> 20.8 us  [body(): lax.all_to_all(jnp.repeat(tokens, spread, axis=0), 'ctx', 0, 0, tiled=True)]
    dot_general x12 -> x5, matrix products: 28 us -> 7.45 us  [the longest x1 2.9 us: body(): jnp.einsum('fr,df->rd', grad_qkv, wqkv_part, preferred_element_type=f32)]
    pallas_call x0 -> x2, Pallas kernels: none -> 20.1 us  [on_device(): pl.pallas_call(kernel, out_shape=[jax.ShapeDtypeStruct(shape, dtype) for...]
    all_gather x1, waiting for transfers between devices: 19.6 us -> 0.02 us  [body(): win_all = lax.all_gather(w_in, 'fsdp', axis=0, tiled=True)]
    reduce_scatter x1 -> x0, waiting for transfers between devices: 13.8 us -> none  [body(): lax.psum_scatter(main_pair, 'ctx', scatter_dimension=0, tiled=True)]
    ppermute x4, starting transfers between devices: 10.3 us -> 21.2 us  [gather_doubling(): came = lax.ppermute(held, axis, [(k, k ^ bit) for k in range(n)])]
  transfers between devices with their start and end apart: 14 -> 16, of which waited for: 10 -> 11; matrix products, arithmetic and copies ran while one was open for 30% -> 10% of each run, Pallas kernels for 0% -> 6%
where the time goes in v2:
time: 339 us; the launch traced here: 335 us
  waiting for transfers between devices  123 us (36%)
  starting transfers between devices  58.9 us (17%)
  blocking collectives  38.4 us (11%)
  local copies, waits for them, and re-layouts  35.6 us (11%)
  other arithmetic  26.4 us (8%)
  Pallas kernels  20.1 us (6%)
  matrix products  17 us (5%)
  between operations  15.2 us (4%)
    unnamed x3, waiting for transfers between devices  50.1 us
    all_to_all x1, blocking collectives, spread_sum(): lax.all_to_all(parts, axis, 0, 0, tiled=True, axis_index_groups=groups)  38.4 us
    ppermute x4, starting transfers between devices, gather_doubling(): came = lax.ppermute(held, axis, [(k, k ^ bit) for k in range(n)])  21.2 us
    all_to_all x1, waiting for transfers between devices, body(): lax.all_to_all(jnp.repeat(tokens, spread, axis=0), 'ctx', 0, 0, tiled=True)  20.8 us
    pallas_call x2, Pallas kernels, on_device(): pl.pallas_call(kernel, out_shape=[jax.ShapeDtypeStruct(shape, dtype) for...  20.1 us
    ppermute x4, waiting for transfers between devices, gather_doubling(): came = lax.ppermute(held, axis, [(k, k ^ bit) for k in range(n)])  17.7 us
    all_to_all x1, waiting for transfers between devices, gather_by_exchange(): lax.all_to_all(jnp.broadcast_to(part[None], (n, *part.shape)), axis, 0, 0)  13.6 us
    unnamed x95, local copies, waits for them, and re-layouts  12.6 us
  transfers between devices with their start and end apart: 16, of which 11 were waited for; matrix products, arithmetic and copies ran while one was open for 10% of the time, Pallas kernels for 6%

profile of v2, /device:TPU:1, one launch (start us, length us, event | category | flops | bytes accessed | tf_op | source)
XLA Modules:
  0.0 334.9 jit_solution(11704794449649033890)
XLA Ops:
  7.2 2.3 broadcast_in_dim.20
  9.4 6.3 %all-to-all-start = ((bf16[8,128,768]{2,1,0:T(8,128)(2,1)}), bf16[8,128,768]{2,1,0:T(8,128)(2,1)S(1)}, u32[]{:S(2)}, u32[]{:S(2)}) async-start(bf16[8,128,768]{2,1,0:T(8,128)(2,1)} %bitcast.1), calls=%async_computation | async-start | bytes 3145728 | tf_op jit(solution)/shard_map/all_to_all | solution.py:266
  16.5 20.8 %all-to-all-done = bf16[8,128,768]{2,1,0:T(8,128)(2,1)S(1)} async-done(((bf16[8,128,768]{2,1,0:T(8,128)(2,1)}), bf16[8,128,768]{2,1,0:T(8,128)(2,1)S(1)}, u32[]{:S(2)}, u32[]{:S(2)}) %all-to-all-start) | async-done | bytes 1572896 | tf_op jit(solution)/shard_map/all_to_all | solution.py:266
  37.3 1.3 broadcast_in_dim.25
  38.9 7.2 %all-to-all-start.2 = ((bf16[8,120,768]{2,1,0:T(8,128)(2,1)}), bf16[8,120,768]{2,1,0:T(8,128)(2,1)}, u32[]{:S(2)}, u32[]{:S(2)}) async-start(bf16[8,120,768]{2,1,0:T(8,128)(2,1)} %broadcast_in_dim.25), calls=%async_computation.2 | async-start | bytes 2949120 | tf_op jit(solution)/shard_map/all_to_all | solution.py:50
  47.4 3.0 collective-permute-start
  50.4 9.0 %collective-permute-done = bf16[1,48,640]{2,1,0:T(8,128)(2,1)S(1)} collective-permute-done((bf16[1,48,640]{2,1,0:T(8,128)(2,1)S(1)}, bf16[1,48,640]{2,1,0:T(8,128)(2,1)S(1)}, u32[]{:S(2)}, u32[]{:S(2)}) %collective-permute-start) | collective-permute-done | bytes 61472 | tf_op jit(solution)/shard_map/ppermute | solution.py:40
  59.4 15.7 %collective-permute-start.1 = (bf16[2,48,640]{2,1,0:T(8,128)(2,1)S(1)}, bf16[2,48,640]{2,1,0:T(8,128)(2,1)S(1)}, u32[]{:S(2)}, u32[]{:S(2)}) collective-permute-start(bf16[2,48,640]{2,1,0:T(8,128)(2,1)S(1)} %maximum_select_fusion.4), channel_id=1, source_target_pairs={{0,4},{1,5},{2,6},{3,7},{4,0},{5,1},{6,2},{7,3},{8,12},{9,13},{10,... | collective-permute-start | bytes 368648 | tf_op jit(solution)/shard_map/ppermute | solution.py:40
  75.7 3.6 %collective-permute-done.1 = bf16[2,48,640]{2,1,0:T(8,128)(2,1)S(1)} collective-permute-done((bf16[2,48,640]{2,1,0:T(8,128)(2,1)S(1)}, bf16[2,48,640]{2,1,0:T(8,128)(2,1)S(1)}, u32[]{:S(2)}, u32[]{:S(2)}) %collective-permute-start.1) | collective-permute-done | bytes 122912 | tf_op jit(solution)/shard_map/ppermute | solution.py:40
  79.4 1.4 collective-permute-start.4
  82.2 4.6 %collective-permute-done.2 = bf16[4,48,640]{2,1,0:T(8,128)(2,1)S(1)} collective-permute-done((bf16[4,48,640]{2,1,0:T(8,128)(2,1)S(1)}, bf16[4,48,640]{2,1,0:T(8,128)(2,1)S(1)}, u32[]{:S(2)}, u32[]{:S(2)}) %collective-permute-start.2) | collective-permute-done | bytes 245792 | tf_op jit(solution)/shard_map/ppermute | solution.py:40
  86.9 2.4 collective-permute-start.3
  91.0 12.1 %attention_forward.1 = (bf16[8,192,128]{2,1,0:T(8,128)(2,1)}, bf16[1024,768]{1,0:T(8,128)(2,1)S(1)}, bf16[576,1024]{1,0:T(8,128)(2,1)S(1)}, f32[8,1024]{1,0:T(8,128)S(1)}, f32[192,1024]{1,0:T(8,128)S(1)}) custom-call(bf16[1024,768]{1,0:T(8,128)(2,1)} %bitcast.153, bf16[768,640]{1,0:T(8,128)(2,1)S(1)} %bitcast.148, f32[32,1024]{1,0:T(8,128)S(1)} %get-tuple-element.58.cos_ref, ...), custom_call_target="tpu_custom_call" | custom-call | tf_op jit(solution)/shard_map/attention_forward/pallas_call | solution.py:225
  105.2 3.7 %all-to-all-start.1 = ((bf16[8,192,128]{2,1,0:T(8,128)(2,1)}), bf16[8,192,128]{2,1,0:T(8,128)(2,1)S(1)}, u32[]{:S(2)}, u32[]{:S(2)}) async-start(bf16[8,192,128]{2,1,0:T(8,128)(2,1)} %get-tuple-element.20), calls=%async_computation.1 | async-start | bytes 786432 | tf_op jit(solution)/shard_map/all_to_all | solution.py:294
  109.3 8.5 %all-to-all-done.1 = bf16[8,192,128]{2,1,0:T(8,128)(2,1)S(1)} async-done(((bf16[8,192,128]{2,1,0:T(8,128)(2,1)}), bf16[8,192,128]{2,1,0:T(8,128)(2,1)S(1)}, u32[]{:S(2)}, u32[]{:S(2)}) %all-to-all-start.1) | async-done | bytes 393248 | tf_op jit(solution)/shard_map/all_to_all | solution.py:294
  118.7 2.0 broadcast_select_fusion.1
  123.3 1.4 pad_maximum_fusion
  124.9 3.2 fusion.37
  128.2 1.8 fusion.10
  131.5 1.3 multiply_reduce_fusion.1
  132.8 1.2 fusion.33
  134.8 1.3 fusion.4
  136.1 1.9 copy.97
  138.0 1.7 bitcast_convert_fusion
  140.4 1.2 copy-done.18
  144.9 2.1 dynamic-slice_bitcast_fusion
  146.9 1.5 copy-done.15
  149.2 1.7 convert_reduce_fusion
  150.9 3.5 %all-to-all-start.3 = ((bf16[8,192,128]{2,1,0:T(8,128)(2,1)}), bf16[8,192,128]{2,1,0:T(8,128)(2,1)S(1)}, u32[]{:S(2)}, u32[]{:S(2)}) async-start(bf16[8,192,128]{2,1,0:T(8,128)(2,1)} %bitcast.181), calls=%async_computation.3 | async-start | bytes 786432 | tf_op jit(solution)/shard_map/all_to_all | solution.py:360
  154.7 2.0 fusion.2
  156.7 1.6 slice.117
  158.3 5.0 %all-to-all-done.3.do_ref = bf16[8,192,128]{2,1,0:T(8,128)(2,1)S(1)} async-done(((bf16[8,192,128]{2,1,0:T(8,128)(2,1)}), bf16[8,192,128]{2,1,0:T(8,128)(2,1)S(1)}, u32[]{:S(2)}, u32[]{:S(2)}) %all-to-all-start.3) | async-done | bytes 393248 | tf_op jit(solution)/shard_map/all_to_all | solution.py:360
  164.4 8.0 %attention_backward.1 = bf16[576,1024]{1,0:T(8,128)(2,1)S(1)} custom-call(bf16[8,192,128]{2,1,0:T(8,128)(2,1)S(1)} %all-to-all-done.3.do_ref, bf16[576,1024]{1,0:T(8,128)(2,1)S(1)} %get-tuple-element.23.qkv_ref, f32[8,1024]{1,0:T(8,128)S(1)} %get-tuple-element.24.lse_ref, f32[192,1024]{1,0:T(8,128)S(1)} %copy-done.3, ...), custom_call_target="tpu_custom_call" | custom-call | tf_op jit(solution)/shard_map/attention_backward/pallas_call | solution.py:225
  172.4 2.9 multiply_reduce_fusion
  175.4 4.3 %fusion = bf16[8,256,768]{2,1,0:T(8,128)(2,1)} fusion(bf16[8,256,768]{2,1,0:T(8,128)(2,1)} %collective-permute-done.6, bf16[8,2,256,768]{3,2,1,0:T(8,128)(2,1)S(1)} %bitcast.159, s32[]{:T(128)S(6)} %select_n.165), kind=kLoop, calls=%fused_computation.1 | loop fusion | flops 6291456 | bytes 9437188 | tf_op jit(solution)/shard_map/convert_element_type | solution.py:79
  179.7 1.2 copy-done.1
  185.5 1.6 collective-permute-done.5
  187.4 38.4 %all_to_all.40 = bf16[8,48,768]{2,1,0:T(8,128)(2,1)} all-to-all(bf16[8,48,768]{2,1,0:T(8,128)(2,1)S(1)} %fusion.11), channel_id=1, replica_groups={{0,2,4,6,8,10,12,14},{1,3,5,7,9,11,13,15},{16,18,20,22,24,26,28,30},{17..., dimensions={0} | all-to-all | bytes 1179648 | tf_op jit(solution)/shard_map/all_to_all | solution.py:74
  225.8 4.4 %all-to-all-start.4 = ((bf16[8,128,768]{2,1,0:T(8,128)(2,1)}), bf16[8,128,768]{2,1,0:T(8,128)(2,1)}, u32[]{:S(2)}, u32[]{:S(2)}) async-start(bf16[8,128,768]{2,1,0:T(8,128)(2,1)} %bitcast.180), calls=%async_computation.4 | async-start | bytes 3145728 | tf_op jit(solution)/shard_map/all_to_all | solution.py:385
  231.8 49.5 %all-reduce.3.cloned.1.call-done = bf16[8,8,32,768]{3,2,0,1:T(8,128)(2,1)} async-done(((bf16[8,8,32,768]{3,2,0,1:T(8,128)(2,1)}), bf16[8,8,32,768]{3,2,0,1:T(8,128)(2,1)}) %all-reduce.3.cloned.1.call-update) | async-done | bytes 3145744
  281.2 2.4 dynamic-slice_bitcast_fusion.1
  283.7 5.7 %all-to-all-start.6 = ((bf16[8,32,768]{2,1,0:T(8,128)(2,1)}), bf16[8,32,768]{2,1,0:T(8,128)(2,1)}, u32[]{:S(2)}, u32[]{:S(2)}) async-start(bf16[8,32,768]{2,1,0:T(8,128)(2,1)} %dynamic-slice_bitcast_fusion.1), calls=%async_computation.6 | async-start | bytes 786432 | tf_op jit(solution)/shard_map/all_to_all | solution.py:74
  289.4 1.4 fusion.3
  291.9 1.7 convert_reduce_fusion.1
  293.7 6.1 %all-to-all-done.6 = bf16[8,32,768]{2,1,0:T(8,128)(2,1)} async-done(((bf16[8,32,768]{2,1,0:T(8,128)(2,1)}), bf16[8,32,768]{2,1,0:T(8,128)(2,1)}, u32[]{:S(2)}, u32[]{:S(2)}) %all-to-all-start.6) | async-done | bytes 393248 | tf_op jit(solution)/shard_map/all_to_all | solution.py:74
  301.9 3.7 %all-to-all-start.7 = ((bf16[8,80,768]{2,1,0:T(8,128)(2,1)}), bf16[8,80,768]{2,1,0:T(8,128)(2,1)S(1)}, u32[]{:S(2)}, u32[]{:S(2)}) async-start(bf16[8,80,768]{2,1,0:T(8,128)(2,1)} %broadcast_in_dim.27), calls=%async_computation.7 | async-start | bytes 1966080 | tf_op jit(solution)/shard_map/all_to_all | solution.py:23
  305.9 1.2 fusion.17
  307.1 13.6 %all-to-all-done.7 = bf16[8,80,768]{2,1,0:T(8,128)(2,1)S(1)} async-done(((bf16[8,80,768]{2,1,0:T(8,128)(2,1)}), bf16[8,80,768]{2,1,0:T(8,128)(2,1)S(1)}, u32[]{:S(2)}, u32[]{:S(2)}) %all-to-all-start.7) | async-done | bytes 983072 | tf_op jit(solution)/shard_map/all_to_all | solution.py:23
  (185 shorter events, 37.6 us)
Async XLA Ops:
  9.4 7.1 %copy-start.35 = (bf16[72,768]{1,0:T(8,128)(2,1)S(1)}, bf16[72,768]{1,0:T(8,128)(2,1)}, u32[]{:S(2)}) copy-start(bf16[72,768]{1,0:T(8,128)(2,1)} %param.18) | copy-start | bytes 331780
  9.4 7.1 %copy-start.36 = (bf16[48,768]{1,0:T(8,128)(2,1)S(1)}, bf16[48,768]{1,0:T(8,128)(2,1)}, u32[]{:S(2)}) copy-start(bf16[48,768]{1,0:T(8,128)(2,1)} %param.15) | copy-start | bytes 221188
  9.4 27.9 %all-to-all-start = ((bf16[8,128,768]{2,1,0:T(8,128)(2,1)}), bf16[8,128,768]{2,1,0:T(8,128)(2,1)S(1)}, u32[]{:S(2)}, u32[]{:S(2)}) async-start(bf16[8,128,768]{2,1,0:T(8,128)(2,1)} %bitcast.1), calls=%async_computation | async-start | bytes 3145728 | tf_op jit(solution)/shard_map/all_to_all | solution.py:266
  15.8 109.1 %all-gather.2.cloned.1.call-start = ((), (), s32[]{:S(2)}) async-start(), calls=%async_computation.8 | async-start | bytes 3760128 | tf_op jit(solution)/shard_map/all_gather | solution.py:272
  38.6 7.4 %copy-start.38 = (bf16[48]{0:T(256)(128)(2,1)S(1)}, bf16[48]{0:T(256)(128)(2,1)}, u32[]{:S(2)}) copy-start(bf16[48]{0:T(256)(128)(2,1)} %param.13) | copy-start | bytes 292
  38.6 7.5 %copy-start.39 = (bf16[48]{0:T(256)(128)(2,1)S(1)}, bf16[48]{0:T(256)(128)(2,1)}, u32[]{:S(2)}) copy-start(bf16[48]{0:T(256)(128)(2,1)} %param.16) | copy-start | bytes 292
  38.6 7.6 %copy-start.34 = (bf16[48,2304]{1,0:T(8,128)(2,1)S(1)}, bf16[48,2304]{1,0:T(8,128)(2,1)}, u32[]{:S(2)}) copy-start(bf16[48,2304]{1,0:T(8,128)(2,1)} %param.14) | copy-start | bytes 663556
  38.6 36.4 %copy-start.40 = (s32[8]{0:T(128)S(1)}, s32[8]{0:T(128)}, u32[]{:S(2)}) copy-start(s32[8]{0:T(128)} %param.12) | copy-start | bytes 100
  38.7 36.4 %copy-start.41 = (s32[2]{0:T(128)S(1)}, s32[2]{0:T(128)}, u32[]{:S(2)}) copy-start(s32[2]{0:T(128)} %param.11) | copy-start | bytes 28
  38.9 40.5 %all-to-all-start.2 = ((bf16[8,120,768]{2,1,0:T(8,128)(2,1)}), bf16[8,120,768]{2,1,0:T(8,128)(2,1)}, u32[]{:S(2)}, u32[]{:S(2)}) async-start(bf16[8,120,768]{2,1,0:T(8,128)(2,1)} %broadcast_in_dim.25), calls=%async_computation.2 | async-start | bytes 2949120 | tf_op jit(solution)/shard_map/all_to_all | solution.py:50
  47.4 12.0 %collective-permute-start = (bf16[1,48,640]{2,1,0:T(8,128)(2,1)S(1)}, bf16[1,48,640]{2,1,0:T(8,128)(2,1)S(1)}, u32[]{:S(2)}, u32[]{:S(2)}) collective-permute-start(bf16[1,48,640]{2,1,0:T(8,128)(2,1)S(1)} %get-tuple-element.56), channel_id=1, source_target_pairs={{0,8},{1,9},{2,10},{3,11},{4,12},{5,13},{6,14},{7,15},{8,0},{9,1},... | collective-permute-start | bytes 184328 | tf_op jit(solution)/shard_map/ppermute | solution.py:40
  59.4 19.9 %collective-permute-start.1 = (bf16[2,48,640]{2,1,0:T(8,128)(2,1)S(1)}, bf16[2,48,640]{2,1,0:T(8,128)(2,1)S(1)}, u32[]{:S(2)}, u32[]{:S(2)}) collective-permute-start(bf16[2,48,640]{2,1,0:T(8,128)(2,1)S(1)} %maximum_select_fusion.4), channel_id=1, source_target_pairs={{0,4},{1,5},{2,6},{3,7},{4,0},{5,1},{6,2},{7,3},{8,12},{9,13},{10,... | collective-permute-start | bytes 368648 | tf_op jit(solution)/shard_map/ppermute | solution.py:40
  79.3 7.5 %collective-permute-start.2 = (bf16[4,48,640]{2,1,0:T(8,128)(2,1)S(1)}, bf16[4,48,640]{2,1,0:T(8,128)(2,1)S(1)}, u32[]{:S(2)}, u32[]{:S(2)}) collective-permute-start(bf16[4,48,640]{2,1,0:T(8,128)(2,1)S(1)} %bitcast.185), channel_id=1, source_target_pairs={{0,2},{1,3},{2,0},{3,1},{4,6},{5,7},{6,4},{7,5},{8,10},{9,11},{10,... | collective-permute-start | bytes 737288 | tf_op jit(solution)/shard_map/ppermute | solution.py:40
  79.4 39.3 %collective-permute-start.4 = (bf16[8,120,768]{2,1,0:T(8,128)(2,1)}, bf16[8,120,768]{2,1,0:T(8,128)(2,1)}, u32[]{:S(2)}, u32[]{:S(2)}) collective-permute-start(bf16[8,120,768]{2,1,0:T(8,128)(2,1)} %all-to-all-done.2), channel_id=1, source_target_pairs={{0,1},{1,0},{2,3},{3,2},{4,5},{5,4},{6,7},{7,6},{8,9},{9,8},{10,11... | collective-permute-start | bytes 4423688 | tf_op jit(solution)/shard_map/ppermute | solution.py:57
  86.9 3.8 %collective-permute-start.3 = (bf16[8,48,640]{2,1,0:T(8,128)(2,1)S(1)}, bf16[8,48,640]{2,1,0:T(8,128)(2,1)S(1)}, u32[]{:S(2)}, u32[]{:S(2)}) collective-permute-start(bf16[8,48,640]{2,1,0:T(8,128)(2,1)S(1)} %bitcast.176), channel_id=1, source_target_pairs={{0,1},{1,0},{2,3},{3,2},{4,5},{5,4},{6,7},{7,6},{8,9},{9,8},{10,11... | collective-permute-start | bytes 1474568 | tf_op jit(solution)/shard_map/ppermute | solution.py:40
  105.2 12.6 %all-to-all-start.1 = ((bf16[8,192,128]{2,1,0:T(8,128)(2,1)}), bf16[8,192,128]{2,1,0:T(8,128)(2,1)S(1)}, u32[]{:S(2)}, u32[]{:S(2)}) async-start(bf16[8,192,128]{2,1,0:T(8,128)(2,1)} %get-tuple-element.20), calls=%async_computation.1 | async-start | bytes 786432 | tf_op jit(solution)/shard_map/all_to_all | solution.py:294
  117.8 3.2 copy-start.21
  121.1 1.8 copy-start.13
  122.9 1.8 copy-start.8
  124.9 3.3 copy-start.16
  124.9 3.3 copy-start.28
  128.2 3.0 copy-start.20
  132.8 2.0 copy-start.14
  138.0 1.7 copy-start.29
  144.9 3.6 %copy-start.15 = (bf16[8,2,256,768]{3,2,1,0:T(8,128)(2,1)}, bf16[8,2,256,768]{3,2,1,0:T(8,128)(2,1)S(1)}, u32[]{:S(2)}) copy-start(bf16[8,2,256,768]{3,2,1,0:T(8,128)(2,1)S(1)} %constant_dynamic-update-slice_fusion) | copy-start | bytes 18874372
  148.5 26.9 %collective-permute-start.6 = (bf16[8,256,768]{2,1,0:T(8,128)(2,1)}, bf16[8,256,768]{2,1,0:T(8,128)(2,1)}, u32[]{:S(2)}, u32[]{:S(2)}) collective-permute-start(bf16[8,256,768]{2,1,0:T(8,128)(2,1)} %dynamic-slice_bitcast_fusion), channel_id=1, source_target_pairs={{0,1},{1,0},{2,3},{3,2},{4,5},{5,4},{6,7},{7,6},{8,9},{9,8},{10,11... | collective-permute-start | bytes 9437192 | tf_op jit(solution)/shard_map/ppermute | solution.py:68
  150.9 12.3 %all-to-all-start.3 = ((bf16[8,192,128]{2,1,0:T(8,128)(2,1)}), bf16[8,192,128]{2,1,0:T(8,128)(2,1)S(1)}, u32[]{:S(2)}, u32[]{:S(2)}) async-start(bf16[8,192,128]{2,1,0:T(8,128)(2,1)} %bitcast.181), calls=%async_computation.3 | async-start | bytes 786432 | tf_op jit(solution)/shard_map/all_to_all | solution.py:360
  154.4 126.8 %all-reduce.3.cloned.1.call-start = ((), (), s32[]{:S(2)}) async-start(), calls=%async_computation.9 | async-start | bytes 6291456
  164.4 8.0 %copy-start.7 = (bf16[8,128,768]{2,1,0:T(8,128)(2,1)S(1)}, bf16[8,128,768]{2,1,0:T(8,128)(2,1)}, u32[]{:S(2)}) copy-start(bf16[8,128,768]{2,1,0:T(8,128)(2,1)} %copy-done.6) | copy-start | bytes 4718596
  164.4 10.9 %slice-start = ((s8[6291456]{0:T(1024)(128)(4,1)}), s8[4194304]{0:T(1024)(128)(4,1)S(1)}, s32[]{:S(2)}) async-start(s8[6291456]{0:T(1024)(128)(4,1)} %bitcast.158), calls=%async_computation.10 | async-start | bytes 8388608
  172.4 2.9 copy-start
  172.4 2.9 slice-start.1
  179.7 1.8 copy-start.5
  182.8 1.9 copy-start.26
  184.8 2.4 collective-permute-start.5
  225.8 4.5 %copy-start.42 = (u32[128]{0:T(128)S(1)}, u32[128]{0:T(128)}, u32[]{:S(2)}) copy-start(u32[128]{0:T(128)} %constant.118) | copy-start | bytes 1540
  225.8 5.1 %copy-start.12 = (bf16[2,128,768]{2,1,0:T(8,128)(2,1)S(1)}, bf16[2,128,768]{2,1,0:T(8,128)(2,1)}, u32[]{:S(2)}) copy-start(bf16[2,128,768]{2,1,0:T(8,128)(2,1)} %param.10) | copy-start | bytes 1179652
  225.8 63.6 %copy-start.17 = (bf16[8,2,72,768]{3,2,1,0:T(8,128)(2,1)S(1)}, bf16[8,2,72,768]{3,2,1,0:T(8,128)(2,1)}, u32[]{:S(2)}) copy-start(bf16[8,2,72,768]{3,2,1,0:T(8,128)(2,1)} %pad_maximum_fusion) | copy-start | bytes 5308420
  225.8 57.9 %all-to-all-start.4 = ((bf16[8,128,768]{2,1,0:T(8,128)(2,1)}), bf16[8,128,768]{2,1,0:T(8,128)(2,1)}, u32[]{:S(2)}, u32[]{:S(2)}) async-start(bf16[8,128,768]{2,1,0:T(8,128)(2,1)} %bitcast.180), calls=%async_computation.4 | async-start | bytes 3145728 | tf_op jit(solution)/shard_map/all_to_all | solution.py:385
  230.2 59.1 %copy-start.10 = (f32[256,768]{1,0:T(8,128)S(1)}, f32[256,768]{1,0:T(8,128)}, u32[]{:S(2)}) copy-start(f32[256,768]{1,0:T(8,128)} %copy-done.8) | copy-start | bytes 2359300
  230.2 59.1 %copy-start.25 = (bf16[256,1152]{1,0:T(8,128)(2,1)S(1)}, bf16[256,1152]{1,0:T(8,128)(2,1)}, u32[]{:S(2)}) copy-start(bf16[256,1152]{1,0:T(8,128)(2,1)} %get-tuple-element.27) | copy-start | bytes 1769476
  283.7 16.1 %all-to-all-start.6 = ((bf16[8,32,768]{2,1,0:T(8,128)(2,1)}), bf16[8,32,768]{2,1,0:T(8,128)(2,1)}, u32[]{:S(2)}, u32[]{:S(2)}) async-start(bf16[8,32,768]{2,1,0:T(8,128)(2,1)} %dynamic-slice_bitcast_fusion.1), calls=%async_computation.6 | async-start | bytes 786432 | tf_op jit(solution)/shard_map/all_to_all | solution.py:74
  300.8 4.7 %copy-start.37 = (f32[2,128]{1,0:T(2,128)S(1)}, f32[2,128]{1,0:T(2,128)}, u32[]{:S(2)}) copy-start(f32[2,128]{1,0:T(2,128)} %get-tuple-element.62) | copy-start | bytes 3076
  301.9 4.0 %copy-start.23 = (f32[256,768]{1,0:T(8,128)S(1)}, f32[256,768]{1,0:T(8,128)}, u32[]{:S(2)}) copy-start(f32[256,768]{1,0:T(8,128)} %get-tuple-element.40) | copy-start | bytes 2359300
  301.9 18.8 %all-to-all-start.7 = ((bf16[8,80,768]{2,1,0:T(8,128)(2,1)}), bf16[8,80,768]{2,1,0:T(8,128)(2,1)S(1)}, u32[]{:S(2)}, u32[]{:S(2)}) async-start(bf16[8,80,768]{2,1,0:T(8,128)(2,1)} %broadcast_in_dim.27), calls=%async_computation.7 | async-start | bytes 1966080 | tf_op jit(solution)/shard_map/all_to_all | solution.py:23
  324.8 2.3 copy-start.31
  324.8 2.3 copy-start.32
  324.8 2.3 copy-start.33
  (13 other events, 16.4 us)
Sparse Core Ops, SparseCore 0:
  19.0 67.7 all-gather.1
  179.8 101.3 all-reduce.2

commit v3 on v2

--- a/solution.py
+++ b/solution.py
@@ -59,13 +59,8 @@
     return jnp.where(even, mine, other), jnp.where(even, other, mine)
 
 
-def core_sum(parts, axis):
-    n = lax.axis_size(axis)
-    core = lax.axis_index(axis) % 2
-    paired = parts.reshape(n // 2, 2, *parts.shape[1:])
-    away = lax.dynamic_index_in_dim(paired, 1 - core, 1, keepdims=False)
-    kept = lax.dynamic_index_in_dim(paired, core, 1, keepdims=False)
-    came = lax.ppermute(away, axis, core_pairs(n))
+def core_sum(kept, away, axis):
+    came = lax.ppermute(away, axis, core_pairs(lax.axis_size(axis)))
     return low(kept.astype(jnp.float32) + came.astype(jnp.float32))
 
 
@@ -168,7 +163,21 @@
 
 
 def backward_kernel(
-    do_ref, qkv_ref, lse_ref, o_ref, cos_ref, sin_ref, bias_ref, keep_ref, g_ref, dk_ref, dv_ref
+    do_ref,
+    qkv_ref,
+    lse_ref,
+    o_ref,
+    cos_ref,
+    sin_ref,
+    bias_ref,
+    keep_ref,
+    seq_ref,
+    w_ref,
+    g_ref,
+    ga_ref,
+    gain_ref,
+    dk_ref,
+    dv_ref,
 ):
     span, full_len = o_ref.shape
     group = span // HD
@@ -218,17 +227,168 @@
         g_ref[2 * span + head * HD : 2 * span + (head + 1) * HD] = dv_ref[...].astype(
             jnp.bfloat16
         )
-
-
-def on_device(kernel, outs, args, scratch=(), name=None):
+    for start in range(0, full_len, ROWS):
+        rows = slice(start, start + ROWS)
+        grad_a = product(g_ref[:, rows].T, w_ref[:, : 3 * span], NT)
+        x = seq_ref[rows].astype(jnp.float32)
+        centre = x - jnp.mean(x, -1, keepdims=True)
+        variance = jnp.mean(centre * centre, -1, keepdims=True)
+        summed = jnp.sum(grad_a * (centre * lax.rsqrt(variance + EPS)), 0, keepdims=True)
+        gain_ref[...] = summed if start == 0 else gain_ref[...] + summed
+        for first in range(0, ROWS, blk):
+            ga_ref[(start + first) // blk] = grad_a[first : first + blk].astype(jnp.bfloat16)
+
+
+def mlp_kernel(
+    tok_ref,
+    att_ref,
+    cot_ref,
+    gain_ref,
+    wout_ref,
+    win_ref,
+    wdown_ref,
+    do_ref,
+    gm_ref,
+    mixed_ref,
+    b_ref,
+    hid_ref,
+    gg_ref,
+    grad_gain_ref,
+):
+    seqs, local_len, width = tok_ref.shape
+    spread = do_ref.shape[0] // seqs
+    span = do_ref.shape[1]
+    hidden = hid_ref.shape[1]
+    resid = jnp.concatenate([tok_ref[k] for k in range(seqs)], 0).astype(jnp.float32)
+    att = jnp.concatenate([att_ref[k].T for k in range(seqs)], 0)
+    cot = jnp.concatenate([cot_ref[k] for k in range(seqs)], 0)
+    mixed = resid + product(att, wout_ref[...])
+    mixed_ref[...] = mixed
+    centre = mixed - jnp.mean(mixed, -1, keepdims=True)
+    inverse = lax.rsqrt(jnp.mean(centre * centre, -1, keepdims=True) + EPS)
+    normed = centre * inverse
+    b_low = (normed * gain_ref[...]).astype(jnp.bfloat16)
+    b_ref[...] = b_low
+    for first in range(0, hidden, hidden // 3):
+        here = slice(first, first + hidden // 3)
+        there = slice(hidden + first, hidden + first + hidden // 3)
+        gate_in = product(b_low, win_ref[:, here])
+        up_half = product(b_low, win_ref[:, there])
+        grad_hid = product(cot, wdown_ref[here], NT)
+        normal_cdf = 0.5 * (1.0 + lax.erf(gate_in * INV_ROOT_TWO))
+        gelu_out = gate_in * normal_cdf
+        hid_ref[:, here] = (gelu_out * up_half).astype(jnp.bfloat16)
+        normal_pdf = jnp.exp(-0.5 * gate_in * gate_in) * INV_ROOT_TWO_PI
+        gg_ref[:, here] = (grad_hid * up_half * (normal_cdf + gate_in * normal_pdf)).astype(
+            jnp.bfloat16
+        )
+        gg_ref[:, there] = (grad_hid * gelu_out).astype(jnp.bfloat16)
+    grad_b = product(gg_ref[...], win_ref[...], NT)
+    grad_gain_ref[...] = jnp.sum(grad_b * normed, 0, keepdims=True)
+    scaled = grad_b * gain_ref[...]
+    grad_mixed = cot.astype(jnp.float32) + inverse * (
+        scaled
+        - jnp.mean(scaled, -1, keepdims=True)
+        - normed * jnp.mean(scaled * normed, -1, keepdims=True)
+    )
+    gm_ref[...] = grad_mixed
+    grad_heads = product(wout_ref[...], grad_mixed.astype(jnp.bfloat16), NT).astype(jnp.bfloat16)
+    for seq in range(seqs):
+        for part in range(spread):
+            do_ref[seq * spread + part] = grad_heads[
+                part * span : (part + 1) * span, seq * local_len : (seq + 1) * local_len
+            ]
+
+
+def mlp_weights_kernel(
+    core_ref,
+    att_ref,
+    cot_ref,
+    wdown_ref,
+    gm_ref,
+    mixed_ref,
+    b_ref,
+    hid_ref,
+    gg_ref,
+    out_ref,
+    kept_ref,
+    away_ref,
+    extra_ref,
+    in_ref,
+    up_ref,
+    down_ref,
+):
+    seqs, _, local_len = att_ref.shape
+    width = cot_ref.shape[2]
+    ctx, pairs, chunk, _ = kept_ref.shape
+    depth = in_ref.shape[0] // (2 * pairs)
+    down_rows = down_ref.shape[0] // (2 * pairs)
+    count = in_ref.shape[1] // width
+    split = ctx * chunk - (count + 1) * depth
+    cot = jnp.concatenate([cot_ref[k] for k in range(seqs)], 0)
+    att = jnp.concatenate([att_ref[k] for k in range(seqs)], 1)
+    in_ref[...] = product(b_ref[...].T, gg_ref[...])
+    up_ref[...] = product(att, gm_ref[...].astype(jnp.bfloat16))
+    down_ref[...] = product(hid_ref[...].T, cot)
+    core = core_ref[0]
+    for pair in range(pairs):
+        for ref, which in ((kept_ref, core), (away_ref, 1 - core)):
+            wide = pl.ds(pl.multiple_of((2 * pair + which) * depth, 8), depth)
+            tall = pl.ds(pl.multiple_of((2 * pair + which) * down_rows, 8), split)
+            rows = jnp.concatenate(
+                [in_ref[wide, k * width : (k + 1) * width] for k in range(count)]
+                + [up_ref[wide], down_ref[tall]],
+                0,
+            ).astype(jnp.bfloat16)
+            for part in range(ctx):
+                ref[part, pair] = rows[part * chunk : (part + 1) * chunk]
+    for owner in range(2 * pairs):
+        extra_ref[owner] = down_ref[owner * down_rows + split : (owner + 1) * down_rows]
+    result = mixed_ref[...] + product(hid_ref[...], wdown_ref[...])
+    for seq in range(seqs):
+        out_ref[seq] = result[seq * local_len : (seq + 1) * local_len].astype(jnp.bfloat16)
+
+
+def qkv_weights_kernel(
+    core_ref, a_ref, g_ref, gain_one_ref, gain_two_ref, extra_ref, kept_ref, away_ref, w_ref
+):
+    pairs, depth, width = kept_ref.shape
+    span3 = g_ref.shape[0]
+    used = width - 128
+    w_ref[:, :span3] = product(a_ref[...].T, g_ref[...], NT)
+    lane = used - 128
+    gains = jnp.concatenate(
+        [
+            jnp.zeros((span3 - lane, width), jnp.float32),
+            gain_one_ref[...],
+            gain_two_ref[...],
+            jnp.zeros((used - span3 - 2, width), jnp.float32),
+        ],
+        0,
+    ).T
+    w_ref[:, span3:used] = gains[:, span3 - lane :]
+    for owner in range(2 * pairs):
+        extra = extra_ref[owner]
+        w_ref[owner * depth : (owner + 1) * depth, used:] = jnp.concatenate(
+            [extra[:, k * 128 : (k + 1) * 128] for k in range(width // 128)], 0
+        )
+    core = core_ref[0]
+    for pair in range(pairs):
+        for ref, which in ((kept_ref, core), (away_ref, 1 - core)):
+            rows = pl.ds(pl.multiple_of((2 * pair + which) * depth, 8), depth)
+            ref[pair] = w_ref[rows].astype(jnp.bfloat16)
+
+
+def on_device(kernel, outs, args, scratch=(), scalars=0, name=None):
     space = pl.BlockSpec(memory_space=pltpu.VMEM)
+    scalar = pl.BlockSpec(memory_space=pltpu.SMEM)
     return pl.pallas_call(
         kernel,
         out_shape=[jax.ShapeDtypeStruct(shape, dtype) for shape, dtype in outs],
-        in_specs=[space] * len(args),
+        in_specs=[scalar] * scalars + [space] * (len(args) - scalars),
         out_specs=[space] * len(outs),
         scratch_shapes=list(scratch),
-        compiler_params=pltpu.CompilerParams(vmem_limit_bytes=48 * 1024 * 1024),
+        compiler_params=pltpu.CompilerParams(vmem_limit_bytes=56 * 1024 * 1024),
         name=name,
     )(*args)
 
@@ -265,15 +425,14 @@
     ).reshape(fsdp * depth, 640)
     sequence = lax.all_to_all(jnp.repeat(tokens, spread, axis=0), "ctx", 0, 0, tiled=True)
 
-    wqkv_part = first_all[:, : 3 * span]
+    win_all = lax.all_gather(w_in, "fsdp", axis=0, tiled=True)
+    stacked, sequence, first_all = lax.optimization_barrier(
+        (jnp.concatenate([w_out, w_down], 0), sequence, first_all)
+    )
+    stacked_all = gather_two_level(stacked, "fsdp")
+
     gain_one = first_all[:, 3 * span]
     gain_two = first_all[:, 3 * span + 1]
-
-    win_all = lax.all_gather(w_in, "fsdp", axis=0, tiled=True)
-    stacked, sequence = lax.optimization_barrier(
-        (jnp.concatenate([w_out, w_down], 0), sequence)
-    )
-    stacked_all = gather_two_level(stacked, "fsdp")
 
     cosine, sine = tables(all_pos)
     bias = jnp.where(all_keep, 0.0, NEGATIVE).astype(f32)[:, None]
@@ -302,89 +461,101 @@
     wdown_all = whole(depth, down_rows)
 
     resid = tokens.astype(f32).reshape(rows, width)
-    mixed = resid + jnp.einsum(
-        "sdr,de->sre", att_turned, wout_all, preferred_element_type=f32
-    ).reshape(rows, width)
-    normed_mid, normed_two, inverse_two = norm_forward(mixed, gain_two)
-    b_low = low(normed_mid)
-    gate_up = jnp.dot(b_low, win_all, preferred_element_type=f32)
-    gate_in = gate_up[:, :hidden]
-    up_half = gate_up[:, hidden:]
-    normal_cdf = 0.5 * (1.0 + lax.erf(gate_in * INV_ROOT_TWO))
-    gelu_out = gate_in * normal_cdf
-    hid_low = low(gelu_out * up_half)
-    output = mixed + jnp.dot(hid_low, wdown_all, preferred_element_type=f32)
-
-    grad_low = cotangent.reshape(rows, width)
-    grad_out = grad_low.astype(f32)
-    grad_hid = jnp.einsum("rd,fd->rf", grad_low, wdown_all, preferred_element_type=f32)
-    normal_pdf = jnp.exp(-0.5 * gate_in * gate_in) * INV_ROOT_TWO_PI
-    grad_gate = grad_hid * up_half * (normal_cdf + gate_in * normal_pdf)
-    grad_up = grad_hid * gelu_out
-    grad_gate_up = low(jnp.concatenate([grad_gate, grad_up], 1))
-    grad_b = jnp.einsum("rf,df->rd", grad_gate_up, win_all, preferred_element_type=f32)
-    grad_norm_two, grad_gain_two = norm_backward(grad_b, gain_two, normed_two, inverse_two)
-    grad_mixed = grad_out + grad_norm_two
-    grad_att = low(grad_mixed)
-    grad_att = grad_att.reshape(seqs, local_len, width)
-    grad_heads = low(
-        jnp.einsum("de,sre->sdr", wout_all, grad_att, preferred_element_type=f32)
-    ).reshape(ctx, span, local_len)
-    hid_low, b_low, grad_gate_up, grad_heads = lax.optimization_barrier(
-        (hid_low, b_low, grad_gate_up, grad_heads)
-    )
-    grad_wout = jnp.einsum("sdr,sre->de", att_turned, grad_att, preferred_element_type=f32)
-    grad_wdown = jnp.einsum("rf,rd->fd", hid_low, grad_low, preferred_element_type=f32)
-    grad_win = low(jnp.einsum("rd,rf->df", b_low, grad_gate_up, preferred_element_type=f32))
     count = w_in.shape[1] // width
     main_rows = ((count + 1) * depth + down_rows) // (8 * ctx) * 8 * ctx
     chunk = main_rows // ctx
-    grad_wdown = low(grad_wdown).reshape(fsdp, down_rows, width)
     split = main_rows - (count + 1) * depth
-    grads_main = jnp.concatenate(
+    extra = down_rows - split
+    pairs = fsdp // 2
+    core = (lax.axis_index("fsdp") % 2).astype(jnp.int32)[None]
+    grad_heads, grad_mixed, mixed, b_low, hid_low, grad_gate_up, grad_gain_two = on_device(
+        mlp_kernel,
         [
-            *[
-                grad_win[:, k * width : (k + 1) * width].reshape(fsdp, depth, width)
-                for k in range(count)
-            ],
-            low(grad_wout).reshape(fsdp, depth, width),
-            grad_wdown[:, :split],
+            ((ctx, span, local_len), jnp.bfloat16),
+            ((rows, width), f32),
+            ((rows, width), f32),
+            ((rows, width), jnp.bfloat16),
+            ((rows, hidden), jnp.bfloat16),
+            ((rows, 2 * hidden), jnp.bfloat16),
+            ((1, width), f32),
         ],
-        1,
-    )
-    main_pair = core_sum(grads_main, "fsdp")
-    main_pair = main_pair.reshape(fsdp // 2, ctx, chunk, width).transpose(1, 0, 2, 3)
-    main_part = lax.psum_scatter(main_pair, "ctx", scatter_dimension=0, tiled=True)
-    main_part = main_part.reshape(fsdp // 2, chunk, width)
+        (
+            tokens,
+            att_turned,
+            cotangent,
+            gain_two.astype(f32)[None, :],
+            wout_all,
+            win_all,
+            wdown_all,
+        ),
+        name="mlp",
+    )
+    output, main_kept, main_away, down_extra = on_device(
+        mlp_weights_kernel,
+        [
+            (tokens.shape, jnp.bfloat16),
+            ((ctx, pairs, chunk, width), jnp.bfloat16),
+            ((ctx, pairs, chunk, width), jnp.bfloat16),
+            ((fsdp, extra, width), f32),
+        ],
+        (
+            core,
+            att_turned,
+            cotangent,
+            wdown_all,
+            grad_mixed,
+            mixed,
+            b_low,
+            hid_low,
+            grad_gate_up,
+        ),
+        [
+            pltpu.VMEM((fsdp * depth, 2 * hidden), f32),
+            pltpu.VMEM((width, width), f32),
+            pltpu.VMEM((hidden, width), f32),
+        ],
+        scalars=1,
+        name="mlp_weights",
+    )
+    main_pair = core_sum(main_kept, main_away, "fsdp")
+    main_part = lax.psum_scatter(
+        main_pair.reshape(-1, chunk, width), "ctx", scatter_dimension=0, tiled=True
+    )
+    main_part = lax.optimization_barrier(main_part)
 
     all_grad = lax.all_to_all(grad_heads, "ctx", 0, 0, tiled=True)
-    grad_qkv = on_device(
+    grad_qkv, grad_a_part, grad_gain_one = on_device(
         backward_kernel,
-        [((3 * span, full_len), jnp.bfloat16)],
-        (all_grad, qkv, log_total, unrounded, cosine, sine, bias, keep_row),
+        [
+            ((3 * span, full_len), jnp.bfloat16),
+            ((ctx, local_len, width), jnp.bfloat16),
+            ((1, width), f32),
+        ],
+        (
+            all_grad,
+            qkv,
+            log_total,
+            unrounded,
+            cosine,
+            sine,
+            bias,
+            keep_row,
+            sequence,
+            first_all,
+        ),
         [pltpu.VMEM((HD, full_len), f32)] * 2,
         name="attention_backward",
-    )[0]
-    grad_a_part = jnp.einsum("fr,df->rd", grad_qkv, wqkv_part, preferred_element_type=f32)
-    grad_wqkv = low(jnp.einsum("rd,fr->df", a_low, grad_qkv, preferred_element_type=f32))
-    _, seq_normed, _ = norm_forward(sequence.astype(f32), gain_one)
-    grad_gain_one = jnp.sum(grad_a_part * seq_normed, 0)
-    last = jnp.concatenate(
-        [
-            grad_wqkv,
-            jnp.stack([low(grad_gain_one), low(grad_gain_two)], 1),
-            jnp.zeros((fsdp * depth, 640 - 3 * span - 2), jnp.bfloat16),
-        ],
-        1,
-    )
-    last = jnp.concatenate(
-        [last.reshape(fsdp, -1, width), grad_wdown[:, split:]], 1
-    )
-    last = core_sum(last, "fsdp")
-    last_rows = last.shape[1]
-    grad_a_parts = lax.all_to_all(
-        low(grad_a_part).reshape(ctx, local_len, width), "ctx", 0, 0, tiled=True
-    )
+    )
+    grad_a_parts = lax.all_to_all(grad_a_part, "ctx", 0, 0, tiled=True)
+    last_kept, last_away = on_device(
+        qkv_weights_kernel,
+        [((pairs, depth, width), jnp.bfloat16)] * 2,
+        (core, a_low, grad_qkv, grad_gain_one, grad_gain_two, down_extra),
+        [pltpu.VMEM((width, width), f32)],
+        scalars=1,
+        name="qkv_weights",
+    )
+    last = core_sum(last_kept, last_away, "fsdp")
     grad_a = jnp.sum(
         grad_a_parts.reshape(seqs, spread, local_len, width).astype(f32), 1
     ).reshape(rows, width)
@@ -396,10 +567,10 @@
     main_part = spread_sum(main_part, "fsdp")
     share = jnp.concatenate([last, main_part], 0)
     ends = gather_by_exchange(share, "ctx", ctx)
-    extra = down_rows - split
-    last_all = ends[:, : last_rows - extra].reshape(ctx, depth, 640).astype(f32)
-    down_end = jnp.sum(ends[:, last_rows - extra : last_rows].astype(f32), 0)
-    summed = ends[:, last_rows:].reshape(main_rows, width).astype(f32)
+    last_all = ends[:, :depth].astype(f32)
+    down_end = jnp.sum(last_all[:, :, width - 128 :], 0)
+    down_end = down_end.reshape(-1, extra, 128).transpose(1, 0, 2).reshape(extra, width)
+    summed = ends[:, depth:].reshape(main_rows, width).astype(f32)
     grad_wqkv_out = (
         jnp.sum(last_all[:, :, : 3 * span].reshape(seqs, spread, depth, 3, span), 0)
         .transpose(1, 2, 0, 3)
@@ -407,7 +578,7 @@
     )
     gains_out = jnp.sum(last_all[:, :, 3 * span : 3 * span + 2], 0)
     return (
-        low(output.reshape(tokens.shape)),
+        output,
         grad_input.reshape(tokens.shape),
         gains_out[:, 0],
         grad_wqkv_out,

time: 339 us -> 267 us (0.79)
  waiting for transfers between devices: 123 us -> 65.9 us
  Pallas kernels: 20.1 us -> 47.8 us
  starting transfers between devices: 58.9 us -> 38.9 us
  blocking collectives: 38.4 us -> 58.2 us
  local copies, waits for them, and re-layouts: 35.6 us -> 16.3 us
  matrix products: 17 us -> 0 us
  other arithmetic: 26.4 us -> 21.2 us
    unnamed x3 -> x2, waiting for transfers between devices: 50.1 us -> 0.7 us
    all_to_all x0 -> x2, blocking collectives: none -> 43.1 us  [the longest x1 27.6 us: gather_two_level(): lax.all_to_all(jnp.broadcast_to(part[None], (n // 2, *part.shape)), axis,...]
    pallas_call x2 -> x5, Pallas kernels: 20.1 us -> 47.8 us  [on_device(): pl.pallas_call(kernel, out_shape=[jax.ShapeDtypeStruct(shape, dtype) for...]
    all_to_all x1, blocking collectives: 38.4 us -> 15.2 us  [spread_sum(): lax.all_to_all(parts, axis, 0, 0, tiled=True, axis_index_groups=groups)]
    all_to_all x1, waiting for transfers between devices: 20.8 us -> 3.06 us  [body(): lax.all_to_all(jnp.repeat(tokens, spread, axis=0), 'ctx', 0, 0, tiled=True)]
    dot_general x11 -> x0, matrix products: 17 us -> none  [the longest x1 3.25 us: body(): gate_up = jnp.dot(b_low, win_all, preferred_element_type=f32)]
    all_to_all x3 -> x1, waiting for transfers between devices: 4.98 us -> 20.9 us  [body(): grad_a_parts = lax.all_to_all(grad_a_part, 'ctx', 0, 0, tiled=True)]
    all_to_all x3 -> x1, starting transfers between devices: 15 us -> 3.71 us  [body(): grad_a_parts = lax.all_to_all(grad_a_part, 'ctx', 0, 0, tiled=True)]
  transfers between devices with their start and end apart: 16 -> 14, of which waited for: 11 -> 10; matrix products, arithmetic and copies ran while one was open for 10% -> 8% of each run, Pallas kernels for 6% -> 12%
where the time goes in v3:
time: 267 us; the launch traced here: 263 us
  waiting for transfers between devices  65.9 us (25%)
  blocking collectives  58.2 us (22%)
  Pallas kernels  47.8 us (18%)
  starting transfers between devices  38.9 us (15%)
  other arithmetic  21.2 us (8%)
  local copies, waits for them, and re-layouts  16.3 us (6%)
  between operations  14.7 us (6%)
    pallas_call x5, Pallas kernels, on_device(): pl.pallas_call(kernel, out_shape=[jax.ShapeDtypeStruct(shape, dtype) for...  47.8 us
    all_to_all x1, blocking collectives, gather_two_level(): lax.all_to_all(jnp.broadcast_to(part[None], (n // 2, *part.shape)), axis,...  27.6 us
    all_to_all x1, waiting for transfers between devices, body(): grad_a_parts = lax.all_to_all(grad_a_part, 'ctx', 0, 0, tiled=True)  20.9 us
    all_to_all x1, blocking collectives, body(): all_grad = lax.all_to_all(grad_heads, 'ctx', 0, 0, tiled=True)  15.4 us
    all_to_all x1, blocking collectives, spread_sum(): lax.all_to_all(parts, axis, 0, 0, tiled=True, axis_index_groups=groups)  15.2 us
    all_to_all x1, waiting for transfers between devices, gather_by_exchange(): lax.all_to_all(jnp.broadcast_to(part[None], (n, *part.shape)), axis, 0, 0)  13.7 us
    ppermute x4, starting transfers between devices, gather_doubling(): came = lax.ppermute(held, axis, [(k, k ^ bit) for k in range(n)])  13.5 us
    all_to_all x1, waiting for transfers between devices, spread_sum(): lax.all_to_all(parts, axis, 0, 0, tiled=True, axis_index_groups=groups)  9.91 us
  transfers between devices with their start and end apart: 14, of which 10 were waited for; matrix products, arithmetic and copies ran while one was open for 8% of the time, Pallas kernels for 12%

profile of v3, /device:TPU:1, one launch (start us, length us, event | category | flops | bytes accessed | tf_op | source)
XLA Modules:
  0.0 263.1 jit_solution(14084239551404081481)
XLA Ops:
  7.9 1.2 reshape.371
  11.5 4.5 %collective-permute-start = (bf16[1,48,640]{2,1,0:T(8,128)(2,1)S(1)}, bf16[1,48,640]{2,1,0:T(8,128)(2,1)S(1)}, u32[]{:S(2)}, u32[]{:S(2)}) collective-permute-start(bf16[1,48,640]{2,1,0:T(8,128)(2,1)S(1)} %get-tuple-element.69), channel_id=1, source_target_pairs={{0,8},{1,9},{2,10},{3,11},{4,12},{5,13},{6,14},{7,15},{8,0},{9,1},... | collective-permute-start | bytes 184328 | tf_op jit(solution)/shard_map/ppermute | solution.py:40
  16.0 1.3 broadcast_in_dim.21
  17.3 4.5 %all-to-all-start = ((bf16[8,128,768]{2,1,0:T(8,128)(2,1)}), bf16[8,128,768]{2,1,0:T(8,128)(2,1)S(1)}, u32[]{:S(2)}, u32[]{:S(2)}) async-start(bf16[8,128,768]{2,1,0:T(8,128)(2,1)} %bitcast.1), calls=%async_computation | async-start | bytes 3145728 | tf_op jit(solution)/shard_map/all_to_all | solution.py:426
  21.8 3.0 %collective-permute-start.1 = (bf16[2,48,640]{2,1,0:T(8,128)(2,1)S(1)}, bf16[2,48,640]{2,1,0:T(8,128)(2,1)S(1)}, u32[]{:S(2)}, u32[]{:S(2)}) collective-permute-start(bf16[2,48,640]{2,1,0:T(8,128)(2,1)S(1)} %maximum_select_fusion.4), channel_id=1, source_target_pairs={{0,4},{1,5},{2,6},{3,7},{4,0},{5,1},{6,2},{7,3},{8,12},{9,13},{10,... | collective-permute-start | bytes 368648 | tf_op jit(solution)/shard_map/ppermute | solution.py:40
  24.8 2.3 collective-permute-done.1
  27.2 2.4 collective-permute-start.2
  29.6 4.1 %collective-permute-done.2 = bf16[4,48,640]{2,1,0:T(8,128)(2,1)S(1)} collective-permute-done((bf16[4,48,640]{2,1,0:T(8,128)(2,1)S(1)}, bf16[4,48,640]{2,1,0:T(8,128)(2,1)S(1)}, u32[]{:S(2)}, u32[]{:S(2)}) %collective-permute-start.2) | collective-permute-done | bytes 245792 | tf_op jit(solution)/shard_map/ppermute | solution.py:40
  33.9 3.5 %collective-permute-start.3 = (bf16[8,48,640]{2,1,0:T(8,128)(2,1)S(1)}, bf16[8,48,640]{2,1,0:T(8,128)(2,1)S(1)}, u32[]{:S(2)}, u32[]{:S(2)}) collective-permute-start(bf16[8,48,640]{2,1,0:T(8,128)(2,1)S(1)} %bitcast.88), channel_id=1, source_target_pairs={{0,1},{1,0},{2,3},{3,2},{4,5},{5,4},{6,7},{7,6},{8,9},{9,8},{10,11... | collective-permute-start | bytes 1474568 | tf_op jit(solution)/shard_map/ppermute | solution.py:40
  37.4 1.5 collective-permute-done.3
  39.1 1.0 copy.69
  40.1 3.1 %all-to-all-done = bf16[8,128,768]{2,1,0:T(8,128)(2,1)S(1)} async-done(((bf16[8,128,768]{2,1,0:T(8,128)(2,1)}), bf16[8,128,768]{2,1,0:T(8,128)(2,1)S(1)}, u32[]{:S(2)}, u32[]{:S(2)}) %all-to-all-start) | async-done | bytes 1572896 | tf_op jit(solution)/shard_map/all_to_all | solution.py:426
  43.3 27.6 %all_to_all.40 = bf16[8,120,768]{2,1,0:T(8,128)(2,1)S(1)} all-to-all(bf16[8,120,768]{2,1,0:T(8,128)(2,1)S(1)} %broadcast_in_dim.26), channel_id=1, replica_groups={{0,2,4,6,8,10,12,14},{1,3,5,7,9,11,13,15},{16,18,20,22,24,26,28,30},{17..., dimensions={0} | all-to-all | bytes 2949120 | tf_op jit(solution)/shard_map/all_to_all | solution.py:50
  71.0 2.7 %collective-permute-start.4 = (bf16[8,120,768]{2,1,0:T(8,128)(2,1)S(1)}, bf16[8,120,768]{2,1,0:T(8,128)(2,1)}, u32[]{:S(2)}, u32[]{:S(2)}) collective-permute-start(bf16[8,120,768]{2,1,0:T(8,128)(2,1)S(1)} %all_to_all.40), channel_id=1, source_target_pairs={{0,1},{1,0},{2,3},{3,2},{4,5},{5,4},{6,7},{7,6},{8,9},{9,8},{10,11... | collective-permute-start | bytes 4423688 | tf_op jit(solution)/shard_map/ppermute | solution.py:57
  75.0 1.0 copy.70.bias_ref
  76.0 1.3 fusion.9
  77.4 1.2 multiply_sine_fusion
  78.6 12.8 %attention_forward.1 = (bf16[8,192,128]{2,1,0:T(8,128)(2,1)}, bf16[1024,768]{1,0:T(8,128)(2,1)}, bf16[576,1024]{1,0:T(8,128)(2,1)}, f32[8,1024]{1,0:T(8,128)}, f32[192,1024]{1,0:T(8,128)}) custom-call(bf16[1024,768]{1,0:T(8,128)(2,1)} %bitcast.77, bf16[768,640]{1,0:T(8,128)(2,1)} %bitcast.80, f32[32,1024]{1,0:T(8,128)} %get-tuple-element.71.cos_ref, ...), custom_call_target="tpu_custom_call" | custom-call | tf_op jit(solution)/shard_map/attention_forward/pallas_call | solution.py:385
  91.4 4.6 %all-to-all-start.1 = ((bf16[8,192,128]{2,1,0:T(8,128)(2,1)}), bf16[8,192,128]{2,1,0:T(8,128)(2,1)S(1)}, u32[]{:S(2)}, u32[]{:S(2)}) async-start(bf16[8,192,128]{2,1,0:T(8,128)(2,1)} %get-tuple-element.34), calls=%async_computation.1 | async-start | bytes 786432 | tf_op jit(solution)/shard_map/all_to_all | solution.py:453
  96.2 1.3 convert_reduce_fusion.2
  98.2 1.6 broadcast_select_fusion.1
  99.9 1.1 copy.72
  101.2 1.4 pad_maximum_fusion
  102.5 2.4 all-to-all-done.1
  105.6 8.9 %mlp.1 = (bf16[8,192,128]{2,1,0:T(8,128)(2,1)}, f32[256,768]{1,0:T(8,128)}, f32[256,768]{1,0:T(8,128)}, bf16[256,768]{1,0:T(8,128)(2,1)}, bf16[256,1152]{1,0:T(8...) custom-call(bf16[2,128,768]{2,1,0:T(8,128)(2,1)} %tok_ref.1, bf16[2,768,128]{2,1,0:T(8,128)(2,1)} %bitcast.84, ...), custom_call_target="tpu_custom_call" | custom-call | tf_op jit(solution)/shard_map/mlp/pallas_call | solution.py:385
  114.6 8.2 %mlp_weights.1 = (bf16[2,128,768]{2,1,0:T(8,128)(2,1)}, bf16[8,8,32,768]{3,2,1,0:T(8,128)(2,1)}, bf16[8,8,32,768]{3,2,1,0:T(8,128)(2,1)}, f32[16,8,768]{2,1,0:T(8,128)}) custom-call(s32[1]{0:T(128)} %bitcast.core_ref, bf16[2,768,128]{2,1,0:T(8,128)(2,1)} %bitcast.85, bf16[2,128,768]{2,1,0:T(8,128)(2,1)} %cot_ref.3, bf16[1152,768]{1,0:T(8,128)(2,1)} %bitcast.76, ...), custom_call_target="tpu_custom_call" | custom-call | tf_op jit(solution)/shard_map/mlp_weights/pallas_call | solution.py:385
  123.5 5.5 %collective-permute-done.6 = bf16[8,8,32,768]{3,2,1,0:T(8,128)(2,1)S(1)} collective-permute-done((bf16[8,8,32,768]{3,2,1,0:T(8,128)(2,1)}, bf16[8,8,32,768]{3,2,1,0:T(8,128)(2,1)S(1)}, u32[]{:S(2)}, u32[]{:S(2)}) %collective-permute-start.6) | collective-permute-done | bytes 3145760 | tf_op jit(solution)/shard_map/ppermute | solution.py:63
  129.0 4.7 %add_convert_fusion = bf16[8,8,32,768]{3,2,1,0:T(8,128)(2,1)} fusion(bf16[8,8,32,768]{3,2,1,0:T(8,128)(2,1)S(1)} %collective-permute-done.6, bf16[8,8,32,768]{3,2,1,0:T(8,128)(2,1)} %get-tuple-element.54), kind=kLoop, calls=%fused_computation | loop fusion | flops 6291456 | bytes 9437184 | tf_op jit(solution)/shard_map/convert_element_type | solution.py:74
  133.7 1.0 copy-done.6
  134.7 15.4 %all_to_all.41.do_ref = bf16[8,192,128]{2,1,0:T(8,128)(2,1)} all-to-all(bf16[8,192,128]{2,1,0:T(8,128)(2,1)S(1)} %copy-done.6), channel_id=1, replica_groups=mesh['ctx'=8,'fsdp'=16] {'ctx'}, dimensions={0} | all-to-all | bytes 786432 | tf_op jit(solution)/shard_map/all_to_all | solution.py:526
  150.2 13.5 %attention_backward.1 = (bf16[576,1024]{1,0:T(8,128)(2,1)}, bf16[8,128,768]{2,1,0:T(8,128)(2,1)}, f32[1,768]{1,0:T(1,128)}) custom-call(bf16[8,192,128]{2,1,0:T(8,128)(2,1)} %all_to_all.41.do_ref, bf16[576,1024]{1,0:T(8,128)(2,1)} %get-tuple-element.43.qkv_ref, f32[8,1024]{1,0:T(8,128)} %get-tuple-element.44.lse_ref, f32[192,1024]{1,0:T(8,128)} %get-tuple-element.45.o_ref, ...), custom_call_target="tpu_custom_call" | custom-call | tf_op jit(solution)/shard_map/attention_backward/pallas_call | solution.py:385
  163.6 4.4 %qkv_weights.1 = (bf16[8,48,768]{2,1,0:T(8,128)(2,1)}, bf16[8,48,768]{2,1,0:T(8,128)(2,1)}) custom-call(s32[1]{0:T(128)} %bitcast.core_ref, bf16[1024,768]{1,0:T(8,128)(2,1)} %get-tuple-element.47.a_ref, bf16[576,1024]{1,0:T(8,128)(2,1)} %get-tuple-element.48.g_ref, f32[1,768]{1,0:T(1,128)} %get-tuple-element.49.gain_one_ref, ...), custom_call_target="tpu_custom_call" | custom-call | tf_op jit(solution)/shard_map/qkv_weights/pallas_call | solution.py:385
  168.0 0.9 collective-permute-start.5
  168.9 1.8 collective-permute-done.5
  170.8 1.2 add_convert_fusion.1
  172.0 15.2 %all_to_all.42 = bf16[8,48,768]{2,1,0:T(8,128)(2,1)S(1)} all-to-all(bf16[8,48,768]{2,1,0:T(8,128)(2,1)S(1)} %add_convert_fusion.1), channel_id=1, replica_groups={{0,2,4,6,8,10,12,14},{1,3,5,7,9,11,13,15},{16,18,20,22,24,26,28,30},{17..., dimensions={0} | all-to-all | bytes 1179648 | tf_op jit(solution)/shard_map/all_to_all | solution.py:69
  187.2 3.7 %all-to-all-start.4 = ((bf16[8,128,768]{2,1,0:T(8,128)(2,1)}), bf16[8,128,768]{2,1,0:T(8,128)(2,1)S(1)}, u32[]{:S(2)}, u32[]{:S(2)}) async-start(bf16[8,128,768]{2,1,0:T(8,128)(2,1)} %get-tuple-element.46), calls=%async_computation.4 | async-start | bytes 3145728 | tf_op jit(solution)/shard_map/all_to_all | solution.py:549
  191.3 20.9 %all-to-all-done.4 = bf16[8,128,768]{2,1,0:T(8,128)(2,1)S(1)} async-done(((bf16[8,128,768]{2,1,0:T(8,128)(2,1)}), bf16[8,128,768]{2,1,0:T(8,128)(2,1)S(1)}, u32[]{:S(2)}, u32[]{:S(2)}) %all-to-all-start.4) | async-done | bytes 1572896 | tf_op jit(solution)/shard_map/all_to_all | solution.py:549
  212.2 3.5 %all-to-all-start.6 = ((bf16[8,32,768]{2,1,0:T(8,128)(2,1)}), bf16[8,32,768]{2,1,0:T(8,128)(2,1)S(1)}, u32[]{:S(2)}, u32[]{:S(2)}) async-start(bf16[8,32,768]{2,1,0:T(8,128)(2,1)} %reduce-scatter.2.cloned.1.call-done), calls=%async_computation.7 | async-start | bytes 786432 | tf_op jit(solution)/shard_map/all_to_all | solution.py:69
  216.0 9.9 %all-to-all-done.6 = bf16[8,32,768]{2,1,0:T(8,128)(2,1)S(1)} async-done(((bf16[8,32,768]{2,1,0:T(8,128)(2,1)}), bf16[8,32,768]{2,1,0:T(8,128)(2,1)S(1)}, u32[]{:S(2)}, u32[]{:S(2)}) %all-to-all-start.6) | async-done | bytes 393248 | tf_op jit(solution)/shard_map/all_to_all | solution.py:69
  226.0 1.0 broadcast_in_dim.27
  227.1 4.6 %all-to-all-start.7 = ((bf16[8,80,768]{2,1,0:T(8,128)(2,1)}), bf16[8,80,768]{2,1,0:T(8,128)(2,1)}, u32[]{:S(2)}, u32[]{:S(2)}) async-start(bf16[8,80,768]{2,1,0:T(8,128)(2,1)} %broadcast_in_dim.27), calls=%async_computation.8 | async-start | bytes 1966080 | tf_op jit(solution)/shard_map/all_to_all | solution.py:23
  232.0 1.2 fusion.4
  233.2 13.7 %all-to-all-done.7 = bf16[8,80,768]{2,1,0:T(8,128)(2,1)} async-done(((bf16[8,80,768]{2,1,0:T(8,128)(2,1)}), bf16[8,80,768]{2,1,0:T(8,128)(2,1)}, u32[]{:S(2)}, u32[]{:S(2)}) %all-to-all-start.7) | async-done | bytes 983072 | tf_op jit(solution)/shard_map/all_to_all | solution.py:23
  246.9 1.2 slice_convert_fusion
  248.2 1.3 slice_convert_fusion.1
  252.7 1.1 reshape.382
  255.2 0.8 pad_maximum_fusion.2
  (77 shorter events, 13.3 us)
Async XLA Ops:
  7.2 8.8 %copy-start = (bf16[2,128,768]{2,1,0:T(8,128)(2,1)S(1)}, bf16[2,128,768]{2,1,0:T(8,128)(2,1)}, u32[]{:S(2)}) copy-start(bf16[2,128,768]{2,1,0:T(8,128)(2,1)} %tok_ref.1) | copy-start | bytes 1179652
  7.2 97.7 %all-gather.2.cloned.1.call-start = ((), (), s32[]{:S(2)}) async-start(), calls=%async_computation.9 | async-start | bytes 3760128 | tf_op jit(solution)/shard_map/all_gather | solution.py:428
  11.5 10.3 %collective-permute-start = (bf16[1,48,640]{2,1,0:T(8,128)(2,1)S(1)}, bf16[1,48,640]{2,1,0:T(8,128)(2,1)S(1)}, u32[]{:S(2)}, u32[]{:S(2)}) collective-permute-start(bf16[1,48,640]{2,1,0:T(8,128)(2,1)S(1)} %get-tuple-element.69), channel_id=1, source_target_pairs={{0,8},{1,9},{2,10},{3,11},{4,12},{5,13},{6,14},{7,15},{8,0},{9,1},... | collective-permute-start | bytes 184328 | tf_op jit(solution)/shard_map/ppermute | solution.py:40
  17.3 25.9 %all-to-all-start = ((bf16[8,128,768]{2,1,0:T(8,128)(2,1)}), bf16[8,128,768]{2,1,0:T(8,128)(2,1)S(1)}, u32[]{:S(2)}, u32[]{:S(2)}) async-start(bf16[8,128,768]{2,1,0:T(8,128)(2,1)} %bitcast.1), calls=%async_computation | async-start | bytes 3145728 | tf_op jit(solution)/shard_map/all_to_all | solution.py:426
  21.8 5.3 %collective-permute-start.1 = (bf16[2,48,640]{2,1,0:T(8,128)(2,1)S(1)}, bf16[2,48,640]{2,1,0:T(8,128)(2,1)S(1)}, u32[]{:S(2)}, u32[]{:S(2)}) collective-permute-start(bf16[2,48,640]{2,1,0:T(8,128)(2,1)S(1)} %maximum_select_fusion.4), channel_id=1, source_target_pairs={{0,4},{1,5},{2,6},{3,7},{4,0},{5,1},{6,2},{7,3},{8,12},{9,13},{10,... | collective-permute-start | bytes 368648 | tf_op jit(solution)/shard_map/ppermute | solution.py:40
  27.1 10.3 %copy-start.7 = (bf16[72,768]{1,0:T(8,128)(2,1)S(1)}, bf16[72,768]{1,0:T(8,128)(2,1)}, u32[]{:S(2)}) copy-start(bf16[72,768]{1,0:T(8,128)(2,1)} %param.18) | copy-start | bytes 331780
  27.1 10.3 %copy-start.8 = (bf16[48,768]{1,0:T(8,128)(2,1)S(1)}, bf16[48,768]{1,0:T(8,128)(2,1)}, u32[]{:S(2)}) copy-start(bf16[48,768]{1,0:T(8,128)(2,1)} %param.15) | copy-start | bytes 221188
  27.2 6.6 %collective-permute-start.2 = (bf16[4,48,640]{2,1,0:T(8,128)(2,1)S(1)}, bf16[4,48,640]{2,1,0:T(8,128)(2,1)S(1)}, u32[]{:S(2)}, u32[]{:S(2)}) collective-permute-start(bf16[4,48,640]{2,1,0:T(8,128)(2,1)S(1)} %bitcast.90), channel_id=1, source_target_pairs={{0,2},{1,3},{2,0},{3,1},{4,6},{5,7},{6,4},{7,5},{8,10},{9,11},{10,... | collective-permute-start | bytes 737288 | tf_op jit(solution)/shard_map/ppermute | solution.py:40
  33.9 5.0 %collective-permute-start.3 = (bf16[8,48,640]{2,1,0:T(8,128)(2,1)S(1)}, bf16[8,48,640]{2,1,0:T(8,128)(2,1)S(1)}, u32[]{:S(2)}, u32[]{:S(2)}) collective-permute-start(bf16[8,48,640]{2,1,0:T(8,128)(2,1)S(1)} %bitcast.88), channel_id=1, source_target_pairs={{0,1},{1,0},{2,3},{3,2},{4,5},{5,4},{6,7},{7,6},{8,9},{9,8},{10,11... | collective-permute-start | bytes 1474568 | tf_op jit(solution)/shard_map/ppermute | solution.py:40
  43.2 27.8 %copy-start.2 = (bf16[8,128,768]{2,1,0:T(8,128)(2,1)}, bf16[8,128,768]{2,1,0:T(8,128)(2,1)S(1)}, u32[]{:S(2)}) copy-start(bf16[8,128,768]{2,1,0:T(8,128)(2,1)S(1)} %all-to-all-done) | copy-start | bytes 4718596
  43.3 30.3 %copy-start.9 = (s32[2]{0:T(128)S(1)}, s32[2]{0:T(128)}, u32[]{:S(2)}) copy-start(s32[2]{0:T(128)} %param.11) | copy-start | bytes 28
  43.3 30.9 %copy-start.10 = (s32[8]{0:T(128)S(1)}, s32[8]{0:T(128)}, u32[]{:S(2)}) copy-start(s32[8]{0:T(128)} %param.12) | copy-start | bytes 100
  71.0 27.2 %collective-permute-start.4 = (bf16[8,120,768]{2,1,0:T(8,128)(2,1)S(1)}, bf16[8,120,768]{2,1,0:T(8,128)(2,1)}, u32[]{:S(2)}, u32[]{:S(2)}) collective-permute-start(bf16[8,120,768]{2,1,0:T(8,128)(2,1)S(1)} %all_to_all.40), channel_id=1, source_target_pairs={{0,1},{1,0},{2,3},{3,2},{4,5},{5,4},{6,7},{7,6},{8,9},{9,8},{10,11... | collective-permute-start | bytes 4423688 | tf_op jit(solution)/shard_map/ppermute | solution.py:57
  91.4 13.5 %all-to-all-start.1 = ((bf16[8,192,128]{2,1,0:T(8,128)(2,1)}), bf16[8,192,128]{2,1,0:T(8,128)(2,1)S(1)}, u32[]{:S(2)}, u32[]{:S(2)}) async-start(bf16[8,192,128]{2,1,0:T(8,128)(2,1)} %get-tuple-element.34), calls=%async_computation.1 | async-start | bytes 786432 | tf_op jit(solution)/shard_map/all_to_all | solution.py:453
  96.0 95.3 %reduce-scatter.2.cloned.1.call-start = ((), (), s32[]{:S(2)}) async-start(), calls=%async_computation.10 | async-start | bytes 3538944 | tf_op jit(solution)/shard_map/reduce_scatter | solution.py:521
  104.9 0.7 copy-start.4
  122.8 6.3 %collective-permute-start.6 = (bf16[8,8,32,768]{3,2,1,0:T(8,128)(2,1)}, bf16[8,8,32,768]{3,2,1,0:T(8,128)(2,1)S(1)}, u32[]{:S(2)}, u32[]{:S(2)}) collective-permute-start(bf16[8,8,32,768]{3,2,1,0:T(8,128)(2,1)} %get-tuple-element.55), channel_id=1, source_target_pairs={{0,1},{1,0},{2,3},{3,2},{4,5},{5,4},{6,7},{7,6},{8,9},{9,8},{10,11... | collective-permute-start | bytes 9437192 | tf_op jit(solution)/shard_map/ppermute | solution.py:63
  133.7 1.0 copy-start.6
  168.0 2.7 %collective-permute-start.5 = (bf16[8,48,768]{2,1,0:T(8,128)(2,1)}, bf16[8,48,768]{2,1,0:T(8,128)(2,1)S(1)}, u32[]{:S(2)}, u32[]{:S(2)}) collective-permute-start(bf16[8,48,768]{2,1,0:T(8,128)(2,1)} %get-tuple-element.53), channel_id=1, source_target_pairs={{0,1},{1,0},{2,3},{3,2},{4,5},{5,4},{6,7},{7,6},{8,9},{9,8},{10,11... | collective-permute-start | bytes 1769480 | tf_op jit(solution)/shard_map/ppermute | solution.py:63
  187.2 3.7 %copy-start.1 = (bf16[2,128,768]{2,1,0:T(8,128)(2,1)S(1)}, bf16[2,128,768]{2,1,0:T(8,128)(2,1)}, u32[]{:S(2)}) copy-start(bf16[2,128,768]{2,1,0:T(8,128)(2,1)} %tok_ref.1) | copy-start | bytes 1179652
  187.2 25.1 %all-to-all-start.4 = ((bf16[8,128,768]{2,1,0:T(8,128)(2,1)}), bf16[8,128,768]{2,1,0:T(8,128)(2,1)S(1)}, u32[]{:S(2)}, u32[]{:S(2)}) async-start(bf16[8,128,768]{2,1,0:T(8,128)(2,1)} %get-tuple-element.46), calls=%async_computation.4 | async-start | bytes 3145728 | tf_op jit(solution)/shard_map/all_to_all | solution.py:549
  212.2 13.7 %all-to-all-start.6 = ((bf16[8,32,768]{2,1,0:T(8,128)(2,1)}), bf16[8,32,768]{2,1,0:T(8,128)(2,1)S(1)}, u32[]{:S(2)}, u32[]{:S(2)}) async-start(bf16[8,32,768]{2,1,0:T(8,128)(2,1)} %reduce-scatter.2.cloned.1.call-done), calls=%async_computation.7 | async-start | bytes 786432 | tf_op jit(solution)/shard_map/all_to_all | solution.py:69
  227.1 4.9 %copy-start.5 = (f32[256,768]{1,0:T(8,128)S(1)}, f32[256,768]{1,0:T(8,128)}, u32[]{:S(2)}) copy-start(f32[256,768]{1,0:T(8,128)} %get-tuple-element.36.gm_ref) | copy-start | bytes 2359300
  227.1 19.8 %all-to-all-start.7 = ((bf16[8,80,768]{2,1,0:T(8,128)(2,1)}), bf16[8,80,768]{2,1,0:T(8,128)(2,1)}, u32[]{:S(2)}, u32[]{:S(2)}) async-start(bf16[8,80,768]{2,1,0:T(8,128)(2,1)} %broadcast_in_dim.27), calls=%async_computation.8 | async-start | bytes 1966080 | tf_op jit(solution)/shard_map/all_to_all | solution.py:23
  248.0 1.5 copy-start.3
  249.6 1.3 slice-start
Sparse Core Ops, SparseCore 0:
  10.4 77.0 all-gather.1
  133.9 42.9 reduce-scatter.1

commit v4 on v3

--- a/solution.py
+++ b/solution.py
@@ -56,12 +56,14 @@
     )
     other = lax.ppermute(mine, axis, core_pairs(n))
     even = lax.axis_index(axis) % 2 == 0
-    return jnp.where(even, mine, other), jnp.where(even, other, mine)
-
-
-def core_sum(kept, away, axis):
+    return mine, (jnp.where(even, mine, other), jnp.where(even, other, mine))
+
+
+def core_sum(kept, away, axis, micros, after=(), name=None):
     came = lax.ppermute(away, axis, core_pairs(lax.axis_size(axis)))
-    return low(kept.astype(jnp.float32) + came.astype(jnp.float32))
+    return on_device(
+        sum_kernel, [(kept.shape, jnp.bfloat16)], (kept, came), micros, after=after, name=name
+    )[0]
 
 
 def spread_sum(parts, axis):
@@ -111,7 +113,19 @@
 
 
 def forward_kernel(
-    seq_ref, w_ref, cos_ref, sin_ref, bias_ref, keep_ref, out_ref, a_ref, qkv_ref, lse_ref, o_ref
+    seq_ref,
+    w_ref,
+    cos_ref,
+    sin_ref,
+    bias_ref,
+    keep_ref,
+    out_ref,
+    a_ref,
+    qkv_ref,
+    lse_ref,
+    o_ref,
+    mean_ref,
+    inverse_ref,
 ):
     full_len, width = seq_ref.shape
     span = o_ref.shape[0]
@@ -123,9 +137,12 @@
     for start in range(0, full_len, ROWS):
         rows = slice(start, start + ROWS)
         x = seq_ref[rows].astype(jnp.float32)
-        centre = x - jnp.mean(x, -1, keepdims=True)
-        variance = jnp.mean(centre * centre, -1, keepdims=True)
-        a_low = (centre * lax.rsqrt(variance + EPS) * gain).astype(jnp.bfloat16)
+        mean = jnp.mean(x, -1, keepdims=True)
+        centre = x - mean
+        inverse = lax.rsqrt(jnp.mean(centre * centre, -1, keepdims=True) + EPS)
+        mean_ref[rows] = mean
+        inverse_ref[rows] = inverse
+        a_low = (centre * inverse * gain).astype(jnp.bfloat16)
         a_ref[rows] = a_low
         joined = product(w_turned, a_low, NT)
         cosine = cos_ref[:, rows]
@@ -172,6 +189,8 @@
     bias_ref,
     keep_ref,
     seq_ref,
+    mean_ref,
+    inverse_ref,
     w_ref,
     g_ref,
     ga_ref,
@@ -230,10 +249,8 @@
     for start in range(0, full_len, ROWS):
         rows = slice(start, start + ROWS)
         grad_a = product(g_ref[:, rows].T, w_ref[:, : 3 * span], NT)
-        x = seq_ref[rows].astype(jnp.float32)
-        centre = x - jnp.mean(x, -1, keepdims=True)
-        variance = jnp.mean(centre * centre, -1, keepdims=True)
-        summed = jnp.sum(grad_a * (centre * lax.rsqrt(variance + EPS)), 0, keepdims=True)
+        normed = (seq_ref[rows].astype(jnp.float32) - mean_ref[rows]) * inverse_ref[rows]
+        summed = jnp.sum(grad_a * normed, 0, keepdims=True)
         gain_ref[...] = summed if start == 0 else gain_ref[...] + summed
         for first in range(0, ROWS, blk):
             ga_ref[(start + first) // blk] = grad_a[first : first + blk].astype(jnp.bfloat16)
@@ -300,57 +317,94 @@
             ]
 
 
-def mlp_weights_kernel(
+def half_weights(which, att_ref, cot_ref, gm_ref, b_ref, hid_ref, gg_ref, part_ref, extra_ref, turned, tall):
+    seqs, width, local_len = att_ref.shape
+    ctx, pairs, chunk, _ = part_ref.shape
+    count = gg_ref.shape[1] // width
+    depth = width // (2 * pairs)
+    down_rows = hid_ref.shape[1] // (2 * pairs)
+    split = ctx * chunk - (count + 1) * depth
+    cot = jnp.concatenate([cot_ref[k] for k in range(seqs)], 0)
+    turned[:width] = b_ref[...].astype(jnp.float32).T
+    turned[width : 2 * width] = jnp.concatenate(
+        [att_ref[k] for k in range(seqs)], 1
+    ).astype(jnp.float32)
+    turned[2 * width :] = hid_ref[...].astype(jnp.float32).T
+
+    def chosen(first, height):
+        return jnp.concatenate(
+            [
+                turned[pl.ds(pl.multiple_of(first + (2 * k + which) * height, 8), height)]
+                for k in range(pairs)
+            ],
+            0,
+        ).astype(jnp.bfloat16)
+
+    grad_up = product(chosen(width, depth), gm_ref[...].astype(jnp.bfloat16))
+    tall[...] = product(chosen(2 * width, down_rows), cot)
+    grad_in = product(chosen(0, depth), gg_ref[...])
+    for pair in range(pairs):
+        wide = slice(pair * depth, (pair + 1) * depth)
+        rows = jnp.concatenate(
+            [grad_in[wide, k * width : (k + 1) * width] for k in range(count)]
+            + [grad_up[wide], tall[pair * down_rows : pair * down_rows + split]],
+            0,
+        ).astype(jnp.bfloat16)
+        for part in range(ctx):
+            part_ref[part, pair] = rows[part * chunk : (part + 1) * chunk]
+        extra_ref[pair] = tall[pair * down_rows + split : (pair + 1) * down_rows]
+
+
+def sent_weights_kernel(core_ref, *refs):
+    half_weights(1 - core_ref[0], *refs)
+
+
+def kept_weights_kernel(
     core_ref,
     att_ref,
     cot_ref,
-    wdown_ref,
     gm_ref,
-    mixed_ref,
     b_ref,
     hid_ref,
     gg_ref,
+    wdown_ref,
+    mixed_ref,
+    part_ref,
+    extra_ref,
     out_ref,
+    turned,
+    tall,
+):
+    half_weights(
+        core_ref[0],
+        att_ref,
+        cot_ref,
+        gm_ref,
+        b_ref,
+        hid_ref,
+        gg_ref,
+        part_ref,
+        extra_ref,
+        turned,
+        tall,
+    )
+    local_len = out_ref.shape[1]
+    result = mixed_ref[...] + product(hid_ref[...], wdown_ref[...])
+    for seq in range(out_ref.shape[0]):
+        out_ref[seq] = result[seq * local_len : (seq + 1) * local_len].astype(jnp.bfloat16)
+
+
+def qkv_weights_kernel(
+    core_ref,
+    a_ref,
+    g_ref,
+    gain_one_ref,
+    gain_two_ref,
+    kept_extra_ref,
+    away_extra_ref,
     kept_ref,
     away_ref,
-    extra_ref,
-    in_ref,
-    up_ref,
-    down_ref,
-):
-    seqs, _, local_len = att_ref.shape
-    width = cot_ref.shape[2]
-    ctx, pairs, chunk, _ = kept_ref.shape
-    depth = in_ref.shape[0] // (2 * pairs)
-    down_rows = down_ref.shape[0] // (2 * pairs)
-    count = in_ref.shape[1] // width
-    split = ctx * chunk - (count + 1) * depth
-    cot = jnp.concatenate([cot_ref[k] for k in range(seqs)], 0)
-    att = jnp.concatenate([att_ref[k] for k in range(seqs)], 1)
-    in_ref[...] = product(b_ref[...].T, gg_ref[...])
-    up_ref[...] = product(att, gm_ref[...].astype(jnp.bfloat16))
-    down_ref[...] = product(hid_ref[...].T, cot)
-    core = core_ref[0]
-    for pair in range(pairs):
-        for ref, which in ((kept_ref, core), (away_ref, 1 - core)):
-            wide = pl.ds(pl.multiple_of((2 * pair + which) * depth, 8), depth)
-            tall = pl.ds(pl.multiple_of((2 * pair + which) * down_rows, 8), split)
-            rows = jnp.concatenate(
-                [in_ref[wide, k * width : (k + 1) * width] for k in range(count)]
-                + [up_ref[wide], down_ref[tall]],
-                0,
-            ).astype(jnp.bfloat16)
-            for part in range(ctx):
-                ref[part, pair] = rows[part * chunk : (part + 1) * chunk]
-    for owner in range(2 * pairs):
-        extra_ref[owner] = down_ref[owner * down_rows + split : (owner + 1) * down_rows]
-    result = mixed_ref[...] + product(hid_ref[...], wdown_ref[...])
-    for seq in range(seqs):
-        out_ref[seq] = result[seq * local_len : (seq + 1) * local_len].astype(jnp.bfloat16)
-
-
-def qkv_weights_kernel(
-    core_ref, a_ref, g_ref, gain_one_ref, gain_two_ref, extra_ref, kept_ref, away_ref, w_ref
+    w_ref,
 ):
     pairs, depth, width = kept_ref.shape
     span3 = g_ref.shape[0]
@@ -366,31 +420,117 @@
         ],
         0,
     ).T
-    w_ref[:, span3:used] = gains[:, span3 - lane :]
-    for owner in range(2 * pairs):
-        extra = extra_ref[owner]
-        w_ref[owner * depth : (owner + 1) * depth, used:] = jnp.concatenate(
-            [extra[:, k * 128 : (k + 1) * 128] for k in range(width // 128)], 0
-        )
+    w_ref[:, span3:] = gains[:, span3 - lane :]
     core = core_ref[0]
     for pair in range(pairs):
-        for ref, which in ((kept_ref, core), (away_ref, 1 - core)):
+        for ref, extra_ref, which in (
+            (kept_ref, kept_extra_ref, core),
+            (away_ref, away_extra_ref, 1 - core),
+        ):
             rows = pl.ds(pl.multiple_of((2 * pair + which) * depth, 8), depth)
-            ref[pair] = w_ref[rows].astype(jnp.bfloat16)
-
-
-def on_device(kernel, outs, args, scratch=(), scalars=0, name=None):
+            extra = extra_ref[pair]
+            ref[pair] = jnp.concatenate(
+                [
+                    w_ref[rows],
+                    jnp.concatenate(
+                        [extra[:, k * 128 : (k + 1) * 128] for k in range(width // 128)], 0
+                    ),
+                ],
+                1,
+            ).astype(jnp.bfloat16)
+
+
+def first_kernel(group_ref, w_ref, gains_ref, out_ref):
+    depth, used = out_ref.shape
+    spread = 4
+    span = w_ref.shape[1] // (3 * spread)
+    own_group = group_ref[0]
+    gains = gains_ref[...]
+
+    for which in range(spread):
+
+        @pl.when(own_group == which)
+        def _():
+            picked = [
+                w_ref[
+                    :, (k * spread + which) * span : (k * spread + which + 1) * span
+                ].astype(jnp.float32)
+                for k in range(3)
+            ]
+            out_ref[...] = jnp.concatenate([*picked, gains], 1).astype(jnp.bfloat16)
+
+
+def finish_kernel(
+    ends_ref, gain_one_ref, qkv_ref, wout_ref, gain_two_ref, win_ref, wdown_ref
+):
+    ctx, _, width = ends_ref.shape
+    depth = qkv_ref.shape[0]
+    down_rows = wdown_ref.shape[0]
+    count = win_ref.shape[1] // width
+    spread = ctx // 2
+    span = width // spread
+    f32 = jnp.float32
+    last = [ends_ref[k, :depth].astype(f32) for k in range(ctx)]
+    for group in range(spread):
+        both = last[group] + last[group + spread]
+        for part in range(3):
+            qkv_ref[:, part * width + group * span : part * width + (group + 1) * span] = both[
+                :, part * span : (part + 1) * span
+            ]
+    total = last[0]
+    for k in range(1, ctx):
+        total = total + last[k]
+    lane = 3 * span // 128 * 128
+    gains = total[:, lane : lane + 128].T
+    gain_one_ref[...] = gains[3 * span - lane : 3 * span - lane + 1]
+    gain_two_ref[...] = gains[3 * span - lane + 1 : 3 * span - lane + 2]
+    main = jnp.concatenate([ends_ref[k, depth:].astype(f32) for k in range(ctx)], 0)
+    for k in range(count):
+        win_ref[:, k * width : (k + 1) * width] = main[k * depth : (k + 1) * depth]
+    wout_ref[...] = main[count * depth : (count + 1) * depth]
+    split = main.shape[0] - (count + 1) * depth
+    extra = down_rows - split
+    wdown_ref[:split] = main[(count + 1) * depth :]
+    wdown_ref[split:] = jnp.concatenate(
+        [total[k * extra : (k + 1) * extra, width - 128 :] for k in range(width // 128)], 1
+    )
+
+
+def on_device(kernel, outs, args, micros, scratch=(), scalars=0, after=(), name=None):
     space = pl.BlockSpec(memory_space=pltpu.VMEM)
     scalar = pl.BlockSpec(memory_space=pltpu.SMEM)
+    given = len(args)
+
+    def ordered(*refs):
+        kernel(*refs[:given], *refs[given + len(after) :])
+
     return pl.pallas_call(
-        kernel,
+        ordered,
         out_shape=[jax.ShapeDtypeStruct(shape, dtype) for shape, dtype in outs],
-        in_specs=[scalar] * scalars + [space] * (len(args) - scalars),
+        in_specs=[scalar] * scalars
+        + [space] * (given - scalars)
+        + [pl.BlockSpec(memory_space=pl.ANY)] * len(after),
         out_specs=[space] * len(outs),
         scratch_shapes=list(scratch),
         compiler_params=pltpu.CompilerParams(vmem_limit_bytes=56 * 1024 * 1024),
+        cost_estimate=pl.CostEstimate(
+            flops=int(micros * 2e10), bytes_accessed=int(micros * 4e7), transcendentals=0
+        ),
         name=name,
-    )(*args)
+    )(*args, *after)
+
+
+def sum_kernel(left_ref, right_ref, out_ref):
+    for k in range(out_ref.shape[0]):
+        out_ref[k] = (left_ref[k].astype(jnp.float32) + right_ref[k].astype(jnp.float32)).astype(
+            jnp.bfloat16
+        )
+
+
+def spread_kernel(tokens_ref, out_ref):
+    copies = out_ref.shape[0] // tokens_ref.shape[0]
+    for k in range(out_ref.shape[0]):
+        out_ref[k] = tokens_ref[k // copies]
 
 
 def body(tokens, lengths, deal, gain_attn, w_qkv, w_out, gain_mlp, w_in, w_down, cotangent):
@@ -415,22 +555,30 @@
     length = lax.dynamic_slice_in_dim(lengths, own_seq, 1)[0]
     all_keep = all_pos < length
 
-    qkv_own = lax.dynamic_index_in_dim(
-        w_qkv.reshape(depth, 3, spread, span), own_group, 2, keepdims=False
-    ).reshape(depth, 3 * span)
-    gains_wide = jnp.stack([gain_attn, gain_mlp], 1)
-    fill = jnp.zeros((depth, 640 - 3 * span - 2), jnp.bfloat16)
-    first_all = gather_doubling(
-        jnp.concatenate([qkv_own, gains_wide, fill], 1), "fsdp"
-    ).reshape(fsdp * depth, 640)
-    sequence = lax.all_to_all(jnp.repeat(tokens, spread, axis=0), "ctx", 0, 0, tiled=True)
-
+    used = 3 * span + 64
+    gains_wide = jnp.pad(
+        jnp.stack([gain_attn, gain_mlp], 1).astype(f32), ((0, 0), (0, used - 3 * span - 2))
+    )
+    first = on_device(
+        first_kernel,
+        [((depth, used), jnp.bfloat16)],
+        (own_group.astype(jnp.int32)[None], w_qkv, gains_wide),
+        1,
+        scalars=1,
+        name="first_pack",
+    )[0]
+    first_all = gather_doubling(first, "fsdp").reshape(fsdp * depth, used)
     win_all = lax.all_gather(w_in, "fsdp", axis=0, tiled=True)
-    stacked, sequence, first_all = lax.optimization_barrier(
-        (jnp.concatenate([w_out, w_down], 0), sequence, first_all)
-    )
-    stacked_all = gather_two_level(stacked, "fsdp")
-
+    stacked_mine, stacked_all = gather_two_level(jnp.concatenate([w_out, w_down], 0), "fsdp")
+    to_send = on_device(
+        spread_kernel,
+        [((ctx, local_len, width), jnp.bfloat16)],
+        (tokens,),
+        1,
+        after=(stacked_mine,),
+        name="spread_tokens",
+    )[0]
+    sequence = lax.all_to_all(to_send, "ctx", 0, 0, tiled=True)
     gain_one = first_all[:, 3 * span]
     gain_two = first_all[:, 3 * span + 1]
 
@@ -438,7 +586,7 @@
     bias = jnp.where(all_keep, 0.0, NEGATIVE).astype(f32)[:, None]
     keep_row = all_keep.astype(f32)[None, :]
     sequence = sequence.reshape(full_len, width)
-    attended, a_low, qkv, log_total, unrounded = on_device(
+    attended, a_low, qkv, log_total, unrounded, mean, inverse = on_device(
         forward_kernel,
         [
             ((ctx, span, local_len), jnp.bfloat16),
@@ -446,8 +594,11 @@
             ((3 * span, full_len), jnp.bfloat16),
             ((8, full_len), f32),
             ((span, full_len), f32),
+            ((full_len, 1), f32),
+            ((full_len, 1), f32),
         ],
         (sequence, first_all, cosine, sine, bias, keep_row),
+        12,
         name="attention_forward",
     )
     att_back = lax.all_to_all(attended, "ctx", 0, 0, tiled=True)
@@ -488,40 +639,41 @@
             win_all,
             wdown_all,
         ),
+        9,
         name="mlp",
     )
-    output, main_kept, main_away, down_extra = on_device(
-        mlp_weights_kernel,
-        [
-            (tokens.shape, jnp.bfloat16),
-            ((ctx, pairs, chunk, width), jnp.bfloat16),
-            ((ctx, pairs, chunk, width), jnp.bfloat16),
-            ((fsdp, extra, width), f32),
-        ],
-        (
-            core,
-            att_turned,
-            cotangent,
-            wdown_all,
-            grad_mixed,
-            mixed,
-            b_low,
-            hid_low,
-            grad_gate_up,
-        ),
-        [
-            pltpu.VMEM((fsdp * depth, 2 * hidden), f32),
-            pltpu.VMEM((width, width), f32),
-            pltpu.VMEM((hidden, width), f32),
-        ],
+    weights_in = (core, att_turned, cotangent, grad_mixed, b_low, hid_low, grad_gate_up)
+    half_outs = [
+        ((ctx, pairs, chunk, width), jnp.bfloat16),
+        ((pairs, extra, width), f32),
+    ]
+    half_scratch = [
+        pltpu.VMEM((2 * width + hidden, rows), f32),
+        pltpu.VMEM((hidden // 2, width), f32),
+    ]
+    main_away, away_extra = on_device(
+        sent_weights_kernel,
+        half_outs,
+        weights_in,
+        5,
+        half_scratch,
         scalars=1,
-        name="mlp_weights",
-    )
-    main_pair = core_sum(main_kept, main_away, "fsdp")
+        name="sent_weights",
+    )
+    main_kept, kept_extra, output = on_device(
+        kept_weights_kernel,
+        [*half_outs, (tokens.shape, jnp.bfloat16)],
+        (*weights_in, wdown_all, mixed),
+        0.05,
+        half_scratch,
+        scalars=1,
+        after=(main_away,),
+        name="kept_weights",
+    )
+    main_pair = core_sum(main_kept, main_away, "fsdp", 0.02, name="sum_cores")
     main_part = lax.psum_scatter(
         main_pair.reshape(-1, chunk, width), "ctx", scatter_dimension=0, tiled=True
     )
-    main_part = lax.optimization_barrier(main_part)
 
     all_grad = lax.all_to_all(grad_heads, "ctx", 0, 0, tiled=True)
     grad_qkv, grad_a_part, grad_gain_one = on_device(
@@ -541,21 +693,28 @@
             bias,
             keep_row,
             sequence,
+            mean,
+            inverse,
             first_all,
         ),
+        12,
         [pltpu.VMEM((HD, full_len), f32)] * 2,
+        after=(main_pair,),
         name="attention_backward",
     )
     grad_a_parts = lax.all_to_all(grad_a_part, "ctx", 0, 0, tiled=True)
     last_kept, last_away = on_device(
         qkv_weights_kernel,
         [((pairs, depth, width), jnp.bfloat16)] * 2,
-        (core, a_low, grad_qkv, grad_gain_one, grad_gain_two, down_extra),
-        [pltpu.VMEM((width, width), f32)],
+        (core, a_low, grad_qkv, grad_gain_one, grad_gain_two, kept_extra, away_extra),
+        0.1,
+        [pltpu.VMEM((width, used), f32)],
         scalars=1,
         name="qkv_weights",
     )
-    last = core_sum(last_kept, last_away, "fsdp")
+    last = core_sum(
+        last_kept, last_away, "fsdp", 0.05, after=(grad_a_parts,), name="sum_cores_last"
+    )
     grad_a = jnp.sum(
         grad_a_parts.reshape(seqs, spread, local_len, width).astype(f32), 1
     ).reshape(rows, width)
@@ -567,25 +726,29 @@
     main_part = spread_sum(main_part, "fsdp")
     share = jnp.concatenate([last, main_part], 0)
     ends = gather_by_exchange(share, "ctx", ctx)
-    last_all = ends[:, :depth].astype(f32)
-    down_end = jnp.sum(last_all[:, :, width - 128 :], 0)
-    down_end = down_end.reshape(-1, extra, 128).transpose(1, 0, 2).reshape(extra, width)
-    summed = ends[:, depth:].reshape(main_rows, width).astype(f32)
-    grad_wqkv_out = (
-        jnp.sum(last_all[:, :, : 3 * span].reshape(seqs, spread, depth, 3, span), 0)
-        .transpose(1, 2, 0, 3)
-        .reshape(depth, 3 * width)
-    )
-    gains_out = jnp.sum(last_all[:, :, 3 * span : 3 * span + 2], 0)
+    finished = on_device(
+        finish_kernel,
+        [
+            ((1, depth), f32),
+            (w_qkv.shape, f32),
+            (w_out.shape, f32),
+            ((1, depth), f32),
+            (w_in.shape, f32),
+            (w_down.shape, f32),
+        ],
+        (ends,),
+        3,
+        name="finish",
+    )
     return (
         output,
         grad_input.reshape(tokens.shape),
-        gains_out[:, 0],
-        grad_wqkv_out,
-        summed[count * depth : (count + 1) * depth],
-        gains_out[:, 1],
-        jnp.concatenate([summed[k * depth : (k + 1) * depth] for k in range(count)], 1),
-        jnp.concatenate([summed[(count + 1) * depth :], down_end], 0),
+        finished[0].reshape(depth),
+        finished[1],
+        finished[2],
+        finished[3].reshape(depth),
+        finished[4],
+        finished[5],
     )
 
 

time: 267 us -> 259 us (0.970)
  blocking collectives: 58.2 us -> 0 us
  waiting for transfers between devices: 65.9 us -> 93.5 us
  starting transfers between devices: 38.9 us -> 57.9 us
  Pallas kernels: 47.8 us -> 64.5 us
  other arithmetic: 21.2 us -> 13.5 us
    all_to_all x3 -> x0, blocking collectives: 58.2 us -> none  [the longest x1 27.6 us: gather_two_level(): lax.all_to_all(jnp.broadcast_to(part[None], (n // 2, *part.shape)), axis,...]
    pallas_call x5 -> x11, Pallas kernels: 47.8 us -> 64.5 us  [on_device(): pl.pallas_call(ordered, out_shape=[jax.ShapeDtypeStruct(shape, dtype) for...]
    all_to_all x1 -> x3, waiting for transfers between devices: 3.06 us -> 15.5 us  [the longest x1 15.5 us: body(): sequence = lax.all_to_all(to_send, 'ctx', 0, 0, tiled=True)]
    all_to_all x1 -> x3, starting transfers between devices: 4.47 us -> 16.6 us  [the longest x1 8.46 us: gather_two_level(): lax.all_to_all(jnp.broadcast_to(part[None], (n // 2, *part.shape)), axis,...]
    all_to_all x1 -> x2, waiting for transfers between devices: 9.91 us -> 22 us  [spread_sum(): lax.all_to_all(parts, axis, 0, 0, tiled=True, axis_index_groups=groups)]
    convert_element_type x4 -> x0, other arithmetic: 8.39 us -> none  [the longest x2 5.9 us: low(): return values.astype(jnp.bfloat16)]
    all_to_all x1 -> x2, starting transfers between devices: 3.45 us -> 9.2 us  [spread_sum(): lax.all_to_all(parts, axis, 0, 0, tiled=True, axis_index_groups=groups)]
    ppermute x2, waiting for transfers between devices: 7.34 us -> 1.84 us  [core_sum(): came = lax.ppermute(away, axis, core_pairs(lax.axis_size(axis)))]
  transfers between devices with their start and end apart: 14 -> 17, of which waited for: 10 -> 9; matrix products, arithmetic and copies ran while one was open for 8% -> 6% of each run, Pallas kernels for 12% -> 19%
where the time goes in v4:
time: 259 us; the launch traced here: 258 us
  waiting for transfers between devices  93.5 us (36%)
  Pallas kernels  64.5 us (25%)
  starting transfers between devices  57.9 us (22%)
  between operations  14.3 us (6%)
  local copies, waits for them, and re-layouts  13.9 us (5%)
  other arithmetic  13.5 us (5%)
    pallas_call x11, Pallas kernels, on_device(): pl.pallas_call(ordered, out_shape=[jax.ShapeDtypeStruct(shape, dtype) for...  64.5 us
    all_to_all x1, waiting for transfers between devices, body(): grad_a_parts = lax.all_to_all(grad_a_part, 'ctx', 0, 0, tiled=True)  24.5 us
    all_to_all x2, waiting for transfers between devices, spread_sum(): lax.all_to_all(parts, axis, 0, 0, tiled=True, axis_index_groups=groups)  22 us
    all_to_all x1, waiting for transfers between devices, body(): sequence = lax.all_to_all(to_send, 'ctx', 0, 0, tiled=True)  15.5 us
    ppermute x4, starting transfers between devices, gather_doubling(): came = lax.ppermute(held, axis, [(k, k ^ bit) for k in range(n)])  15.4 us
    all_to_all x1, waiting for transfers between devices, gather_by_exchange(): lax.all_to_all(jnp.broadcast_to(part[None], (n, *part.shape)), axis, 0, 0)  13.6 us
    ppermute x4, waiting for transfers between devices, gather_doubling(): came = lax.ppermute(held, axis, [(k, k ^ bit) for k in range(n)])  12.5 us
    all_to_all x2, starting transfers between devices, spread_sum(): lax.all_to_all(parts, axis, 0, 0, tiled=True, axis_index_groups=groups)  9.2 us
  transfers between devices with their start and end apart: 17, of which 9 were waited for; matrix products, arithmetic and copies ran while one was open for 6% of the time, Pallas kernels for 19%

profile of v4, /device:TPU:1, one launch (start us, length us, event | category | flops | bytes accessed | tf_op | source)
XLA Modules:
  0.0 257.7 jit_solution(1543417525802462470)
XLA Ops:
  7.2 1.0 pad_maximum_fusion.2
  8.1 1.2 broadcast_in_dim.19
  9.3 8.5 %all-to-all-start = ((bf16[8,120,768]{2,1,0:T(8,128)(2,1)}), bf16[8,120,768]{2,1,0:T(8,128)(2,1)}, u32[]{:S(2)}, u32[]{:S(2)}) async-start(bf16[8,120,768]{2,1,0:T(8,128)(2,1)} %broadcast_in_dim.19), calls=%async_computation | async-start | bytes 2949120 | tf_op jit(solution)/shard_map/all_to_all | solution.py:50
  18.6 1.7 first_pack.1
  20.3 2.9 %collective-permute-start = (bf16[1,48,640]{2,1,0:T(8,128)(2,1)}, bf16[1,48,640]{2,1,0:T(8,128)(2,1)S(1)}, u32[]{:S(2)}, u32[]{:S(2)}) collective-permute-start(bf16[1,48,640]{2,1,0:T(8,128)(2,1)} %bitcast.84), channel_id=1, source_target_pairs={{0,8},{1,9},{2,10},{3,11},{4,12},{5,13},{6,14},{7,15},{8,0},{9,1},... | collective-permute-start | bytes 184328 | tf_op jit(solution)/shard_map/ppermute | solution.py:40
  23.2 9.0 %collective-permute-done = bf16[1,48,640]{2,1,0:T(8,128)(2,1)S(1)} collective-permute-done((bf16[1,48,640]{2,1,0:T(8,128)(2,1)}, bf16[1,48,640]{2,1,0:T(8,128)(2,1)S(1)}, u32[]{:S(2)}, u32[]{:S(2)}) %collective-permute-start) | collective-permute-done | bytes 61472 | tf_op jit(solution)/shard_map/ppermute | solution.py:40
  32.2 0.9 maximum_select_fusion.4
  33.2 10.9 %collective-permute-start.1 = (bf16[2,48,640]{2,1,0:T(8,128)(2,1)S(1)}, bf16[2,48,640]{2,1,0:T(8,128)(2,1)S(1)}, u32[]{:S(2)}, u32[]{:S(2)}) collective-permute-start(bf16[2,48,640]{2,1,0:T(8,128)(2,1)S(1)} %maximum_select_fusion.4), channel_id=1, source_target_pairs={{0,4},{1,5},{2,6},{3,7},{4,0},{5,1},{6,2},{7,3},{8,12},{9,13},{10,... | collective-permute-start | bytes 368648 | tf_op jit(solution)/shard_map/ppermute | solution.py:40
  45.6 3.6 %collective-permute-done.1 = bf16[2,48,640]{2,1,0:T(8,128)(2,1)S(1)} collective-permute-done((bf16[2,48,640]{2,1,0:T(8,128)(2,1)S(1)}, bf16[2,48,640]{2,1,0:T(8,128)(2,1)S(1)}, u32[]{:S(2)}, u32[]{:S(2)}) %collective-permute-start.1) | collective-permute-done | bytes 122912 | tf_op jit(solution)/shard_map/ppermute | solution.py:40
  49.5 2.2 spread_tokens.1
  51.7 4.6 %all-to-all-start.1 = ((bf16[8,128,768]{2,1,0:T(8,128)(2,1)}), bf16[8,128,768]{2,1,0:T(8,128)(2,1)S(1)}, u32[]{:S(2)}, u32[]{:S(2)}) async-start(bf16[8,128,768]{2,1,0:T(8,128)(2,1)} %spread_tokens.1), calls=%async_computation.1 | async-start | bytes 3145728 | tf_op jit(solution)/shard_map/all_to_all | solution.py:581
  57.1 1.3 fusion.7
  58.5 1.4 collective-permute-start.3
  59.9 1.0 copy.47.refs_4_.refs_6_
  61.0 1.2 multiply_sine_fusion
  64.0 15.5 %all-to-all-done.1 = bf16[8,128,768]{2,1,0:T(8,128)(2,1)S(1)} async-done(((bf16[8,128,768]{2,1,0:T(8,128)(2,1)}), bf16[8,128,768]{2,1,0:T(8,128)(2,1)S(1)}, u32[]{:S(2)}, u32[]{:S(2)}) %all-to-all-start.1) | async-done | bytes 1572896 | tf_op jit(solution)/shard_map/all_to_all | solution.py:581
  79.5 1.2 copy-done.7
  80.7 12.9 %attention_forward.1 = (bf16[8,192,128]{2,1,0:T(8,128)(2,1)}, bf16[1024,768]{1,0:T(8,128)(2,1)}, bf16[576,1024]{1,0:T(8,128)(2,1)}, f32[8,1024]{1,0:T(8,128)}, f...) custom-call(bf16[1024,768]{1,0:T(8,128)(2,1)} %bitcast.76, bf16[768,640]{1,0:T(8,128)(2,1)} %bitcast.71, ...), custom_call_target="tpu_custom_call" | custom-call | flops 240000008192 | bytes 480000000 | tf_op jit(solution)/shard_map/attention_forward/pallas_call | solution.py:507
  93.6 4.6 %all-to-all-start.2 = ((bf16[8,192,128]{2,1,0:T(8,128)(2,1)}), bf16[8,192,128]{2,1,0:T(8,128)(2,1)S(1)}, u32[]{:S(2)}, u32[]{:S(2)}) async-start(bf16[8,192,128]{2,1,0:T(8,128)(2,1)} %get-tuple-element.38), calls=%async_computation.2 | async-start | bytes 786432 | tf_op jit(solution)/shard_map/all_to_all | solution.py:604
  98.2 2.0 broadcast_select_fusion.1
  100.5 1.4 copy.49
  102.0 1.1 copy.48
  103.1 3.5 %all-to-all-done.2 = bf16[8,192,128]{2,1,0:T(8,128)(2,1)S(1)} async-done(((bf16[8,192,128]{2,1,0:T(8,128)(2,1)}), bf16[8,192,128]{2,1,0:T(8,128)(2,1)S(1)}, u32[]{:S(2)}, u32[]{:S(2)}) %all-to-all-start.2) | async-done | bytes 393248 | tf_op jit(solution)/shard_map/all_to_all | solution.py:604
  107.4 8.9 %mlp.1 = (bf16[8,192,128]{2,1,0:T(8,128)(2,1)}, f32[256,768]{1,0:T(8,128)}, f32[256,768]{1,0:T(8,128)}, bf16[256,768]{1,0:T(8,128)(2,1)}, bf16[256,1152]{1,0:T(8...) custom-call(bf16[2,128,768]{2,1,0:T(8,128)(2,1)} %refs_0_.3, bf16[2,768,128]{2,1,0:T(8,128)(2,1)} %bitcast.73, ...), custom_call_target="tpu_custom_call" | custom-call | flops 179999997952 | bytes 360000000 | tf_op jit(solution)/shard_map/mlp/pallas_call | solution.py:507
  116.4 5.0 %sent_weights.1 = (bf16[8,8,32,768]{3,2,1,0:T(8,128)(2,1)}, f32[8,8,768]{2,1,0:T(8,128)}) custom-call(s32[1]{0:T(128)} %bitcast.refs_0_, bf16[2,768,128]{2,1,0:T(8,128)(2,1)} %bitcast.74, bf16[2,128,768]{2,1,0:T(8,128)(2,1)} %refs_2_.5, f32[256,768]{1,0:T(8,128)} %get-tuple-element.39.refs_3_, bf16[256,768]{1,0:T(8,128)(2,1)} %get-tuple-element.40.refs_4_, ...), custom_call_target="tpu_custom_call" | custom-call | flops 99999997952 | bytes 200000000 | tf_op jit(solution)/shard_map/sent_weights/pallas_call | solution.py:507
  121.4 1.1 collective-permute-start.5
  122.5 3.5 %all-to-all-start.3 = ((bf16[8,192,128]{2,1,0:T(8,128)(2,1)}), bf16[8,192,128]{2,1,0:T(8,128)(2,1)S(1)}, u32[]{:S(2)}, u32[]{:S(2)}) async-start(bf16[8,192,128]{2,1,0:T(8,128)(2,1)} %get-tuple-element.46), calls=%async_computation.3 | async-start | bytes 786432 | tf_op jit(solution)/shard_map/all_to_all | solution.py:678
  126.3 6.1 %kept_weights.1 = (bf16[8,8,32,768]{3,2,1,0:T(8,128)(2,1)}, f32[8,8,768]{2,1,0:T(8,128)}, bf16[2,128,768]{2,1,0:T(8,128)(2,1)}) custom-call(s32[1]{0:T(128)} %bitcast.refs_0_, bf16[2,768,128]{2,1,0:T(8,128)(2,1)} %bitcast.75, bf16[2,128,768]{2,1,0:T(8,128)(2,1)} %refs_2_.5, f32[256,768]{1,0:T(8,128)} %get-tuple-element.39.refs_3_, ...), custom_call_target="tpu_custom_call" | custom-call | flops 1000000000 | bytes 2000000 | tf_op jit(solution)/shard_map/kept_weights/pallas_call | solution.py:507
  132.4 1.7 copy-done.4
  134.1 5.2 %sum_cores.1.refs_12_ = bf16[8,8,32,768]{3,2,1,0:T(8,128)(2,1)} custom-call(bf16[8,8,32,768]{3,2,1,0:T(8,128)(2,1)} %get-tuple-element.52.refs_0_, bf16[8,8,32,768]{3,2,1,0:T(8,128)(2,1)} %copy-done.4), custom_call_target="tpu_custom_call" | custom-call | flops 400000000 | bytes 800000 | tf_op jit(solution)/shard_map/sum_cores/pallas_call | solution.py:507
  140.1 13.4 %attention_backward.1 = (bf16[576,1024]{1,0:T(8,128)(2,1)}, bf16[8,128,768]{2,1,0:T(8,128)(2,1)}, f32[1,768]{1,0:T(1,128)}) custom-call(bf16[8,192,128]{2,1,0:T(8,128)(2,1)} %copy-done.9, bf16[576,1024]{1,0:T(8,128)(2,1)} %get-tuple-element.47.refs_1_, f32[8,1024]{1,0:T(8,128)} %get-tuple-element.48.refs_2_, f32[192,1024]{1,0:T(8,128)} %get-tuple-element.49.refs_3_, ...), custom_call_target="tpu_custom_call" | custom-call | flops 240000008192 | bytes 480000000 | tf_op jit(solution)/shard_map/attention_backward/pallas_call | solution.py:507
  153.5 4.8 %all-to-all-start.4 = ((bf16[8,128,768]{2,1,0:T(8,128)(2,1)}), bf16[8,128,768]{2,1,0:T(8,128)(2,1)S(1)}, u32[]{:S(2)}, u32[]{:S(2)}) async-start(bf16[8,128,768]{2,1,0:T(8,128)(2,1)} %get-tuple-element.53), calls=%async_computation.4 | async-start | bytes 3145728 | tf_op jit(solution)/shard_map/all_to_all | solution.py:705
  158.2 4.4 %qkv_weights.1 = (bf16[8,48,768]{2,1,0:T(8,128)(2,1)}, bf16[8,48,768]{2,1,0:T(8,128)(2,1)}) custom-call(s32[1]{0:T(128)} %bitcast.refs_0_, bf16[1024,768]{1,0:T(8,128)(2,1)} %get-tuple-element.54.refs_1_, bf16[576,1024]{1,0:T(8,128)(2,1)} %get-tuple-element.55.refs_2_, f32[1,768]{1,0:T(1,128)} %get-tuple-element.56.refs_3_, ...), custom_call_target="tpu_custom_call" | custom-call | flops 2000000000 | bytes 4000000 | tf_op jit(solution)/shard_map/qkv_weights/pallas_call | solution.py:507
  163.2 1.8 collective-permute-done.6.refs_1_
  165.0 24.5 %all-to-all-done.4.refs_2_ = bf16[8,128,768]{2,1,0:T(8,128)(2,1)S(1)} async-done(((bf16[8,128,768]{2,1,0:T(8,128)(2,1)}), bf16[8,128,768]{2,1,0:T(8,128)(2,1)S(1)}, u32[]{:S(2)}, u32[]{:S(2)}) %all-to-all-start.4) | async-done | bytes 1572896 | tf_op jit(solution)/shard_map/all_to_all | solution.py:705
  189.5 1.2 copy-done
  190.7 2.3 sum_cores_last.1
  193.0 4.0 %all-to-all-start.5 = ((bf16[8,48,768]{2,1,0:T(8,128)(2,1)}), bf16[8,48,768]{2,1,0:T(8,128)(2,1)S(1)}, u32[]{:S(2)}, u32[]{:S(2)}) async-start(bf16[8,48,768]{2,1,0:T(8,128)(2,1)} %sum_cores_last.1), calls=%async_computation.5 | async-start | bytes 1179648 | tf_op jit(solution)/shard_map/all_to_all | solution.py:71
  197.4 11.9 %all-to-all-done.5 = bf16[8,48,768]{2,1,0:T(8,128)(2,1)S(1)} async-done(((bf16[8,48,768]{2,1,0:T(8,128)(2,1)}), bf16[8,48,768]{2,1,0:T(8,128)(2,1)S(1)}, u32[]{:S(2)}, u32[]{:S(2)}) %all-to-all-start.5) | async-done | bytes 589856 | tf_op jit(solution)/shard_map/all_to_all | solution.py:71
  209.3 5.2 %all-to-all-start.6 = ((bf16[8,32,768]{2,1,0:T(8,128)(2,1)}), bf16[8,32,768]{2,1,0:T(8,128)(2,1)}, u32[]{:S(2)}, u32[]{:S(2)}) async-start(bf16[8,32,768]{2,1,0:T(8,128)(2,1)} %reduce-scatter.2.cloned.1.call-done), calls=%async_computation.7 | async-start | bytes 786432 | tf_op jit(solution)/shard_map/all_to_all | solution.py:71
  214.8 10.1 %all-to-all-done.6 = bf16[8,32,768]{2,1,0:T(8,128)(2,1)} async-done(((bf16[8,32,768]{2,1,0:T(8,128)(2,1)}), bf16[8,32,768]{2,1,0:T(8,128)(2,1)}, u32[]{:S(2)}, u32[]{:S(2)}) %all-to-all-start.6) | async-done | bytes 393248 | tf_op jit(solution)/shard_map/all_to_all | solution.py:71
  224.9 1.1 reduce_sum.75
  226.0 1.1 broadcast_in_dim.24
  227.0 5.3 %all-to-all-start.7 = ((bf16[8,80,768]{2,1,0:T(8,128)(2,1)}), bf16[8,80,768]{2,1,0:T(8,128)(2,1)S(1)}, u32[]{:S(2)}, u32[]{:S(2)}) async-start(bf16[8,80,768]{2,1,0:T(8,128)(2,1)} %broadcast_in_dim.24), calls=%async_computation.8 | async-start | bytes 1966080 | tf_op jit(solution)/shard_map/all_to_all | solution.py:23
  232.7 1.2 fusion.4
  233.9 13.6 %all-to-all-done.7.refs_0_ = bf16[8,80,768]{2,1,0:T(8,128)(2,1)S(1)} async-done(((bf16[8,80,768]{2,1,0:T(8,128)(2,1)}), bf16[8,80,768]{2,1,0:T(8,128)(2,1)S(1)}, u32[]{:S(2)}, u32[]{:S(2)}) %all-to-all-start.7) | async-done | bytes 983072 | tf_op jit(solution)/shard_map/all_to_all | solution.py:23
  247.5 1.0 copy-done.8
  248.5 2.4 finish.1
  (74 shorter events, 9.2 us)
Async XLA Ops:
  9.3 8.5 %copy-start.12 = (bf16[48]{0:T(256)(128)(2,1)S(1)}, bf16[48]{0:T(256)(128)(2,1)}, u32[]{:S(2)}) copy-start(bf16[48]{0:T(256)(128)(2,1)} %param.16) | copy-start | bytes 292
  9.3 8.5 %copy-start.13 = (bf16[48]{0:T(256)(128)(2,1)S(1)}, bf16[48]{0:T(256)(128)(2,1)}, u32[]{:S(2)}) copy-start(bf16[48]{0:T(256)(128)(2,1)} %param.13) | copy-start | bytes 292
  9.3 40.1 %all-to-all-start = ((bf16[8,120,768]{2,1,0:T(8,128)(2,1)}), bf16[8,120,768]{2,1,0:T(8,128)(2,1)}, u32[]{:S(2)}, u32[]{:S(2)}) async-start(bf16[8,120,768]{2,1,0:T(8,128)(2,1)} %broadcast_in_dim.19), calls=%async_computation | async-start | bytes 2949120 | tf_op jit(solution)/shard_map/all_to_all | solution.py:50
  17.8 88.9 %all-gather.2.cloned.1.call-start = ((), (), s32[]{:S(2)}) async-start(), calls=%async_computation.9 | async-start | bytes 3760128 | tf_op jit(solution)/shard_map/all_gather | solution.py:571
  18.6 25.5 %copy-start.14 = (s32[8]{0:T(128)S(1)}, s32[8]{0:T(128)}, u32[]{:S(2)}) copy-start(s32[8]{0:T(128)} %param.12) | copy-start | bytes 100
  18.6 25.5 %copy-start.15 = (s32[2]{0:T(128)S(1)}, s32[2]{0:T(128)}, u32[]{:S(2)}) copy-start(s32[2]{0:T(128)} %param.11) | copy-start | bytes 28
  20.3 11.9 %collective-permute-start = (bf16[1,48,640]{2,1,0:T(8,128)(2,1)}, bf16[1,48,640]{2,1,0:T(8,128)(2,1)S(1)}, u32[]{:S(2)}, u32[]{:S(2)}) collective-permute-start(bf16[1,48,640]{2,1,0:T(8,128)(2,1)} %bitcast.84), channel_id=1, source_target_pairs={{0,8},{1,9},{2,10},{3,11},{4,12},{5,13},{6,14},{7,15},{8,0},{9,1},... | collective-permute-start | bytes 184328 | tf_op jit(solution)/shard_map/ppermute | solution.py:40
  33.2 16.0 %collective-permute-start.1 = (bf16[2,48,640]{2,1,0:T(8,128)(2,1)S(1)}, bf16[2,48,640]{2,1,0:T(8,128)(2,1)S(1)}, u32[]{:S(2)}, u32[]{:S(2)}) collective-permute-start(bf16[2,48,640]{2,1,0:T(8,128)(2,1)S(1)} %maximum_select_fusion.4), channel_id=1, source_target_pairs={{0,4},{1,5},{2,6},{3,7},{4,0},{5,1},{6,2},{7,3},{8,12},{9,13},{10,... | collective-permute-start | bytes 368648 | tf_op jit(solution)/shard_map/ppermute | solution.py:40
  49.2 9.2 %collective-permute-start.2 = (bf16[4,48,640]{2,1,0:T(8,128)(2,1)S(1)}, bf16[4,48,640]{2,1,0:T(8,128)(2,1)S(1)}, u32[]{:S(2)}, u32[]{:S(2)}) collective-permute-start(bf16[4,48,640]{2,1,0:T(8,128)(2,1)S(1)} %bitcast.79), channel_id=1, source_target_pairs={{0,2},{1,3},{2,0},{3,1},{4,6},{5,7},{6,4},{7,5},{8,10},{9,11},{10,... | collective-permute-start | bytes 737288 | tf_op jit(solution)/shard_map/ppermute | solution.py:40
  51.7 27.8 %all-to-all-start.1 = ((bf16[8,128,768]{2,1,0:T(8,128)(2,1)}), bf16[8,128,768]{2,1,0:T(8,128)(2,1)S(1)}, u32[]{:S(2)}, u32[]{:S(2)}) async-start(bf16[8,128,768]{2,1,0:T(8,128)(2,1)} %spread_tokens.1), calls=%async_computation.1 | async-start | bytes 3145728 | tf_op jit(solution)/shard_map/all_to_all | solution.py:581
  58.5 3.7 %collective-permute-start.3 = (bf16[8,48,640]{2,1,0:T(8,128)(2,1)S(1)}, bf16[8,48,640]{2,1,0:T(8,128)(2,1)S(1)}, u32[]{:S(2)}, u32[]{:S(2)}) collective-permute-start(bf16[8,48,640]{2,1,0:T(8,128)(2,1)S(1)} %bitcast.68), channel_id=1, source_target_pairs={{0,1},{1,0},{2,3},{3,2},{4,5},{5,4},{6,7},{7,6},{8,9},{9,8},{10,11... | collective-permute-start | bytes 1474568 | tf_op jit(solution)/shard_map/ppermute | solution.py:40
  62.5 17.0 %copy-start.5 = (bf16[8,2,48,640]{3,2,1,0:T(8,128)(2,1)}, bf16[8,2,48,640]{3,2,1,0:T(8,128)(2,1)S(1)}, u32[]{:S(2)}) copy-start(bf16[8,2,48,640]{3,2,1,0:T(8,128)(2,1)S(1)} %copy.46) | copy-start | bytes 2949124
  64.0 34.1 %collective-permute-start.4 = (bf16[8,120,768]{2,1,0:T(8,128)(2,1)}, bf16[8,120,768]{2,1,0:T(8,128)(2,1)}, u32[]{:S(2)}, u32[]{:S(2)}) collective-permute-start(bf16[8,120,768]{2,1,0:T(8,128)(2,1)} %all-to-all-done.refs_1_), channel_id=1, source_target_pairs={{0,1},{1,0},{2,3},{3,2},{4,5},{5,4},{6,7},{7,6},{8,9},{9,8},{10,11... | collective-permute-start | bytes 4423688 | tf_op jit(solution)/shard_map/ppermute | solution.py:57
  79.5 1.2 copy-start.7
  93.6 13.1 %all-to-all-start.2 = ((bf16[8,192,128]{2,1,0:T(8,128)(2,1)}), bf16[8,192,128]{2,1,0:T(8,128)(2,1)S(1)}, u32[]{:S(2)}, u32[]{:S(2)}) async-start(bf16[8,192,128]{2,1,0:T(8,128)(2,1)} %get-tuple-element.38), calls=%async_computation.2 | async-start | bytes 786432 | tf_op jit(solution)/shard_map/all_to_all | solution.py:604
  106.7 0.7 copy-start.6
  121.4 11.0 %collective-permute-start.5 = (bf16[8,8,32,768]{3,2,1,0:T(8,128)(2,1)}, bf16[8,8,32,768]{3,2,1,0:T(8,128)(2,1)S(1)}, u32[]{:S(2)}, u32[]{:S(2)}) collective-permute-start(bf16[8,8,32,768]{3,2,1,0:T(8,128)(2,1)} %get-tuple-element.44.refs_9_), channel_id=1, source_target_pairs={{0,1},{1,0},{2,3},{3,2},{4,5},{5,4},{6,7},{7,6},{8,9},{9,8},{10,11... | collective-permute-start | bytes 9437192 | tf_op jit(solution)/shard_map/ppermute | solution.py:63
  122.5 16.8 %all-to-all-start.3 = ((bf16[8,192,128]{2,1,0:T(8,128)(2,1)}), bf16[8,192,128]{2,1,0:T(8,128)(2,1)S(1)}, u32[]{:S(2)}, u32[]{:S(2)}) async-start(bf16[8,192,128]{2,1,0:T(8,128)(2,1)} %get-tuple-element.46), calls=%async_computation.3 | async-start | bytes 786432 | tf_op jit(solution)/shard_map/all_to_all | solution.py:678
  126.0 83.3 %reduce-scatter.2.cloned.1.call-start = ((), (), s32[]{:S(2)}) async-start(), calls=%async_computation.10 | async-start | bytes 3538944 | tf_op jit(solution)/shard_map/reduce_scatter | solution.py:674
  132.4 1.7 copy-start.4
  139.3 0.7 copy-start.9
  153.5 36.1 %all-to-all-start.4 = ((bf16[8,128,768]{2,1,0:T(8,128)(2,1)}), bf16[8,128,768]{2,1,0:T(8,128)(2,1)S(1)}, u32[]{:S(2)}, u32[]{:S(2)}) async-start(bf16[8,128,768]{2,1,0:T(8,128)(2,1)} %get-tuple-element.53), calls=%async_computation.4 | async-start | bytes 3145728 | tf_op jit(solution)/shard_map/all_to_all | solution.py:705
  162.6 2.4 collective-permute-start.6
  165.0 24.5 %copy-start.11 = (bf16[8,48,768]{2,1,0:T(8,128)(2,1)}, bf16[8,48,768]{2,1,0:T(8,128)(2,1)S(1)}, u32[]{:S(2)}) copy-start(bf16[8,48,768]{2,1,0:T(8,128)(2,1)S(1)} %collective-permute-done.6.refs_1_) | copy-start | bytes 1769476
  189.5 1.2 copy-start
  190.7 6.3 %copy-start.2 = (bf16[2,128,768]{2,1,0:T(8,128)(2,1)S(1)}, bf16[2,128,768]{2,1,0:T(8,128)(2,1)}, u32[]{:S(2)}) copy-start(bf16[2,128,768]{2,1,0:T(8,128)(2,1)} %refs_0_.3) | copy-start | bytes 1179652
  193.0 21.5 %copy-start.1 = (bf16[8,128,768]{2,1,0:T(8,128)(2,1)S(1)}, bf16[8,128,768]{2,1,0:T(8,128)(2,1)}, u32[]{:S(2)}) copy-start(bf16[8,128,768]{2,1,0:T(8,128)(2,1)} %copy-done) | copy-start | bytes 4718596
  193.0 16.3 %all-to-all-start.5 = ((bf16[8,48,768]{2,1,0:T(8,128)(2,1)}), bf16[8,48,768]{2,1,0:T(8,128)(2,1)S(1)}, u32[]{:S(2)}, u32[]{:S(2)}) async-start(bf16[8,48,768]{2,1,0:T(8,128)(2,1)} %sum_cores_last.1), calls=%async_computation.5 | async-start | bytes 1179648 | tf_op jit(solution)/shard_map/all_to_all | solution.py:71
  209.3 15.6 %all-to-all-start.6 = ((bf16[8,32,768]{2,1,0:T(8,128)(2,1)}), bf16[8,32,768]{2,1,0:T(8,128)(2,1)}, u32[]{:S(2)}, u32[]{:S(2)}) async-start(bf16[8,32,768]{2,1,0:T(8,128)(2,1)} %reduce-scatter.2.cloned.1.call-done), calls=%async_computation.7 | async-start | bytes 786432 | tf_op jit(solution)/shard_map/all_to_all | solution.py:71
  226.0 6.4 %copy-start.10 = (f32[768]{0:T(1024)S(1)}, f32[768]{0:T(1024)}, u32[]{:S(2)}) copy-start(f32[768]{0:T(1024)} %get-tuple-element.68) | copy-start | bytes 9220
  227.0 5.7 %copy-start.3 = (f32[256,768]{1,0:T(8,128)S(1)}, f32[256,768]{1,0:T(8,128)}, u32[]{:S(2)}) copy-start(f32[256,768]{1,0:T(8,128)} %get-tuple-element.39.refs_3_) | copy-start | bytes 2359300
  227.0 20.4 %all-to-all-start.7 = ((bf16[8,80,768]{2,1,0:T(8,128)(2,1)}), bf16[8,80,768]{2,1,0:T(8,128)(2,1)S(1)}, u32[]{:S(2)}, u32[]{:S(2)}) async-start(bf16[8,80,768]{2,1,0:T(8,128)(2,1)} %broadcast_in_dim.24), calls=%async_computation.8 | async-start | bytes 1966080 | tf_op jit(solution)/shard_map/all_to_all | solution.py:23
  247.5 1.0 copy-start.8
Sparse Core Ops, SparseCore 0:
  23.4 70.5 all-gather.1
  139.4 61.9 reduce-scatter.1

commit v5 on v4

--- a/solution.py
+++ b/solution.py
@@ -31,32 +31,24 @@
     return [list(range(first, n, 2)) for first in range(2)]
 
 
-def gather_doubling(part, axis):
+def doubled(held, axis, bit, after=()):
     n = lax.axis_size(axis)
     index = lax.axis_index(axis)
-    held = part[None]
-    bit = n // 2
-    while bit:
-        came = lax.ppermute(held, axis, [(k, k ^ bit) for k in range(n)])
+    came = lax.ppermute(held, axis, [(k, k ^ bit) for k in range(n)])
+    if after:
+        held = on_device(
+            interleave_kernel,
+            [((held.shape[0], 2, *held.shape[1:]), held.dtype)],
+            ((index // bit % 2).astype(jnp.int32)[None], held, came),
+            0.02,
+            scalars=1,
+            after=after,
+            name="interleave",
+        )[0]
+    else:
         first = (index & bit) == 0
         held = jnp.where(first, jnp.stack([held, came], 1), jnp.stack([came, held], 1))
-        held = held.reshape(-1, *part.shape)
-        bit //= 2
-    return held
-
-
-def gather_two_level(part, axis):
-    n = lax.axis_size(axis)
-    mine = lax.all_to_all(
-        jnp.broadcast_to(part[None], (n // 2, *part.shape)),
-        axis,
-        0,
-        0,
-        axis_index_groups=core_groups(n),
-    )
-    other = lax.ppermute(mine, axis, core_pairs(n))
-    even = lax.axis_index(axis) % 2 == 0
-    return mine, (jnp.where(even, mine, other), jnp.where(even, other, mine))
+    return held.reshape(-1, *held.shape[2:])
 
 
 def core_sum(kept, away, axis, micros, after=(), name=None):
@@ -317,13 +309,27 @@
             ]
 
 
-def half_weights(which, att_ref, cot_ref, gm_ref, b_ref, hid_ref, gg_ref, part_ref, extra_ref, turned, tall):
+def half_weights(
+    which,
+    att_ref,
+    cot_ref,
+    gm_ref,
+    b_ref,
+    hid_ref,
+    gg_ref,
+    part_ref,
+    tail_ref,
+    extra_ref,
+    turned,
+    tall,
+):
     seqs, width, local_len = att_ref.shape
     ctx, pairs, chunk, _ = part_ref.shape
     count = gg_ref.shape[1] // width
     depth = width // (2 * pairs)
     down_rows = hid_ref.shape[1] // (2 * pairs)
-    split = ctx * chunk - (count + 1) * depth
+    front = ctx * chunk
+    split = front + tail_ref.shape[1] - (count + 1) * depth
     cot = jnp.concatenate([cot_ref[k] for k in range(seqs)], 0)
     turned[:width] = b_ref[...].astype(jnp.float32).T
     turned[width : 2 * width] = jnp.concatenate(
@@ -352,6 +358,7 @@
         ).astype(jnp.bfloat16)
         for part in range(ctx):
             part_ref[part, pair] = rows[part * chunk : (part + 1) * chunk]
+        tail_ref[pair] = rows[front:]
         extra_ref[pair] = tall[pair * down_rows + split : (pair + 1) * down_rows]
 
 
@@ -370,6 +377,7 @@
     wdown_ref,
     mixed_ref,
     part_ref,
+    tail_ref,
     extra_ref,
     out_ref,
     turned,
@@ -384,6 +392,7 @@
         hid_ref,
         gg_ref,
         part_ref,
+        tail_ref,
         extra_ref,
         turned,
         tall,
@@ -484,7 +493,15 @@
     gains = total[:, lane : lane + 128].T
     gain_one_ref[...] = gains[3 * span - lane : 3 * span - lane + 1]
     gain_two_ref[...] = gains[3 * span - lane + 1 : 3 * span - lane + 2]
-    main = jnp.concatenate([ends_ref[k, depth:].astype(f32) for k in range(ctx)], 0)
+    chunk = (ends_ref.shape[1] - depth) // 2
+    main = jnp.concatenate(
+        [
+            ends_ref[k, depth + part * chunk : depth + (part + 1) * chunk].astype(f32)
+            for part in range(2)
+            for k in range(ctx)
+        ],
+        0,
+    )
     for k in range(count):
         win_ref[:, k * width : (k + 1) * width] = main[k * depth : (k + 1) * depth]
     wout_ref[...] = main[count * depth : (count + 1) * depth]
@@ -527,10 +544,17 @@
         )
 
 
-def spread_kernel(tokens_ref, out_ref):
-    copies = out_ref.shape[0] // tokens_ref.shape[0]
-    for k in range(out_ref.shape[0]):
-        out_ref[k] = tokens_ref[k // copies]
+def interleave_kernel(late_ref, held_ref, came_ref, out_ref):
+    late = late_ref[0]
+    for k in range(held_ref.shape[0]):
+        out_ref[k, late] = held_ref[k]
+        out_ref[k, 1 - late] = came_ref[k]
+
+
+def stack_kernel(upper_ref, lower_ref, out_ref):
+    rows = upper_ref.shape[0]
+    out_ref[:rows] = upper_ref[...]
+    out_ref[rows:] = lower_ref[...]
 
 
 def body(tokens, lengths, deal, gain_attn, w_qkv, w_out, gain_mlp, w_in, w_down, cotangent):
@@ -563,22 +587,26 @@
         first_kernel,
         [((depth, used), jnp.bfloat16)],
         (own_group.astype(jnp.int32)[None], w_qkv, gains_wide),
-        1,
+        0.05,
         scalars=1,
         name="first_pack",
     )[0]
-    first_all = gather_doubling(first, "fsdp").reshape(fsdp * depth, used)
+    steps = [fsdp >> (k + 1) for k in range(fsdp.bit_length() - 1)]
+    held = first[None]
+    for bit in steps[:-1]:
+        held = doubled(held, "fsdp", bit)
+    first_all = doubled(held, "fsdp", steps[-1]).reshape(fsdp * depth, used)
     win_all = lax.all_gather(w_in, "fsdp", axis=0, tiled=True)
-    stacked_mine, stacked_all = gather_two_level(jnp.concatenate([w_out, w_down], 0), "fsdp")
-    to_send = on_device(
-        spread_kernel,
-        [((ctx, local_len, width), jnp.bfloat16)],
-        (tokens,),
-        1,
-        after=(stacked_mine,),
-        name="spread_tokens",
+    sequence = lax.all_to_all(jnp.repeat(tokens, spread, axis=0), "ctx", 0, 0, tiled=True)
+    stacked = on_device(
+        stack_kernel,
+        [((depth + down_rows, width), jnp.bfloat16)],
+        (w_out, w_down),
+        0.02,
+        after=(held,),
+        name="stack_rest",
     )[0]
-    sequence = lax.all_to_all(to_send, "ctx", 0, 0, tiled=True)
+    rest = doubled(stacked[None], "fsdp", steps[0])
     gain_one = first_all[:, 3 * span]
     gain_two = first_all[:, 3 * span + 1]
 
@@ -598,15 +626,18 @@
             ((full_len, 1), f32),
         ],
         (sequence, first_all, cosine, sine, bias, keep_row),
-        12,
+        0.6,
         name="attention_forward",
     )
+    rest = doubled(rest, "fsdp", steps[1], after=(attended,))
+    for bit in steps[2:]:
+        rest = doubled(rest, "fsdp", bit)
+    stacked_all = rest
     att_back = lax.all_to_all(attended, "ctx", 0, 0, tiled=True)
     att_turned = att_back.reshape(seqs, width, local_len)
 
     def whole(start, height):
-        halves = [part[:, start : start + height] for part in stacked_all]
-        return jnp.stack(halves, 1).reshape(fsdp * height, width)
+        return stacked_all[:, start : start + height].reshape(fsdp * height, width)
 
     wout_all = whole(0, depth)
     wdown_all = whole(depth, down_rows)
@@ -614,7 +645,8 @@
     resid = tokens.astype(f32).reshape(rows, width)
     count = w_in.shape[1] // width
     main_rows = ((count + 1) * depth + down_rows) // (8 * ctx) * 8 * ctx
-    chunk = main_rows // ctx
+    chunk = main_rows // (2 * ctx)
+    front = ctx * chunk
     split = main_rows - (count + 1) * depth
     extra = down_rows - split
     pairs = fsdp // 2
@@ -639,19 +671,20 @@
             win_all,
             wdown_all,
         ),
-        9,
+        0.5,
         name="mlp",
     )
     weights_in = (core, att_turned, cotangent, grad_mixed, b_low, hid_low, grad_gate_up)
     half_outs = [
         ((ctx, pairs, chunk, width), jnp.bfloat16),
+        ((pairs, front, width), jnp.bfloat16),
         ((pairs, extra, width), f32),
     ]
     half_scratch = [
         pltpu.VMEM((2 * width + hidden, rows), f32),
         pltpu.VMEM((hidden // 2, width), f32),
     ]
-    main_away, away_extra = on_device(
+    front_away, tail_away, away_extra = on_device(
         sent_weights_kernel,
         half_outs,
         weights_in,
@@ -660,19 +693,22 @@
         scalars=1,
         name="sent_weights",
     )
-    main_kept, kept_extra, output = on_device(
+    front_kept, tail_kept, kept_extra, output = on_device(
         kept_weights_kernel,
         [*half_outs, (tokens.shape, jnp.bfloat16)],
         (*weights_in, wdown_all, mixed),
         0.05,
         half_scratch,
         scalars=1,
-        after=(main_away,),
+        after=(front_away,),
         name="kept_weights",
     )
-    main_pair = core_sum(main_kept, main_away, "fsdp", 0.02, name="sum_cores")
-    main_part = lax.psum_scatter(
-        main_pair.reshape(-1, chunk, width), "ctx", scatter_dimension=0, tiled=True
+    tail_pair = core_sum(tail_kept, tail_away, "fsdp", 0.02, name="sum_cores_tail")
+    front_pair = core_sum(
+        front_kept, front_away, "fsdp", 0.02, after=(tail_pair,), name="sum_cores_front"
+    )
+    front_part = lax.psum_scatter(
+        front_pair.reshape(-1, chunk, width), "ctx", scatter_dimension=0, tiled=True
     )
 
     all_grad = lax.all_to_all(grad_heads, "ctx", 0, 0, tiled=True)
@@ -699,10 +735,15 @@
         ),
         12,
         [pltpu.VMEM((HD, full_len), f32)] * 2,
-        after=(main_pair,),
+        after=(front_pair,),
         name="attention_backward",
     )
-    grad_a_parts = lax.all_to_all(grad_a_part, "ctx", 0, 0, tiled=True)
+    tail_part = spread_sum(tail_pair, "fsdp").reshape(ctx, chunk, width)
+    both_parts = lax.all_to_all(
+        jnp.concatenate([grad_a_part, tail_part], 1), "ctx", 0, 0, tiled=True
+    )
+    grad_a_parts = both_parts[:, :local_len]
+    tail_share = low(jnp.sum(both_parts[:, local_len:].astype(f32), 0))
     last_kept, last_away = on_device(
         qkv_weights_kernel,
         [((pairs, depth, width), jnp.bfloat16)] * 2,
@@ -713,7 +754,7 @@
         name="qkv_weights",
     )
     last = core_sum(
-        last_kept, last_away, "fsdp", 0.05, after=(grad_a_parts,), name="sum_cores_last"
+        last_kept, last_away, "fsdp", 0.05, after=(both_parts,), name="sum_cores_last"
     )
     grad_a = jnp.sum(
         grad_a_parts.reshape(seqs, spread, local_len, width).astype(f32), 1
@@ -722,9 +763,8 @@
     grad_norm_one, _ = norm_backward(grad_a, gain_one, normed_one, inverse_one)
     grad_input = grad_mixed + grad_norm_one
 
-    last = spread_sum(last, "fsdp")
-    main_part = spread_sum(main_part, "fsdp")
-    share = jnp.concatenate([last, main_part], 0)
+    share = spread_sum(jnp.concatenate([last, front_part], 1), "fsdp")
+    share = jnp.concatenate([share, tail_share], 0)
     ends = gather_by_exchange(share, "ctx", ctx)
     finished = on_device(
         finish_kernel,

time: 259 us -> 269 us (1.039)
  waiting for transfers between devices: 93.5 us -> 87.8 us
  other arithmetic: 13.5 us -> 18.8 us
  starting transfers between devices: 57.9 us -> 61.9 us
  Pallas kernels: 64.5 us -> 67.9 us
  local copies, waits for them, and re-layouts: 13.9 us -> 17.2 us
    all_to_all x3 -> x2, waiting for transfers between devices: 40 us -> 13.2 us  [the longest x1 13.2 us: body(): lax.all_to_all(jnp.concatenate([grad_a_part, tail_part], 1), 'ctx', 0, 0,...]
    ppermute x5 -> x8, waiting for transfers between devices: 12.5 us -> 27.9 us  [doubled(): came = lax.ppermute(held, axis, [(k, k ^ bit) for k in range(n)])]
    all_to_all x3 -> x2, starting transfers between devices: 17.9 us -> 10.9 us  [the longest x1 6.26 us: body(): lax.all_to_all(jnp.concatenate([grad_a_part, tail_part], 1), 'ctx', 0, 0,...]
    all_to_all x2, waiting for transfers between devices: 22 us -> 28.4 us  [spread_sum(): lax.all_to_all(parts, axis, 0, 0, tiled=True, axis_index_groups=groups)]
    all_to_all x2, starting transfers between devices: 9.2 us -> 14.5 us  [spread_sum(): lax.all_to_all(parts, axis, 0, 0, tiled=True, axis_index_groups=groups)]
    ppermute x5 -> x8, starting transfers between devices: 15.5 us -> 19.8 us  [doubled(): came = lax.ppermute(held, axis, [(k, k ^ bit) for k in range(n)])]
    pallas_call x11 -> x13, Pallas kernels: 64.5 us -> 67.9 us  [on_device(): pl.pallas_call(ordered, out_shape=[jax.ShapeDtypeStruct(shape, dtype) for...]
    ppermute x2 -> x3, starting transfers between devices: 1.66 us -> 4.83 us  [core_sum(): came = lax.ppermute(away, axis, core_pairs(lax.axis_size(axis)))]
  transfers between devices with their start and end apart: 17 -> 20, of which waited for: 9 -> 10; matrix products, arithmetic and copies ran while one was open for 6% -> 9% of each run, Pallas kernels for 19% -> 19%
where the time goes in v5:
time: 269 us; the launch traced here: 268 us
  waiting for transfers between devices  87.8 us (33%)
  Pallas kernels  67.9 us (25%)
  starting transfers between devices  61.9 us (23%)
  other arithmetic  18.8 us (7%)
  local copies, waits for them, and re-layouts  17.2 us (6%)
  between operations  14.3 us (5%)
    pallas_call x13, Pallas kernels, on_device(): pl.pallas_call(ordered, out_shape=[jax.ShapeDtypeStruct(shape, dtype) for...  67.9 us
    all_to_all x2, waiting for transfers between devices, spread_sum(): lax.all_to_all(parts, axis, 0, 0, tiled=True, axis_index_groups=groups)  28.4 us
    ppermute x8, waiting for transfers between devices, doubled(): came = lax.ppermute(held, axis, [(k, k ^ bit) for k in range(n)])  27.9 us
    ppermute x8, starting transfers between devices, doubled(): came = lax.ppermute(held, axis, [(k, k ^ bit) for k in range(n)])  19.8 us
    all_to_all x2, starting transfers between devices, spread_sum(): lax.all_to_all(parts, axis, 0, 0, tiled=True, axis_index_groups=groups)  14.5 us
    all_to_all x1, waiting for transfers between devices, body(): lax.all_to_all(jnp.concatenate([grad_a_part, tail_part], 1), 'ctx', 0, 0,...  13.2 us
    all_to_all x1, waiting for transfers between devices, gather_by_exchange(): lax.all_to_all(jnp.broadcast_to(part[None], (n, *part.shape)), axis, 0, 0)  12.7 us
    unnamed x40, local copies, waits for them, and re-layouts  8.72 us
  transfers between devices with their start and end apart: 20, of which 10 were waited for; matrix products, arithmetic and copies ran while one was open for 9% of the time, Pallas kernels for 19%

profile of v5, /device:TPU:1, one launch (start us, length us, event | category | flops | bytes accessed | tf_op | source)
XLA Modules:
  0.0 267.9 jit_solution(14590505433835797387)
XLA Ops:
  9.3 1.7 first_pack.1
  11.0 4.4 %collective-permute-start = (bf16[1,48,640]{2,1,0:T(8,128)(2,1)}, bf16[1,48,640]{2,1,0:T(8,128)(2,1)S(1)}, u32[]{:S(2)}, u32[]{:S(2)}) collective-permute-start(bf16[1,48,640]{2,1,0:T(8,128)(2,1)} %bitcast.99), channel_id=1, source_target_pairs={{0,8},{1,9},{2,10},{3,11},{4,12},{5,13},{6,14},{7,15},{8,0},{9,1},... | collective-permute-start | bytes 184328 | tf_op jit(solution)/shard_map/ppermute | solution.py:37
  15.5 1.3 broadcast_in_dim.21
  16.8 4.6 %all-to-all-start = ((bf16[8,128,768]{2,1,0:T(8,128)(2,1)}), bf16[8,128,768]{2,1,0:T(8,128)(2,1)S(1)}, u32[]{:S(2)}, u32[]{:S(2)}) async-start(bf16[8,128,768]{2,1,0:T(8,128)(2,1)} %bitcast.1), calls=%async_computation | async-start | bytes 3145728 | tf_op jit(solution)/shard_map/all_to_all | solution.py:600
  21.4 3.0 %collective-permute-start.1 = (bf16[2,48,640]{2,1,0:T(8,128)(2,1)S(1)}, bf16[2,48,640]{2,1,0:T(8,128)(2,1)S(1)}, u32[]{:S(2)}, u32[]{:S(2)}) collective-permute-start(bf16[2,48,640]{2,1,0:T(8,128)(2,1)S(1)} %maximum_select_fusion.7), channel_id=1, source_target_pairs={{0,4},{1,5},{2,6},{3,7},{4,0},{5,1},{6,2},{7,3},{8,12},{9,13},{10,... | collective-permute-start | bytes 368648 | tf_op jit(solution)/shard_map/ppermute | solution.py:37
  24.5 2.4 collective-permute-done.1
  27.0 1.6 collective-permute-start.2
  30.5 2.5 collective-permute-done.2
  33.1 4.0 %collective-permute-start.3 = (bf16[8,48,640]{2,1,0:T(8,128)(2,1)S(1)}, bf16[8,48,640]{2,1,0:T(8,128)(2,1)S(1)}, u32[]{:S(2)}, u32[]{:S(2)}) collective-permute-start(bf16[8,48,640]{2,1,0:T(8,128)(2,1)S(1)} %bitcast.79), channel_id=1, source_target_pairs={{0,1},{1,0},{2,3},{3,2},{4,5},{5,4},{6,7},{7,6},{8,9},{9,8},{10,11... | collective-permute-start | bytes 1474568 | tf_op jit(solution)/shard_map/ppermute | solution.py:37
  38.8 1.6 stack_rest.1
  41.3 1.3 fusion.7
  42.6 5.7 %collective-permute-done.4 = bf16[1,120,768]{2,1,0:T(8,128)(2,1)S(1)} collective-permute-done((bf16[1,120,768]{2,1,0:T(8,128)(2,1)}, bf16[1,120,768]{2,1,0:T(8,128)(2,1)S(1)}, u32[]{:S(2)}, u32[]{:S(2)}) %collective-permute-start.4) | collective-permute-done | bytes 184352 | tf_op jit(solution)/shard_map/ppermute | solution.py:37
  49.4 3.4 %collective-permute-start.5 = (bf16[2,120,768]{2,1,0:T(8,128)(2,1)S(1)}, bf16[2,120,768]{2,1,0:T(8,128)(2,1)S(1)}, u32[]{:S(2)}, u32[]{:S(2)}) collective-permute-start(bf16[2,120,768]{2,1,0:T(8,128)(2,1)S(1)} %maximum_select_fusion.4.refs_1_), channel_id=1, source_target_pairs={{0,4},{1,5},{2,6},{3,7},{4,0},{5,1},{6,2},{7,3},{8,12},{9,13},{10,... | collective-permute-start | bytes 1105928 | tf_op jit(solution)/shard_map/ppermute | solution.py:37
  52.8 1.5 maximum_select_fusion.2
  56.5 13.1 %attention_forward.1 = (bf16[8,192,128]{2,1,0:T(8,128)(2,1)}, bf16[1024,768]{1,0:T(8,128)(2,1)}, bf16[576,1024]{1,0:T(8,128)(2,1)}, f32[8,1024]{1,0:T(8,128)}, f...) custom-call(bf16[1024,768]{1,0:T(8,128)(2,1)} %bitcast.88, bf16[768,640]{1,0:T(8,128)(2,1)} %bitcast.82, ...), custom_call_target="tpu_custom_call" | custom-call | flops 12000000000 | bytes 24000000 | tf_op jit(solution)/shard_map/attention_forward/pallas_call | solution.py:524
  70.4 2.1 interleave.1
  73.5 17.3 %collective-permute-done.6 = bf16[4,120,768]{2,1,0:T(8,128)(2,1)S(1)} collective-permute-done((bf16[4,120,768]{2,1,0:T(8,128)(2,1)}, bf16[4,120,768]{2,1,0:T(8,128)(2,1)S(1)}, u32[]{:S(2)}, u32[]{:S(2)}) %collective-permute-start.6) | collective-permute-done | bytes 737312 | tf_op jit(solution)/shard_map/ppermute | solution.py:37
  90.7 1.6 maximum_select_fusion.1
  92.4 1.5 collective-permute-start.7
  93.9 4.7 %all-to-all-start.1 = ((bf16[8,192,128]{2,1,0:T(8,128)(2,1)}), bf16[8,192,128]{2,1,0:T(8,128)(2,1)S(1)}, u32[]{:S(2)}, u32[]{:S(2)}) async-start(bf16[8,192,128]{2,1,0:T(8,128)(2,1)} %get-tuple-element.40.refs_3_), calls=%async_computation.1 | async-start | bytes 786432 | tf_op jit(solution)/shard_map/all_to_all | solution.py:636
  98.6 1.9 convert_reduce_fusion.2
  101.8 1.4 slice.26
  104.3 3.2 %all-to-all-done.1 = bf16[8,192,128]{2,1,0:T(8,128)(2,1)S(1)} async-done(((bf16[8,192,128]{2,1,0:T(8,128)(2,1)}), bf16[8,192,128]{2,1,0:T(8,128)(2,1)S(1)}, u32[]{:S(2)}, u32[]{:S(2)}) %all-to-all-start.1) | async-done | bytes 393248 | tf_op jit(solution)/shard_map/all_to_all | solution.py:636
  108.2 8.9 %mlp.1 = (bf16[8,192,128]{2,1,0:T(8,128)(2,1)}, f32[256,768]{1,0:T(8,128)}, f32[256,768]{1,0:T(8,128)}, bf16[256,768]{1,0:T(8,128)(2,1)}, bf16[256,1152]{1,0:T(8...) custom-call(bf16[2,128,768]{2,1,0:T(8,128)(2,1)} %refs_0_.3, bf16[2,768,128]{2,1,0:T(8,128)(2,1)} %bitcast.85, ...), custom_call_target="tpu_custom_call" | custom-call | flops 10000000000 | bytes 20000000 | tf_op jit(solution)/shard_map/mlp/pallas_call | solution.py:524
  117.2 5.1 %sent_weights.1 = (bf16[8,8,16,768]{3,2,1,0:T(8,128)(2,1)}, bf16[8,128,768]{2,1,0:T(8,128)(2,1)}, f32[8,8,768]{2,1,0:T(8,128)}) custom-call(s32[1]{0:T(128)} %bitcast.refs_0_, bf16[2,768,128]{2,1,0:T(8,128)(2,1)} %bitcast.86, bf16[2,128,768]{2,1,0:T(8,128)(2,1)} %refs_2_.5, f32[256,768]{1,0:T(8,128)} %get-tuple-element.41.refs_3_, ...), custom_call_target="tpu_custom_call" | custom-call | flops 99999997952 | bytes 200000000 | tf_op jit(solution)/shard_map/sent_weights/pallas_call | solution.py:524
  123.0 3.5 %all-to-all-start.2 = ((bf16[8,192,128]{2,1,0:T(8,128)(2,1)}), bf16[8,192,128]{2,1,0:T(8,128)(2,1)S(1)}, u32[]{:S(2)}, u32[]{:S(2)}) async-start(bf16[8,192,128]{2,1,0:T(8,128)(2,1)} %get-tuple-element.48), calls=%async_computation.2 | async-start | bytes 786432 | tf_op jit(solution)/shard_map/all_to_all | solution.py:714
  126.5 6.2 %kept_weights.1 = (bf16[8,8,16,768]{3,2,1,0:T(8,128)(2,1)}, bf16[8,128,768]{2,1,0:T(8,128)(2,1)}, f32[8,8,768]{2,1,0:T(8,128)}, bf16[2,128,768]{2,1,0:T(8,128)(2,1)}) custom-call(s32[1]{0:T(128)} %bitcast.refs_0_, bf16[2,768,128]{2,1,0:T(8,128)(2,1)} %bitcast.87, bf16[2,128,768]{2,1,0:T(8,128)(2,1)} %refs_2_.5, f32[256,768]{1,0:T(8,128)} %get-tuple-element.41.refs_3_, ...), custom_call_target="tpu_custom_call" | custom-call | flops 1000000000 | bytes 2000000 | tf_op jit(solution)/shard_map/kept_weights/pallas_call | solution.py:524
  132.7 1.2 copy-done.10
  133.9 3.4 %sum_cores_tail.1.refs_2_ = bf16[8,128,768]{2,1,0:T(8,128)(2,1)} custom-call(bf16[8,128,768]{2,1,0:T(8,128)(2,1)} %get-tuple-element.55.refs_0_, bf16[8,128,768]{2,1,0:T(8,128)(2,1)} %copy-done.10), custom_call_target="tpu_custom_call" | custom-call | flops 400000000 | bytes 800000 | tf_op jit(solution)/shard_map/sum_cores_tail/pallas_call | solution.py:524
  137.3 1.2 copy-done.9
  138.6 3.4 %sum_cores_front.1.refs_12_ = bf16[8,8,16,768]{3,2,1,0:T(8,128)(2,1)} custom-call(bf16[8,8,16,768]{3,2,1,0:T(8,128)(2,1)} %get-tuple-element.54.refs_0_, bf16[8,8,16,768]{3,2,1,0:T(8,128)(2,1)} %copy-done.9, bf16[8,128,768]{2,1,0:T(8,128)(2,1)} %sum_cores_tail.1.refs_2_), custom_call_target="tpu_custom_call" | custom-call | flops 400000000 | bytes 800000 | tf_op jit(solution)/shard_map/sum_cores_front/pallas_call | solution.py:524
  142.8 4.5 %all-to-all-start.3 = ((bf16[8,128,768]{2,1,0:T(8,128)(2,1)}), bf16[8,128,768]{2,1,0:T(8,128)(2,1)}, u32[]{:S(2)}, u32[]{:S(2)}) async-start(bf16[8,128,768]{2,1,0:T(8,128)(2,1)} %sum_cores_tail.1.refs_2_), calls=%async_computation.3 | async-start | bytes 3145728 | tf_op jit(solution)/shard_map/all_to_all | solution.py:63
  147.3 13.4 %attention_backward.1 = (bf16[576,1024]{1,0:T(8,128)(2,1)}, bf16[8,128,768]{2,1,0:T(8,128)(2,1)}, f32[1,768]{1,0:T(1,128)}) custom-call(bf16[8,192,128]{2,1,0:T(8,128)(2,1)} %copy-done.13, bf16[576,1024]{1,0:T(8,128)(2,1)} %get-tuple-element.49.refs_1_, f32[8,1024]{1,0:T(8,128)} %get-tuple-element.50.refs_2_, f32[192,1024]{1,0:T(8,128)} %get-tuple-element.51.refs_3_, ...), custom_call_target="tpu_custom_call" | custom-call | flops 240000008192 | bytes 480000000 | tf_op jit(solution)/shard_map/attention_backward/pallas_call | solution.py:524
  160.8 14.3 %all-to-all-done.3 = bf16[8,128,768]{2,1,0:T(8,128)(2,1)} async-done(((bf16[8,128,768]{2,1,0:T(8,128)(2,1)}), bf16[8,128,768]{2,1,0:T(8,128)(2,1)}, u32[]{:S(2)}, u32[]{:S(2)}) %all-to-all-start.3) | async-done | bytes 1572896 | tf_op jit(solution)/shard_map/all_to_all | solution.py:63
  175.0 1.7 reduce_sum.83
  176.7 1.3 pad_maximum_fusion
  178.0 6.3 %all-to-all-start.4 = ((bf16[8,144,768]{2,1,0:T(8,128)(2,1)}), bf16[8,144,768]{2,1,0:T(8,128)(2,1)S(1)}, u32[]{:S(2)}, u32[]{:S(2)}) async-start(bf16[8,144,768]{2,1,0:T(8,128)(2,1)} %pad_maximum_fusion), calls=%async_computation.4 | async-start | bytes 3538944 | tf_op jit(solution)/shard_map/all_to_all | solution.py:742
  184.3 4.4 %qkv_weights.1 = (bf16[8,48,768]{2,1,0:T(8,128)(2,1)}, bf16[8,48,768]{2,1,0:T(8,128)(2,1)}) custom-call(s32[1]{0:T(128)} %bitcast.refs_0_, bf16[1024,768]{1,0:T(8,128)(2,1)} %get-tuple-element.58.refs_1_, bf16[576,1024]{1,0:T(8,128)(2,1)} %get-tuple-element.59.refs_2_, f32[1,768]{1,0:T(1,128)} %get-tuple-element.60.refs_3_, ...), custom_call_target="tpu_custom_call" | custom-call | flops 2000000000 | bytes 4000000 | tf_op jit(solution)/shard_map/qkv_weights/pallas_call | solution.py:524
  188.7 4.1 %collective-permute-start.10 = (bf16[8,48,768]{2,1,0:T(8,128)(2,1)}, bf16[8,48,768]{2,1,0:T(8,128)(2,1)S(1)}, u32[]{:S(2)}, u32[]{:S(2)}) collective-permute-start(bf16[8,48,768]{2,1,0:T(8,128)(2,1)} %get-tuple-element.65), channel_id=1, source_target_pairs={{0,1},{1,0},{2,3},{3,2},{4,5},{5,4},{6,7},{7,6},{8,9},{9,8},{10,11... | collective-permute-start | bytes 1769480 | tf_op jit(solution)/shard_map/ppermute | solution.py:55
  192.9 1.7 collective-permute-done.10.refs_1_
  194.6 13.2 %all-to-all-done.4.refs_2_ = bf16[8,144,768]{2,1,0:T(8,128)(2,1)S(1)} async-done(((bf16[8,144,768]{2,1,0:T(8,128)(2,1)}), bf16[8,144,768]{2,1,0:T(8,128)(2,1)S(1)}, u32[]{:S(2)}, u32[]{:S(2)}) %all-to-all-start.4) | async-done | bytes 1769504 | tf_op jit(solution)/shard_map/all_to_all | solution.py:742
  209.0 2.2 sum_cores_last.1
  211.2 2.2 pad_maximum_fusion.1
  213.5 10.0 %all-to-all-start.5 = ((bf16[8,64,768]{2,1,0:T(8,128)(2,1)}), bf16[8,64,768]{2,1,0:T(8,128)(2,1)S(1)}, u32[]{:S(2)}, u32[]{:S(2)}) async-start(bf16[8,64,768]{2,1,0:T(8,128)(2,1)} %pad_maximum_fusion.1), calls=%async_computation.6 | async-start | bytes 1572864 | tf_op jit(solution)/shard_map/all_to_all | solution.py:63
  223.8 14.2 %all-to-all-done.5 = bf16[8,64,768]{2,1,0:T(8,128)(2,1)S(1)} async-done(((bf16[8,64,768]{2,1,0:T(8,128)(2,1)}), bf16[8,64,768]{2,1,0:T(8,128)(2,1)S(1)}, u32[]{:S(2)}, u32[]{:S(2)}) %all-to-all-start.5) | async-done | bytes 786464 | tf_op jit(solution)/shard_map/all_to_all | solution.py:63
  239.1 3.6 %all-to-all-start.6 = ((bf16[8,80,768]{2,1,0:T(8,128)(2,1)}), bf16[8,80,768]{2,1,0:T(8,128)(2,1)S(1)}, u32[]{:S(2)}, u32[]{:S(2)}) async-start(bf16[8,80,768]{2,1,0:T(8,128)(2,1)} %broadcast_in_dim.49), calls=%async_computation.7 | async-start | bytes 1966080 | tf_op jit(solution)/shard_map/all_to_all | solution.py:23
  245.0 12.7 %all-to-all-done.6.refs_0_ = bf16[8,80,768]{2,1,0:T(8,128)(2,1)S(1)} async-done(((bf16[8,80,768]{2,1,0:T(8,128)(2,1)}), bf16[8,80,768]{2,1,0:T(8,128)(2,1)S(1)}, u32[]{:S(2)}, u32[]{:S(2)}) %all-to-all-start.6) | async-done | bytes 983072 | tf_op jit(solution)/shard_map/all_to_all | solution.py:23
  258.7 2.4 finish.1
  (90 shorter events, 22.7 us)
Async XLA Ops:
  7.2 100.3 %all-gather.2.cloned.1.call-start = ((), (), s32[]{:S(2)}) async-start(), calls=%async_computation.8 | async-start | bytes 3760128 | tf_op jit(solution)/shard_map/all_gather | solution.py:599
  9.3 6.1 %copy-start = (bf16[2,128,768]{2,1,0:T(8,128)(2,1)S(1)}, bf16[2,128,768]{2,1,0:T(8,128)(2,1)}, u32[]{:S(2)}) copy-start(bf16[2,128,768]{2,1,0:T(8,128)(2,1)} %refs_0_.3) | copy-start | bytes 1179652
  11.0 10.4 %collective-permute-start = (bf16[1,48,640]{2,1,0:T(8,128)(2,1)}, bf16[1,48,640]{2,1,0:T(8,128)(2,1)S(1)}, u32[]{:S(2)}, u32[]{:S(2)}) collective-permute-start(bf16[1,48,640]{2,1,0:T(8,128)(2,1)} %bitcast.99), channel_id=1, source_target_pairs={{0,8},{1,9},{2,10},{3,11},{4,12},{5,13},{6,14},{7,15},{8,0},{9,1},... | collective-permute-start | bytes 184328 | tf_op jit(solution)/shard_map/ppermute | solution.py:37
  16.8 4.6 %copy-start.18 = (s32[8]{0:T(128)S(1)}, s32[8]{0:T(128)}, u32[]{:S(2)}) copy-start(s32[8]{0:T(128)} %param.12) | copy-start | bytes 100
  16.8 4.6 %copy-start.15 = (bf16[48,640]{1,0:T(8,128)(2,1)S(1)}, bf16[48,640]{1,0:T(8,128)(2,1)}, u32[]{:S(2)}) copy-start(bf16[48,640]{1,0:T(8,128)(2,1)} %first_pack.1) | copy-start | bytes 184324
  16.8 11.9 %copy-start.19 = (s32[2]{0:T(128)S(1)}, s32[2]{0:T(128)}, u32[]{:S(2)}) copy-start(s32[2]{0:T(128)} %param.11) | copy-start | bytes 28
  16.8 38.6 %all-to-all-start = ((bf16[8,128,768]{2,1,0:T(8,128)(2,1)}), bf16[8,128,768]{2,1,0:T(8,128)(2,1)S(1)}, u32[]{:S(2)}, u32[]{:S(2)}) async-start(bf16[8,128,768]{2,1,0:T(8,128)(2,1)} %bitcast.1), calls=%async_computation | async-start | bytes 3145728 | tf_op jit(solution)/shard_map/all_to_all | solution.py:600
  21.4 5.5 %collective-permute-start.1 = (bf16[2,48,640]{2,1,0:T(8,128)(2,1)S(1)}, bf16[2,48,640]{2,1,0:T(8,128)(2,1)S(1)}, u32[]{:S(2)}, u32[]{:S(2)}) collective-permute-start(bf16[2,48,640]{2,1,0:T(8,128)(2,1)S(1)} %maximum_select_fusion.7), channel_id=1, source_target_pairs={{0,4},{1,5},{2,6},{3,7},{4,0},{5,1},{6,2},{7,3},{8,12},{9,13},{10,... | collective-permute-start | bytes 368648 | tf_op jit(solution)/shard_map/ppermute | solution.py:37
  27.0 5.9 %collective-permute-start.2 = (bf16[4,48,640]{2,1,0:T(8,128)(2,1)S(1)}, bf16[4,48,640]{2,1,0:T(8,128)(2,1)S(1)}, u32[]{:S(2)}, u32[]{:S(2)}) collective-permute-start(bf16[4,48,640]{2,1,0:T(8,128)(2,1)S(1)} %bitcast.92), channel_id=1, source_target_pairs={{0,2},{1,3},{2,0},{3,1},{4,6},{5,7},{6,4},{7,5},{8,10},{9,11},{10,... | collective-permute-start | bytes 737288 | tf_op jit(solution)/shard_map/ppermute | solution.py:37
  33.1 5.7 %copy-start.5 = (bf16[4,2,48,640]{3,2,1,0:T(8,128)(2,1)}, bf16[4,2,48,640]{3,2,1,0:T(8,128)(2,1)S(1)}, u32[]{:S(2)}) copy-start(bf16[4,2,48,640]{3,2,1,0:T(8,128)(2,1)S(1)} %copy.47) | copy-start | bytes 1474564
  33.1 19.7 %collective-permute-start.3 = (bf16[8,48,640]{2,1,0:T(8,128)(2,1)S(1)}, bf16[8,48,640]{2,1,0:T(8,128)(2,1)S(1)}, u32[]{:S(2)}, u32[]{:S(2)}) collective-permute-start(bf16[8,48,640]{2,1,0:T(8,128)(2,1)S(1)} %bitcast.79), channel_id=1, source_target_pairs={{0,1},{1,0},{2,3},{3,2},{4,5},{5,4},{6,7},{7,6},{8,9},{9,8},{10,11... | collective-permute-start | bytes 1474568 | tf_op jit(solution)/shard_map/ppermute | solution.py:37
  40.4 7.9 %collective-permute-start.4 = (bf16[1,120,768]{2,1,0:T(8,128)(2,1)}, bf16[1,120,768]{2,1,0:T(8,128)(2,1)S(1)}, u32[]{:S(2)}, u32[]{:S(2)}) collective-permute-start(bf16[1,120,768]{2,1,0:T(8,128)(2,1)} %bitcast.103), channel_id=1, source_target_pairs={{0,8},{1,9},{2,10},{3,11},{4,12},{5,13},{6,14},{7,15},{8,0},{9,1},... | collective-permute-start | bytes 552968 | tf_op jit(solution)/shard_map/ppermute | solution.py:37
  49.4 5.9 %copy-start.11 = (bf16[2,120,768]{2,1,0:T(8,128)(2,1)}, bf16[2,120,768]{2,1,0:T(8,128)(2,1)S(1)}, u32[]{:S(2)}) copy-start(bf16[2,120,768]{2,1,0:T(8,128)(2,1)S(1)} %maximum_select_fusion.4.refs_1_) | copy-start | bytes 1105924
  49.4 20.2 %collective-permute-start.5 = (bf16[2,120,768]{2,1,0:T(8,128)(2,1)S(1)}, bf16[2,120,768]{2,1,0:T(8,128)(2,1)S(1)}, u32[]{:S(2)}, u32[]{:S(2)}) collective-permute-start(bf16[2,120,768]{2,1,0:T(8,128)(2,1)S(1)} %maximum_select_fusion.4.refs_1_), channel_id=1, source_target_pairs={{0,4},{1,5},{2,6},{3,7},{4,0},{5,1},{6,2},{7,3},{8,12},{9,13},{10,... | collective-permute-start | bytes 1105928 | tf_op jit(solution)/shard_map/ppermute | solution.py:37
  55.3 1.2 copy-start.8
  69.6 0.7 copy-start.14
  72.5 18.3 %collective-permute-start.6 = (bf16[4,120,768]{2,1,0:T(8,128)(2,1)}, bf16[4,120,768]{2,1,0:T(8,128)(2,1)S(1)}, u32[]{:S(2)}, u32[]{:S(2)}) collective-permute-start(bf16[4,120,768]{2,1,0:T(8,128)(2,1)} %bitcast.77), channel_id=1, source_target_pairs={{0,2},{1,3},{2,0},{3,1},{4,6},{5,7},{6,4},{7,5},{8,10},{9,11},{10,... | collective-permute-start | bytes 2211848 | tf_op jit(solution)/shard_map/ppermute | solution.py:37
  92.4 8.8 %collective-permute-start.7 = (bf16[8,120,768]{2,1,0:T(8,128)(2,1)S(1)}, bf16[8,120,768]{2,1,0:T(8,128)(2,1)S(1)}, u32[]{:S(2)}, u32[]{:S(2)}) collective-permute-start(bf16[8,120,768]{2,1,0:T(8,128)(2,1)S(1)} %bitcast.75), channel_id=1, source_target_pairs={{0,1},{1,0},{2,3},{3,2},{4,5},{5,4},{6,7},{7,6},{8,9},{9,8},{10,11... | collective-permute-start | bytes 4423688 | tf_op jit(solution)/shard_map/ppermute | solution.py:37
  93.9 13.6 %all-to-all-start.1 = ((bf16[8,192,128]{2,1,0:T(8,128)(2,1)}), bf16[8,192,128]{2,1,0:T(8,128)(2,1)S(1)}, u32[]{:S(2)}, u32[]{:S(2)}) async-start(bf16[8,192,128]{2,1,0:T(8,128)(2,1)} %get-tuple-element.40.refs_3_), calls=%async_computation.1 | async-start | bytes 786432 | tf_op jit(solution)/shard_map/all_to_all | solution.py:636
  107.5 0.7 copy-start.6
  122.3 10.4 %collective-permute-start.9 = (bf16[8,128,768]{2,1,0:T(8,128)(2,1)}, bf16[8,128,768]{2,1,0:T(8,128)(2,1)S(1)}, u32[]{:S(2)}, u32[]{:S(2)}) collective-permute-start(bf16[8,128,768]{2,1,0:T(8,128)(2,1)} %get-tuple-element.56), channel_id=1, source_target_pairs={{0,1},{1,0},{2,3},{3,2},{4,5},{5,4},{6,7},{7,6},{8,9},{9,8},{10,11... | collective-permute-start | bytes 4718600 | tf_op jit(solution)/shard_map/ppermute | solution.py:55
  123.0 14.3 %collective-permute-start.8 = (bf16[8,8,16,768]{3,2,1,0:T(8,128)(2,1)}, bf16[8,8,16,768]{3,2,1,0:T(8,128)(2,1)S(1)}, u32[]{:S(2)}, u32[]{:S(2)}) collective-permute-start(bf16[8,8,16,768]{3,2,1,0:T(8,128)(2,1)} %get-tuple-element.46.refs_9_), channel_id=1, source_target_pairs={{0,1},{1,0},{2,3},{3,2},{4,5},{5,4},{6,7},{7,6},{8,9},{9,8},{10,11... | collective-permute-start | bytes 4718600 | tf_op jit(solution)/shard_map/ppermute | solution.py:55
  123.0 19.0 %all-to-all-start.2 = ((bf16[8,192,128]{2,1,0:T(8,128)(2,1)}), bf16[8,192,128]{2,1,0:T(8,128)(2,1)S(1)}, u32[]{:S(2)}, u32[]{:S(2)}) async-start(bf16[8,192,128]{2,1,0:T(8,128)(2,1)} %get-tuple-element.48), calls=%async_computation.2 | async-start | bytes 786432 | tf_op jit(solution)/shard_map/all_to_all | solution.py:714
  126.5 84.7 %reduce-scatter.2.cloned.1.call-start = ((), (), s32[]{:S(2)}) async-start(), calls=%async_computation.9 | async-start | bytes 1769472 | tf_op jit(solution)/shard_map/reduce_scatter | solution.py:710
  132.7 1.2 copy-start.10
  137.3 1.2 copy-start.9
  142.0 0.7 copy-start.13
  142.8 32.2 %all-to-all-start.3 = ((bf16[8,128,768]{2,1,0:T(8,128)(2,1)}), bf16[8,128,768]{2,1,0:T(8,128)(2,1)}, u32[]{:S(2)}, u32[]{:S(2)}) async-start(bf16[8,128,768]{2,1,0:T(8,128)(2,1)} %sum_cores_tail.1.refs_2_), calls=%async_computation.3 | async-start | bytes 3145728 | tf_op jit(solution)/shard_map/all_to_all | solution.py:63
  160.8 15.9 %copy-start.7 = (bf16[8,128,768]{2,1,0:T(8,128)(2,1)S(1)}, bf16[8,128,768]{2,1,0:T(8,128)(2,1)}, u32[]{:S(2)}) copy-start(bf16[8,128,768]{2,1,0:T(8,128)(2,1)} %get-tuple-element.57) | copy-start | bytes 4718596
  178.0 29.8 %all-to-all-start.4 = ((bf16[8,144,768]{2,1,0:T(8,128)(2,1)}), bf16[8,144,768]{2,1,0:T(8,128)(2,1)S(1)}, u32[]{:S(2)}, u32[]{:S(2)}) async-start(bf16[8,144,768]{2,1,0:T(8,128)(2,1)} %pad_maximum_fusion), calls=%async_computation.4 | async-start | bytes 3538944 | tf_op jit(solution)/shard_map/all_to_all | solution.py:742
  184.3 8.5 %copy-start.1 = (bf16[2,128,768]{2,1,0:T(8,128)(2,1)S(1)}, bf16[2,128,768]{2,1,0:T(8,128)(2,1)}, u32[]{:S(2)}) copy-start(bf16[2,128,768]{2,1,0:T(8,128)(2,1)} %refs_0_.3) | copy-start | bytes 1179652
  188.7 5.9 %collective-permute-start.10 = (bf16[8,48,768]{2,1,0:T(8,128)(2,1)}, bf16[8,48,768]{2,1,0:T(8,128)(2,1)S(1)}, u32[]{:S(2)}, u32[]{:S(2)}) collective-permute-start(bf16[8,48,768]{2,1,0:T(8,128)(2,1)} %get-tuple-element.65), channel_id=1, source_target_pairs={{0,1},{1,0},{2,3},{3,2},{4,5},{5,4},{6,7},{7,6},{8,9},{9,8},{10,11... | collective-permute-start | bytes 1769480 | tf_op jit(solution)/shard_map/ppermute | solution.py:55
  194.6 13.2 %copy-start.17 = (bf16[8,48,768]{2,1,0:T(8,128)(2,1)}, bf16[8,48,768]{2,1,0:T(8,128)(2,1)S(1)}, u32[]{:S(2)}) copy-start(bf16[8,48,768]{2,1,0:T(8,128)(2,1)S(1)} %collective-permute-done.10.refs_1_) | copy-start | bytes 1769476
  207.8 1.2 copy-start.2
  211.2 12.5 %copy-start.3 = (bf16[8,144,768]{2,1,0:T(8,128)(2,1)S(1)}, bf16[8,144,768]{2,1,0:T(8,128)(2,1)}, u32[]{:S(2)}) copy-start(bf16[8,144,768]{2,1,0:T(8,128)(2,1)} %copy-done.2) | copy-start | bytes 5308420
  213.5 24.5 %all-to-all-start.5 = ((bf16[8,64,768]{2,1,0:T(8,128)(2,1)}), bf16[8,64,768]{2,1,0:T(8,128)(2,1)S(1)}, u32[]{:S(2)}, u32[]{:S(2)}) async-start(bf16[8,64,768]{2,1,0:T(8,128)(2,1)} %pad_maximum_fusion.1), calls=%async_computation.6 | async-start | bytes 1572864 | tf_op jit(solution)/shard_map/all_to_all | solution.py:63
  239.1 18.6 %all-to-all-start.6 = ((bf16[8,80,768]{2,1,0:T(8,128)(2,1)}), bf16[8,80,768]{2,1,0:T(8,128)(2,1)S(1)}, u32[]{:S(2)}, u32[]{:S(2)}) async-start(bf16[8,80,768]{2,1,0:T(8,128)(2,1)} %broadcast_in_dim.49), calls=%async_computation.7 | async-start | bytes 1966080 | tf_op jit(solution)/shard_map/all_to_all | solution.py:23
  242.7 0.7 copy-start.16
  242.7 1.1 copy-start.4
  257.7 1.0 copy-start.12
Sparse Core Ops, SparseCore 0:
  10.4 69.8 all-gather.1
  142.1 42.2 reduce-scatter.1
